TPU v7x, 768 devices: a whole 4x8x12 slice. The times are simulated.
768 devices in a mesh: fsdp: 32 (over y, x_hi, core), tensor: 24 (over x_lo, z).
Axes of the slice: x: 4 (x_hi: 2, x_lo: 2; x = x_hi * 2 + x_lo), y: 8, z: 12, core: 2. Of those that a mesh axis runs over, the one named last changes fastest.
Arguments:
- tokens: bfloat16 [6144, 4096], P('fsdp'), may hold values from -80 to 80
- norm_gain: float32 [4096], P('fsdp'), may hold values from 0.25 to 1.75
- gate_weight: bfloat16 [4096, 15360], P('fsdp', 'tensor'), may hold values from -0.09375 to 0.09375
- up_weight: bfloat16 [4096, 15360], P('fsdp', 'tensor'), may hold values from -0.09375 to 0.09375
Outputs:
- hidden: bfloat16 [6144, 15360], P('fsdp', 'tensor')
All inputs are finite; a program needn't handle non-finite values.
Results may differ from a plain program's by a relative error of at most 0.0058.
Values may be sent and summed in bfloat16 or wider, within the bound.
No kernel may reach another device: no remote copies, remote signals or barrier semaphores. Data moves between devices by JAX's collectives and lax.ppermute only.
A program may use at most 32 MiB of HBM per device.

v0:
```python
import jax
import jax.numpy as jnp
from jax import lax
from jax.sharding import PartitionSpec as P

epsilon = 1e-05


def on_device(tokens, norm_gain, gate_weight, up_weight):
    gain_full = lax.all_gather(norm_gain, "fsdp", axis=0, tiled=True)
    values = tokens.astype(jnp.float32)
    row_scale = lax.rsqrt(jnp.mean(values * values, axis=1, keepdims=True) + epsilon)
    normed = (values * row_scale * gain_full[None, :]).astype(jnp.bfloat16)

    def add_rows(piece):
        return jnp.dot(normed, piece, preferred_element_type=jnp.float32)

    gate = add_rows(lax.all_gather(gate_weight, "fsdp", axis=0, tiled=True))
    up = add_rows(lax.all_gather(up_weight, "fsdp", axis=0, tiled=True))
    return (jax.nn.silu(gate) * up).astype(jnp.bfloat16)


def solution(mesh):
    return jax.shard_map(
        on_device,
        mesh=mesh,
        in_specs=(P("fsdp", None), P("fsdp"), P("fsdp", "tensor"), P("fsdp", "tensor")),
        out_specs=P("fsdp", "tensor"),
        check_vma=False,
    )
```

profile of v0, /device:TPU:1, one launch (start us, length us, event | category | flops | bytes accessed | tf_op | source)
XLA Modules:
  0.0 235.0 jit_solution(8563117831426577682)
XLA Ops:
  6.5 0.0 all-gather.4.cloned.1.call-start
  6.5 0.7 all-gather.4.cloned.1.call-update
  7.3 0.0 all-gather.6.cloned.1.call-start
  7.3 0.7 all-gather.6.cloned.1.call-update
  8.0 46.7 %all-gather = f32[32,1,128]{2,1,0:T(1,128)S(1)} all-gather(f32[1,1,128]{2,1,0:T(1,128)} %bitcast.6), channel_id=1, replica_groups=mesh['fsdp'=32,'tensor'=24] {'fsdp'}, dimensions={0}, use_global_device_ids=true | all-gather | bytes 16896 | tf_op jit(solution)/shard_map/all_gather | solution.py:10
  54.8 1.8 fusion
  56.6 64.3 %all-gather.4.cloned.1.call-done = bf16[4096,640]{1,0:T(8,128)(2,1)} async-done(((bf16[128,640]{1,0:T(8,128)(2,1)}), bf16[4096,640]{1,0:T(8,128)(2,1)}) %all-gather.4.cloned.1.call-update) | async-done | bytes 5242896 | tf_op jit(solution)/shard_map/all_gather | solution.py:18
  120.8 0.0 copy-start
  120.8 4.5 %fusion.5 = f32[192,640]{1,0:T(8,128)S(1)} fusion(bf16[4096,640]{1,0:T(8,128)(2,1)} %all-gather.4.cloned.1.call-done, bf16[192,4096]{1,0:T(8,128)(2,1)} %param.4, f32[4096]{0:T(1024)S(1)} %bitcast.4, f32[192]{0:T(256)S(1)} %add_rsqrt_fusion), kind=kOutput, calls=%fused_computation.7 | convolution fusion | flops 1009778688 | bytes 7324416 | tf_op jit(solution)/shard_map/dot_general | solution.py:16
  125.4 98.2 %all-gather.6.cloned.1.call-done = bf16[4096,640]{1,0:T(8,128)(2,1)} async-done(((bf16[128,640]{1,0:T(8,128)(2,1)}), bf16[4096,640]{1,0:T(8,128)(2,1)}) %all-gather.6.cloned.1.call-update) | async-done | bytes 5242896 | tf_op jit(solution)/shard_map/all_gather | solution.py:19
  223.5 0.0 copy-done
  223.5 4.7 %fusion.3 = bf16[192,640]{1,0:T(8,128)(2,1)} fusion(bf16[4096,640]{1,0:T(8,128)(2,1)} %all-gather.6.cloned.1.call-done, f32[192,640]{1,0:T(8,128)S(1)} %fusion.5, bf16[192,4096]{1,0:T(8,128)(2,1)S(1)} %copy-done, f32[4096]{0:T(1024)S(1)} %bitcast.5, f32[192]{0:T(256)S(1)} %add_rsqrt_fusion), kind=kOutput, calls=%fused_computation.6 | convolution fusion | flops 1010515968 | bytes 7570176 | tf_op jit(solution)/shard_map/dot_general | solution.py:16
  (1 shorter events, 0.0 us)
Async XLA Ops:
  6.5 114.3 %all-gather.4.cloned.1.call-start = ((), (), s32[]{:S(2)}) async-start(), calls=%async_computation | async-start | bytes 5406720 | tf_op jit(solution)/shard_map/all_gather | solution.py:18
  7.3 216.3 %all-gather.6.cloned.1.call-start = ((), (), s32[]{:S(2)}) async-start(), calls=%async_computation.1 | async-start | bytes 5406720 | tf_op jit(solution)/shard_map/all_gather | solution.py:19
  120.8 102.7 %copy-start = (bf16[192,4096]{1,0:T(8,128)(2,1)S(1)}, bf16[192,4096]{1,0:T(8,128)(2,1)}, u32[]{:S(2)}) copy-start(bf16[192,4096]{1,0:T(8,128)(2,1)} %param.4) | copy-start | bytes 4718596
Sparse Core Ops, SparseCore 0:
  11.3 109.5 all-gather.3
  124.8 98.7 all-gather.5
where the time goes:
time: 235 us
  waiting for transfers between devices  164 us (70%)
  blocking collectives  46.7 us (20%)
  between operations  13.4 us (6%)
  matrix products  9.19 us (4%)
    all_gather x1, waiting for transfers between devices, on_device(): up = add_rows(lax.all_gather(up_weight, 'fsdp', axis=0, tiled=True))  98.2 us
    all_gather x1, waiting for transfers between devices, on_device(): gate = add_rows(lax.all_gather(gate_weight, 'fsdp', axis=0, tiled=True))  64.3 us
    all_gather x1, blocking collectives, on_device(): gain_full = lax.all_gather(norm_gain, 'fsdp', axis=0, tiled=True)  46.7 us
    dot_general x2, matrix products, add_rows(): return jnp.dot(normed, piece, preferred_element_type=jnp.float32)  9.19 us
  transfers between devices with their start and end apart: 2, of which 2 were waited for; matrix products, arithmetic and copies ran while one was open for 3% of the time, Pallas kernels for 0%

commit v1 on v0

v1 whole, which is shorter than its diff:
```python
import functools

import jax
import jax.numpy as jnp
import numpy as np
from jax import lax
from jax.experimental import pallas as pl
from jax.experimental.pallas import tpu as pltpu
from jax.sharding import PartitionSpec as P

epsilon = 1e-05
vmem_bytes = 40 * 1024 * 1024


def load_blocks(blocks, held, sems):
    copies = [pltpu.make_async_copy(b, held.at[i], sems.at[i]) for i, b in enumerate(blocks)]
    for copy in copies:
        copy.start()
    return copies


def add_blocks(places, tokens, held, copies, total):
    depth = held.shape[1]
    for i, copy in enumerate(copies):
        copy.wait()
        start = pl.multiple_of(places[i] * depth, depth)
        total[...] += jnp.dot(tokens[:, pl.ds(start, depth)], held[i], preferred_element_type=jnp.float32)


def first_kernel(n, places, tokens, *refs):
    blocks, (total, scale, held, sems) = refs[:n], refs[n:]
    copies = load_blocks(blocks, held, sems)
    values = tokens[...].astype(jnp.float32)
    scale[...] = lax.rsqrt(jnp.mean(values * values, axis=1, keepdims=True) + epsilon)
    total[...] = jnp.zeros_like(total)
    add_blocks(places, tokens, held, copies, total)


def next_kernel(n, places, tokens, before, *refs):
    blocks, (total, held, sems) = refs[:n], refs[n:]
    copies = load_blocks(blocks, held, sems)
    total[...] = before[...]
    add_blocks(places, tokens, held, copies, total)


def last_kernel(n, places, tokens, before, scale, *refs):
    blocks, (hidden, total, held, sems) = refs[:n], refs[n:]
    copies = load_blocks(blocks, held, sems)
    total[...] = before[...]
    add_blocks(places, tokens, held, copies, total)
    wide = hidden.shape[1]
    gate = total[:, :wide] * scale[...]
    up = total[:, wide:] * scale[...]
    hidden[...] = (gate / (1.0 + jnp.exp(-gate)) * up).astype(hidden.dtype)


def call(kernel, places, tokens, extra, blocks, out_shape, out_specs, scratch):
    n = len(blocks)
    depth, wide = blocks[0].shape
    rows = tokens.shape[0]
    vmem = pl.BlockSpec(memory_space=pltpu.VMEM)
    return pl.pallas_call(
        functools.partial(kernel, n),
        out_shape=out_shape,
        in_specs=[pl.BlockSpec(memory_space=pltpu.SMEM)] + [vmem] * (1 + len(extra)) + [pl.BlockSpec(memory_space=pl.ANY)] * n,
        out_specs=out_specs,
        scratch_shapes=scratch + [pltpu.VMEM((n, depth, wide), blocks[0].dtype), pltpu.SemaphoreType.DMA((n,))],
        compiler_params=pltpu.CompilerParams(vmem_limit_bytes=vmem_bytes),
        cost_estimate=pl.CostEstimate(
            flops=2 * n * rows * depth * wide, bytes_accessed=2 * n * depth * wide + 4 * rows * wide, transcendentals=0
        ),
    )(places, tokens, *extra, *blocks)


def make_on_device(count):
    high = count // 4

    def move(where):
        pairs = []
        for f in range(count):
            y, x, c = where(f // 4, (f // 2) % 2, f % 2)
            pairs.append((f, (y % high) * 4 + (x % 2) * 2 + c % 2))
        return lambda v: lax.ppermute(v, "fsdp", pairs)

    along = move(lambda y, x, c: (y + 1 - 2 * c, x, c))
    slant = move(lambda y, x, c: (y + 1 - 2 * c, x + 1, c))
    across = move(lambda y, x, c: (y, x + 1, c))
    swap = move(lambda y, x, c: (y, x, c + 1))
    core_pairs = [[f, f + 1] for f in range(0, count, 2)]

    def place(f, steps, other):
        y, x, c = f // 4, (f // 2) % 2, f % 2
        return (y + steps * (2 * c - 1)) % high * 2 + (x + other) % 2

    def places(index, *which):
        table = np.array([[place(f, *w) for w in which] for f in range(count)], np.int32)
        return lax.dynamic_index_in_dim(jnp.asarray(table), index, 0, keepdims=False)

    def join(v):
        return lax.all_gather(v, "fsdp", axis=0, tiled=True, axis_index_groups=core_pairs)

    def on_device(tokens, norm_gain, gate_weight, up_weight):
        index = lax.axis_index("fsdp")
        c = lax.bitwise_and(index, 1)
        gain = norm_gain[:, None]
        own = jnp.concatenate([gate_weight * gain, up_weight * gain], axis=1).astype(jnp.bfloat16)
        depth, wide = own.shape
        chip = join(own)

        a1, b1 = along(chip), slant(chip)
        a2, b2 = along(a1), along(b1)
        a3, b3 = along(a2), along(b2)
        a4 = along(lax.dynamic_slice_in_dim(a3, c * depth, depth, 0))
        b4 = along(lax.dynamic_slice_in_dim(b3, c * depth, depth, 0))
        b0 = across(chip)

        rows = tokens.shape[0]
        sums = jax.ShapeDtypeStruct((rows, wide), jnp.float32)
        vmem = pl.BlockSpec(memory_space=pltpu.VMEM)
        total, scale = call(
            first_kernel,
            places(index, (0, 0), (1, 0), (-1, 0), (1, 1), (-1, 1), (2, 0), (-2, 0)),
            tokens,
            [],
            [chip, a1, swap(a1), b1, swap(b1), a2, swap(a2)],
            (sums, jax.ShapeDtypeStruct((rows, 1), jnp.float32)),
            (vmem, vmem),
            [],
        )
        total = call(
            next_kernel,
            places(index, (0, 1), (2, 1), (-2, 1), (3, 0), (-3, 0), (3, 1), (-3, 1)),
            tokens,
            [total],
            [b0, b2, swap(b2), a3, swap(a3), b3, swap(b3)],
            sums,
            vmem,
            [],
        )
        a4, total = lax.optimization_barrier((a4, total))
        return call(
            last_kernel,
            places(index, (4, 0), (4, 1)),
            tokens,
            [total, scale],
            [join(a4), join(b4)],
            jax.ShapeDtypeStruct((rows, wide // 2), jnp.bfloat16),
            vmem,
            [pltpu.VMEM((rows, wide), jnp.float32)],
        )

    return on_device


def solution(mesh):
    return jax.shard_map(
        make_on_device(mesh.shape["fsdp"]),
        mesh=mesh,
        in_specs=(P("fsdp", None), P("fsdp"), P("fsdp", "tensor"), P("fsdp", "tensor")),
        out_specs=P("fsdp", "tensor"),
        check_vma=False,
    )
```

time: 235 us -> 98.8 us (0.42)
  waiting for transfers between devices: 164 us -> 25.8 us
  starting transfers between devices: 0.04 us -> 42.3 us
  blocking collectives: 46.7 us -> 17.1 us
  between operations: 13.4 us -> 0.24 us
  Pallas kernels: 0 us -> 9.43 us
  matrix products: 9.19 us -> 0 us
    all_gather x2 -> x0, waiting for transfers between devices: 162 us -> none  [the longest x1 98.2 us: on_device(): up = add_rows(lax.all_gather(up_weight, 'fsdp', axis=0, tiled=True))]
    ppermute x0 -> x15, starting transfers between devices: none -> 42.3 us  [move(): return lambda v: lax.ppermute(v, 'fsdp', pairs)]
    all_gather x1 -> x3, blocking collectives: 46.7 us -> 17.1 us  [join(): lax.all_gather(v, 'fsdp', axis=0, tiled=True, axis_index_groups=core_pairs)]
    ppermute x0 -> x15, waiting for transfers between devices: none -> 25.8 us  [move(): return lambda v: lax.ppermute(v, 'fsdp', pairs)]
    pallas_call x0 -> x3, Pallas kernels: none -> 9.43 us  [call(): pl.pallas_call(functools.partial(kernel, n), out_shape=out_shape, in_spec...]
    dot_general x2 -> x0, matrix products: 9.19 us -> none  [add_rows(): return jnp.dot(normed, piece, preferred_element_type=jnp.float32)]
  transfers between devices with their start and end apart: 2 -> 15, of which waited for: 2 -> 5; matrix products, arithmetic and copies ran while one was open for 3% -> 2% of each run, Pallas kernels for 0% -> 7%
where the time goes in v1:
time: 98.8 us; the launch traced here: 98.2 us
  starting transfers between devices  42.3 us (43%)
  waiting for transfers between devices  25.8 us (26%)
  blocking collectives  17.1 us (17%)
  Pallas kernels  9.43 us (10%)
  local copies, waits for them, and re-layouts  2.15 us (2%)
  other arithmetic  1.16 us (1%)
    ppermute x15, starting transfers between devices, move(): return lambda v: lax.ppermute(v, 'fsdp', pairs)  42.3 us
    ppermute x15, waiting for transfers between devices, move(): return lambda v: lax.ppermute(v, 'fsdp', pairs)  25.8 us
    all_gather x3, blocking collectives, join(): lax.all_gather(v, 'fsdp', axis=0, tiled=True, axis_index_groups=core_pairs)  17.1 us
    pallas_call x3, Pallas kernels, call(): pl.pallas_call(functools.partial(kernel, n), out_shape=out_shape, in_spec...  9.43 us
    squeeze x3, local copies, waits for them, and re-layouts, places(): lax.dynamic_index_in_dim(jnp.asarray(table), index, 0, keepdims=False)  2.09 us
  transfers between devices with their start and end apart: 15, of which 5 were waited for; matrix products, arithmetic and copies ran while one was open for 2% of the time, Pallas kernels for 7%

profile of v1, /device:TPU:1, one launch (start us, length us, event | category | flops | bytes accessed | tf_op | source)
XLA Modules:
  0.0 98.2 jit_solution(9661995215029493774)
XLA Ops:
  1.2 12.6 %all_gather.9.refs_0_ = bf16[256,1280]{1,0:T(8,128)(2,1)S(1)} all-gather(bf16[128,1280]{1,0:T(8,128)(2,1)S(1)} %pad_maximum_fusion), channel_id=1, replica_groups={{0,24},{48,72},{96,120},{144,168},{192,216},{240,264},{288,312},{336,36..., dimensions={0}, use_global_device_ids=true | all-gather | bytes 983040 | tf_op jit(solution)/shard_map/all_gather | solution.py:100
  15.7 1.9 %collective-permute-start.5 = (bf16[256,1280]{1,0:T(8,128)(2,1)S(1)}, bf16[256,1280]{1,0:T(8,128)(2,1)}, u32[]{:S(2)}, u32[]{:S(2)}) collective-permute-start(bf16[256,1280]{1,0:T(8,128)(2,1)S(1)} %all_gather.9.refs_0_), channel_id=1, source_target_pairs={{0,144},{24,744},{48,96},{72,696},{96,240},{120,72},{144,192},{168... | collective-permute-start | bytes 1966088 | tf_op jit(solution)/shard_map/ppermute | solution.py:83
  17.6 7.9 %collective-permute-done.refs_1_ = bf16[256,1280]{1,0:T(8,128)(2,1)} collective-permute-done((bf16[256,1280]{1,0:T(8,128)(2,1)S(1)}, bf16[256,1280]{1,0:T(8,128)(2,1)}, u32[]{:S(2)}, u32[]{:S(2)}) %collective-permute-start) | collective-permute-done | bytes 655392 | tf_op jit(solution)/shard_map/ppermute | solution.py:83
  25.5 3.1 %collective-permute-start.1 = (bf16[256,1280]{1,0:T(8,128)(2,1)}, bf16[256,1280]{1,0:T(8,128)(2,1)}, u32[]{:S(2)}, u32[]{:S(2)}) collective-permute-start(bf16[256,1280]{1,0:T(8,128)(2,1)} %collective-permute-done.refs_1_), channel_id=1, source_target_pairs={{0,96},{24,696},{48,144},{72,744},{96,192},{120,24},{144,240},{168... | collective-permute-start | bytes 1966088 | tf_op jit(solution)/shard_map/ppermute | solution.py:83
  28.6 7.9 %collective-permute-done.5.refs_3_ = bf16[256,1280]{1,0:T(8,128)(2,1)} collective-permute-done((bf16[256,1280]{1,0:T(8,128)(2,1)S(1)}, bf16[256,1280]{1,0:T(8,128)(2,1)}, u32[]{:S(2)}, u32[]{:S(2)}) %collective-permute-start.5) | collective-permute-done | bytes 655392 | tf_op jit(solution)/shard_map/ppermute | solution.py:83
  36.5 1.9 %collective-permute-start.9 = (bf16[256,1280]{1,0:T(8,128)(2,1)}, bf16[256,1280]{1,0:T(8,128)(2,1)}, u32[]{:S(2)}, u32[]{:S(2)}) collective-permute-start(bf16[256,1280]{1,0:T(8,128)(2,1)} %collective-permute-done.5.refs_3_), channel_id=1, source_target_pairs={{0,96},{24,696},{48,144},{72,744},{96,192},{120,24},{144,240},{168... | collective-permute-start | bytes 1966088 | tf_op jit(solution)/shard_map/ppermute | solution.py:83
  38.4 2.5 %collective-permute-start.4 = (bf16[256,1280]{1,0:T(8,128)(2,1)}, bf16[256,1280]{1,0:T(8,128)(2,1)}, u32[]{:S(2)}, u32[]{:S(2)}) collective-permute-start(bf16[256,1280]{1,0:T(8,128)(2,1)} %collective-permute-done.refs_1_), channel_id=1, source_target_pairs={{0,24},{24,0},{48,72},{72,48},{96,120},{120,96},{144,168},{168,144... | collective-permute-start | bytes 1966088 | tf_op jit(solution)/shard_map/ppermute | solution.py:83
  40.9 1.9 %collective-permute-start.6 = (bf16[256,1280]{1,0:T(8,128)(2,1)}, bf16[256,1280]{1,0:T(8,128)(2,1)}, u32[]{:S(2)}, u32[]{:S(2)}) collective-permute-start(bf16[256,1280]{1,0:T(8,128)(2,1)} %collective-permute-done.5.refs_3_), channel_id=1, source_target_pairs={{0,24},{24,0},{48,72},{72,48},{96,120},{120,96},{144,168},{168,144... | collective-permute-start | bytes 1966088 | tf_op jit(solution)/shard_map/ppermute | solution.py:83
  42.9 2.3 %collective-permute-done.1.refs_5_ = bf16[256,1280]{1,0:T(8,128)(2,1)} collective-permute-done((bf16[256,1280]{1,0:T(8,128)(2,1)}, bf16[256,1280]{1,0:T(8,128)(2,1)}, u32[]{:S(2)}, u32[]{:S(2)}) %collective-permute-start.1) | collective-permute-done | bytes 655392 | tf_op jit(solution)/shard_map/ppermute | solution.py:83
  45.2 2.5 %collective-permute-start.2 = (bf16[256,1280]{1,0:T(8,128)(2,1)}, bf16[256,1280]{1,0:T(8,128)(2,1)S(1)}, u32[]{:S(2)}, u32[]{:S(2)}) collective-permute-start(bf16[256,1280]{1,0:T(8,128)(2,1)} %collective-permute-done.1.refs_5_), channel_id=1, source_target_pairs={{0,96},{24,696},{48,144},{72,744},{96,192},{120,24},{144,240},{168... | collective-permute-start | bytes 1966088 | tf_op jit(solution)/shard_map/ppermute | solution.py:83
  47.7 4.4 %collective-permute-done.9.refs_1_ = bf16[256,1280]{1,0:T(8,128)(2,1)} collective-permute-done((bf16[256,1280]{1,0:T(8,128)(2,1)}, bf16[256,1280]{1,0:T(8,128)(2,1)}, u32[]{:S(2)}, u32[]{:S(2)}) %collective-permute-start.9) | collective-permute-done | bytes 655392 | tf_op jit(solution)/shard_map/ppermute | solution.py:83
  54.0 2.2 %collective-permute-start.7 = (bf16[256,1280]{1,0:T(8,128)(2,1)}, bf16[256,1280]{1,0:T(8,128)(2,1)}, u32[]{:S(2)}, u32[]{:S(2)}) collective-permute-start(bf16[256,1280]{1,0:T(8,128)(2,1)} %collective-permute-done.1.refs_5_), channel_id=1, source_target_pairs={{0,24},{24,0},{48,72},{72,48},{96,120},{120,96},{144,168},{168,144... | collective-permute-start | bytes 1966088 | tf_op jit(solution)/shard_map/ppermute | solution.py:83
  57.6 6.0 %collective-permute-start.8 = (bf16[256,1280]{1,0:T(8,128)(2,1)S(1)}, bf16[256,1280]{1,0:T(8,128)(2,1)S(1)}, u32[]{:S(2)}, u32[]{:S(2)}) collective-permute-start(bf16[256,1280]{1,0:T(8,128)(2,1)S(1)} %all_gather.9.refs_0_), channel_id=1, source_target_pairs={{0,48},{24,72},{48,0},{72,24},{96,144},{120,168},{144,96},{168,120... | collective-permute-start | bytes 1966088 | tf_op jit(solution)/shard_map/ppermute | solution.py:83
  63.6 2.2 %collective-permute-start.10 = (bf16[256,1280]{1,0:T(8,128)(2,1)}, bf16[256,1280]{1,0:T(8,128)(2,1)S(1)}, u32[]{:S(2)}, u32[]{:S(2)}) collective-permute-start(bf16[256,1280]{1,0:T(8,128)(2,1)} %collective-permute-done.9.refs_1_), channel_id=1, source_target_pairs={{0,24},{24,0},{48,72},{72,48},{96,120},{120,96},{144,168},{168,144... | collective-permute-start | bytes 1966088 | tf_op jit(solution)/shard_map/ppermute | solution.py:83
  65.9 2.1 %collective-permute-start.11 = (bf16[256,1280]{1,0:T(8,128)(2,1)S(1)}, bf16[256,1280]{1,0:T(8,128)(2,1)S(1)}, u32[]{:S(2)}, u32[]{:S(2)}) collective-permute-start(bf16[256,1280]{1,0:T(8,128)(2,1)S(1)} %collective-permute-done.2.refs_3_), channel_id=1, source_target_pairs={{0,24},{24,0},{48,72},{72,48},{96,120},{120,96},{144,168},{168,144... | collective-permute-start | bytes 1966088 | tf_op jit(solution)/shard_map/ppermute | solution.py:83
  68.0 2.2 %collective-permute-start.13 = (bf16[256,1280]{1,0:T(8,128)(2,1)S(1)}, bf16[256,1280]{1,0:T(8,128)(2,1)S(1)}, u32[]{:S(2)}, u32[]{:S(2)}) collective-permute-start(bf16[256,1280]{1,0:T(8,128)(2,1)S(1)} %collective-permute-done.12.refs_5_), channel_id=1, source_target_pairs={{0,24},{24,0},{48,72},{72,48},{96,120},{120,96},{144,168},{168,144... | collective-permute-start | bytes 1966088 | tf_op jit(solution)/shard_map/ppermute | solution.py:83
  70.3 4.9 %collective-permute-start.14 = (bf16[128,1280]{1,0:T(8,128)(2,1)S(1)}, bf16[128,1280]{1,0:T(8,128)(2,1)S(1)}, u32[]{:S(2)}, u32[]{:S(2)}) collective-permute-start(bf16[128,1280]{1,0:T(8,128)(2,1)S(1)} %constant_dynamic-slice_fusion), channel_id=1, source_target_pairs={{0,96},{24,696},{48,144},{72,744},{96,192},{120,24},{144,240},{168... | collective-permute-start | bytes 983048 | tf_op jit(solution)/shard_map/ppermute | solution.py:83
  75.8 3.3 %collective-permute-done.14 = bf16[128,1280]{1,0:T(8,128)(2,1)S(1)} collective-permute-done((bf16[128,1280]{1,0:T(8,128)(2,1)S(1)}, bf16[128,1280]{1,0:T(8,128)(2,1)S(1)}, u32[]{:S(2)}, u32[]{:S(2)}) %collective-permute-start.14) | collective-permute-done | bytes 327712 | tf_op jit(solution)/shard_map/ppermute | solution.py:83
  79.1 5.0 %collective-permute-start.3 = (bf16[128,1280]{1,0:T(8,128)(2,1)S(1)}, bf16[128,1280]{1,0:T(8,128)(2,1)S(1)}, u32[]{:S(2)}, u32[]{:S(2)}) collective-permute-start(bf16[128,1280]{1,0:T(8,128)(2,1)S(1)} %constant_dynamic-slice_fusion.3), channel_id=1, source_target_pairs={{0,96},{24,696},{48,144},{72,744},{96,192},{120,24},{144,240},{168... | collective-permute-start | bytes 983048 | tf_op jit(solution)/shard_map/ppermute | solution.py:83
  84.1 3.4 %shard_map.73 = (f32[192,1280]{1,0:T(8,128)S(1)}, f32[192,1]{1,0:T(8,128)S(1)}) custom-call(s32[7]{0:T(128)S(1)} %fusion.2.places, bf16[192,4096]{1,0:T(8,128)(2,1)S(1)} %copy-done, bf16[256,1280]{1,0:T(8,128)(2,1)S(1)} %all_gather.9.refs_0_, bf16[256,1280]{1,0:T(8,128)(2,1)} %collective-permute-done.refs_1_, ...), custom_call_target="tpu_custom_call" | custom-call | flops 880803840 | bytes 5570560 | tf_op jit(solution)/shard_map/pallas_call | solution.py:62
  87.5 2.3 %all_gather.11.refs_1_ = bf16[256,1280]{1,0:T(8,128)(2,1)S(1)} all-gather(bf16[128,1280]{1,0:T(8,128)(2,1)S(1)} %collective-permute-done.14), channel_id=1, replica_groups={{0,24},{48,72},{96,120},{144,168},{192,216},{240,264},{288,312},{336,36..., dimensions={0}, use_global_device_ids=true | all-gather | bytes 983040 | tf_op jit(solution)/shard_map/all_gather | solution.py:100
  89.8 3.8 %shard_map.74.before = f32[192,1280]{1,0:T(8,128)S(1)} custom-call(s32[7]{0:T(128)S(1)} %fusion.1.places, bf16[192,4096]{1,0:T(8,128)(2,1)S(1)} %copy-done, f32[192,1280]{1,0:T(8,128)S(1)} %get-tuple-element.9.before, bf16[256,1280]{1,0:T(8,128)(2,1)S(1)} %collective-permute-done.8.refs_0_, bf16[256,1280]{1,0:T(8,128)(2,1)} %collective-permute-done.9.refs_1_, ...), custom_call_target="tpu_custom_call" | custom-call | flops 880803840 | bytes 5570560 | tf_op jit(solution)/shard_map/pallas_call | solution.py:62
  93.6 2.3 %all_gather.10.refs_0_ = bf16[256,1280]{1,0:T(8,128)(2,1)S(1)} all-gather(bf16[128,1280]{1,0:T(8,128)(2,1)S(1)} %collective-permute-done.3), channel_id=1, replica_groups={{0,24},{48,72},{96,120},{144,168},{192,216},{240,264},{288,312},{336,36..., dimensions={0}, use_global_device_ids=true | all-gather | bytes 983040 | tf_op jit(solution)/shard_map/all_gather | solution.py:100
  95.9 2.3 %shard_map.75 = bf16[192,640]{1,0:T(8,128)(2,1)} custom-call(s32[2]{0:T(128)S(1)} %fusion.places, bf16[192,4096]{1,0:T(8,128)(2,1)S(1)} %copy-done, f32[192,1280]{1,0:T(8,128)S(1)} %shard_map.74.before, f32[192,1]{1,0:T(8,128)S(1)} %get-tuple-element.11.scale, bf16[256,1280]{1,0:T(8,128)(2,1)S(1)} %all_gather.10.refs_0_, ...), custom_call_target="tpu_custom_call" | custom-call | flops 251658240 | bytes 2293760 | tf_op jit(solution)/shard_map/pallas_call | solution.py:62
  (21 shorter events, 7.2 us)
Async XLA Ops:
  1.1 83.0 %copy-start = (bf16[192,4096]{1,0:T(8,128)(2,1)S(1)}, bf16[192,4096]{1,0:T(8,128)(2,1)}, u32[]{:S(2)}) copy-start(bf16[192,4096]{1,0:T(8,128)(2,1)} %tokens.5) | copy-start | bytes 4718596
  13.7 11.7 %collective-permute-start = (bf16[256,1280]{1,0:T(8,128)(2,1)S(1)}, bf16[256,1280]{1,0:T(8,128)(2,1)}, u32[]{:S(2)}, u32[]{:S(2)}) collective-permute-start(bf16[256,1280]{1,0:T(8,128)(2,1)S(1)} %all_gather.9.refs_0_), channel_id=1, source_target_pairs={{0,96},{24,696},{48,144},{72,744},{96,192},{120,24},{144,240},{168... | collective-permute-start | bytes 1966088 | tf_op jit(solution)/shard_map/ppermute | solution.py:83
  15.7 20.9 %collective-permute-start.5 = (bf16[256,1280]{1,0:T(8,128)(2,1)S(1)}, bf16[256,1280]{1,0:T(8,128)(2,1)}, u32[]{:S(2)}, u32[]{:S(2)}) collective-permute-start(bf16[256,1280]{1,0:T(8,128)(2,1)S(1)} %all_gather.9.refs_0_), channel_id=1, source_target_pairs={{0,144},{24,744},{48,96},{72,696},{96,240},{120,72},{144,192},{168... | collective-permute-start | bytes 1966088 | tf_op jit(solution)/shard_map/ppermute | solution.py:83
  25.5 19.7 %collective-permute-start.1 = (bf16[256,1280]{1,0:T(8,128)(2,1)}, bf16[256,1280]{1,0:T(8,128)(2,1)}, u32[]{:S(2)}, u32[]{:S(2)}) collective-permute-start(bf16[256,1280]{1,0:T(8,128)(2,1)} %collective-permute-done.refs_1_), channel_id=1, source_target_pairs={{0,96},{24,696},{48,144},{72,744},{96,192},{120,24},{144,240},{168... | collective-permute-start | bytes 1966088 | tf_op jit(solution)/shard_map/ppermute | solution.py:83
  36.5 15.6 %collective-permute-start.9 = (bf16[256,1280]{1,0:T(8,128)(2,1)}, bf16[256,1280]{1,0:T(8,128)(2,1)}, u32[]{:S(2)}, u32[]{:S(2)}) collective-permute-start(bf16[256,1280]{1,0:T(8,128)(2,1)} %collective-permute-done.5.refs_3_), channel_id=1, source_target_pairs={{0,96},{24,696},{48,144},{72,744},{96,192},{120,24},{144,240},{168... | collective-permute-start | bytes 1966088 | tf_op jit(solution)/shard_map/ppermute | solution.py:83
  38.4 19.2 %collective-permute-start.4 = (bf16[256,1280]{1,0:T(8,128)(2,1)}, bf16[256,1280]{1,0:T(8,128)(2,1)}, u32[]{:S(2)}, u32[]{:S(2)}) collective-permute-start(bf16[256,1280]{1,0:T(8,128)(2,1)} %collective-permute-done.refs_1_), channel_id=1, source_target_pairs={{0,24},{24,0},{48,72},{72,48},{96,120},{120,96},{144,168},{168,144... | collective-permute-start | bytes 1966088 | tf_op jit(solution)/shard_map/ppermute | solution.py:83
  40.9 22.7 %collective-permute-start.6 = (bf16[256,1280]{1,0:T(8,128)(2,1)}, bf16[256,1280]{1,0:T(8,128)(2,1)}, u32[]{:S(2)}, u32[]{:S(2)}) collective-permute-start(bf16[256,1280]{1,0:T(8,128)(2,1)} %collective-permute-done.5.refs_3_), channel_id=1, source_target_pairs={{0,24},{24,0},{48,72},{72,48},{96,120},{120,96},{144,168},{168,144... | collective-permute-start | bytes 1966088 | tf_op jit(solution)/shard_map/ppermute | solution.py:83
  45.2 20.7 %collective-permute-start.2 = (bf16[256,1280]{1,0:T(8,128)(2,1)}, bf16[256,1280]{1,0:T(8,128)(2,1)S(1)}, u32[]{:S(2)}, u32[]{:S(2)}) collective-permute-start(bf16[256,1280]{1,0:T(8,128)(2,1)} %collective-permute-done.1.refs_5_), channel_id=1, source_target_pairs={{0,96},{24,696},{48,144},{72,744},{96,192},{120,24},{144,240},{168... | collective-permute-start | bytes 1966088 | tf_op jit(solution)/shard_map/ppermute | solution.py:83
  52.1 15.9 %collective-permute-start.12 = (bf16[256,1280]{1,0:T(8,128)(2,1)}, bf16[256,1280]{1,0:T(8,128)(2,1)S(1)}, u32[]{:S(2)}, u32[]{:S(2)}) collective-permute-start(bf16[256,1280]{1,0:T(8,128)(2,1)} %collective-permute-done.9.refs_1_), channel_id=1, source_target_pairs={{0,96},{24,696},{48,144},{72,744},{96,192},{120,24},{144,240},{168... | collective-permute-start | bytes 1966088 | tf_op jit(solution)/shard_map/ppermute | solution.py:83
  54.0 16.2 %collective-permute-start.7 = (bf16[256,1280]{1,0:T(8,128)(2,1)}, bf16[256,1280]{1,0:T(8,128)(2,1)}, u32[]{:S(2)}, u32[]{:S(2)}) collective-permute-start(bf16[256,1280]{1,0:T(8,128)(2,1)} %collective-permute-done.1.refs_5_), channel_id=1, source_target_pairs={{0,24},{24,0},{48,72},{72,48},{96,120},{120,96},{144,168},{168,144... | collective-permute-start | bytes 1966088 | tf_op jit(solution)/shard_map/ppermute | solution.py:83
  57.6 32.2 %collective-permute-start.8 = (bf16[256,1280]{1,0:T(8,128)(2,1)S(1)}, bf16[256,1280]{1,0:T(8,128)(2,1)S(1)}, u32[]{:S(2)}, u32[]{:S(2)}) collective-permute-start(bf16[256,1280]{1,0:T(8,128)(2,1)S(1)} %all_gather.9.refs_0_), channel_id=1, source_target_pairs={{0,48},{24,72},{48,0},{72,24},{96,144},{120,168},{144,96},{168,120... | collective-permute-start | bytes 1966088 | tf_op jit(solution)/shard_map/ppermute | solution.py:83
  63.6 26.2 %collective-permute-start.10 = (bf16[256,1280]{1,0:T(8,128)(2,1)}, bf16[256,1280]{1,0:T(8,128)(2,1)S(1)}, u32[]{:S(2)}, u32[]{:S(2)}) collective-permute-start(bf16[256,1280]{1,0:T(8,128)(2,1)} %collective-permute-done.9.refs_1_), channel_id=1, source_target_pairs={{0,24},{24,0},{48,72},{72,48},{96,120},{120,96},{144,168},{168,144... | collective-permute-start | bytes 1966088 | tf_op jit(solution)/shard_map/ppermute | solution.py:83
  65.9 23.9 %collective-permute-start.11 = (bf16[256,1280]{1,0:T(8,128)(2,1)S(1)}, bf16[256,1280]{1,0:T(8,128)(2,1)S(1)}, u32[]{:S(2)}, u32[]{:S(2)}) collective-permute-start(bf16[256,1280]{1,0:T(8,128)(2,1)S(1)} %collective-permute-done.2.refs_3_), channel_id=1, source_target_pairs={{0,24},{24,0},{48,72},{72,48},{96,120},{120,96},{144,168},{168,144... | collective-permute-start | bytes 1966088 | tf_op jit(solution)/shard_map/ppermute | solution.py:83
  68.0 21.8 %collective-permute-start.13 = (bf16[256,1280]{1,0:T(8,128)(2,1)S(1)}, bf16[256,1280]{1,0:T(8,128)(2,1)S(1)}, u32[]{:S(2)}, u32[]{:S(2)}) collective-permute-start(bf16[256,1280]{1,0:T(8,128)(2,1)S(1)} %collective-permute-done.12.refs_5_), channel_id=1, source_target_pairs={{0,24},{24,0},{48,72},{72,48},{96,120},{120,96},{144,168},{168,144... | collective-permute-start | bytes 1966088 | tf_op jit(solution)/shard_map/ppermute | solution.py:83
  70.3 8.9 %collective-permute-start.14 = (bf16[128,1280]{1,0:T(8,128)(2,1)S(1)}, bf16[128,1280]{1,0:T(8,128)(2,1)S(1)}, u32[]{:S(2)}, u32[]{:S(2)}) collective-permute-start(bf16[128,1280]{1,0:T(8,128)(2,1)S(1)} %constant_dynamic-slice_fusion), channel_id=1, source_target_pairs={{0,96},{24,696},{48,144},{72,744},{96,192},{120,24},{144,240},{168... | collective-permute-start | bytes 983048 | tf_op jit(solution)/shard_map/ppermute | solution.py:83
  79.1 14.5 %collective-permute-start.3 = (bf16[128,1280]{1,0:T(8,128)(2,1)S(1)}, bf16[128,1280]{1,0:T(8,128)(2,1)S(1)}, u32[]{:S(2)}, u32[]{:S(2)}) collective-permute-start(bf16[128,1280]{1,0:T(8,128)(2,1)S(1)} %constant_dynamic-slice_fusion.3), channel_id=1, source_target_pairs={{0,96},{24,696},{48,144},{72,744},{96,192},{120,24},{144,240},{168... | collective-permute-start | bytes 983048 | tf_op jit(solution)/shard_map/ppermute | solution.py:83

commit v2 on v1

v2 whole, which is shorter than its diff:
```python
import functools

import jax
import jax.numpy as jnp
import numpy as np
from jax import lax
from jax.experimental import pallas as pl
from jax.experimental.pallas import tpu as pltpu
from jax.sharding import PartitionSpec as P

epsilon = 1e-05
vmem_bytes = 40 * 1024 * 1024
unit, piece = 128, 256


def pieces(blocks):
    return [(b, at, min(piece, b.shape[0])) for b in blocks for at in range(0, b.shape[0], piece)]


def load_blocks(blocks, held, sems):
    copies, to = [], 0
    for i, (block, at, depth) in enumerate(pieces(blocks)):
        rows = pl.ds(to, depth)
        copies.append((pltpu.make_async_copy(block.at[pl.ds(at, depth)], held.at[rows], sems.at[i]), rows))
        to += depth
    for copy, _ in copies:
        copy.start()
    return copies


def add_blocks(places, held, copies, pairs):
    for i, (copy, rows) in enumerate(copies):
        copy.wait()
        start = pl.multiple_of(places[i] * unit, unit)
        for tokens, total in pairs:
            total[...] += jnp.dot(tokens[:, pl.ds(start, rows.size)], held[rows], preferred_element_type=jnp.float32)


def first_kernel(n, places, tokens, others, *refs):
    blocks, (total, partial, scale, held, sems) = refs[:n], refs[n:]
    copies = load_blocks(blocks, held, sems)
    values = tokens[...].astype(jnp.float32)
    scale[...] = lax.rsqrt(jnp.mean(values * values, axis=1, keepdims=True) + epsilon)
    total[...] = jnp.zeros_like(total)
    partial[...] = jnp.zeros_like(partial)
    add_blocks(places, held, copies, [(tokens, total), (others, partial)])


def next_kernel(n, places, tokens, others, total_before, partial_before, *refs):
    blocks, (total, partial, held, sems) = refs[:n], refs[n:]
    copies = load_blocks(blocks, held, sems)
    total[...] = total_before[...]
    partial[...] = partial_before[...]
    add_blocks(places, held, copies, [(tokens, total), (others, partial)])


def last_kernel(n, places, tokens, total_before, partial_arrived, scale, *refs):
    blocks, (hidden, total, held, sems) = refs[:n], refs[n:]
    copies = load_blocks(blocks, held, sems)
    total[...] = total_before[...] + partial_arrived[...]
    add_blocks(places, held, copies, [(tokens, total)])
    wide = hidden.shape[1]
    gate = total[:, :wide] * scale[...]
    up = total[:, wide:] * scale[...]
    hidden[...] = (gate / (1.0 + jnp.exp(-gate)) * up).astype(hidden.dtype)


def call(kernel, places, arrays, blocks, out_shape, scratch=()):
    n = len(blocks)
    depth, wide = sum(b.shape[0] for b in blocks), blocks[0].shape[1]
    rows = arrays[0].shape[0]
    vmem = pl.BlockSpec(memory_space=pltpu.VMEM)
    return pl.pallas_call(
        functools.partial(kernel, n),
        out_shape=out_shape,
        in_specs=[pl.BlockSpec(memory_space=pltpu.SMEM)] + [vmem] * len(arrays) + [pl.BlockSpec(memory_space=pl.ANY)] * n,
        out_specs=jax.tree.map(lambda _: vmem, out_shape),
        scratch_shapes=list(scratch) + [pltpu.VMEM((depth, wide), blocks[0].dtype), pltpu.SemaphoreType.DMA((len(pieces(blocks)),))],
        compiler_params=pltpu.CompilerParams(vmem_limit_bytes=vmem_bytes),
        cost_estimate=pl.CostEstimate(
            flops=4 * rows * depth * wide, bytes_accessed=2 * depth * wide + 16 * rows * wide, transcendentals=0
        ),
    )(places, *arrays, *blocks)


def make_on_device(count):
    high = count // 4

    def move(where):
        pairs = []
        for f in range(count):
            y, x, c = where(f // 4, (f // 2) % 2, f % 2)
            pairs.append((f, (y % high) * 4 + (x % 2) * 2 + c % 2))
        return lambda v: lax.ppermute(v, "fsdp", pairs)

    along = move(lambda y, x, c: (y + 1 - 2 * c, x, c))
    slant = move(lambda y, x, c: (y + 1 - 2 * c, x + 1, c))
    across = move(lambda y, x, c: (y, x + 1, c))
    swap = move(lambda y, x, c: (y, x, c + 1))
    core_pairs = [[f, f + 1] for f in range(0, count, 2)]

    def place(f, steps, other, half=False):
        y, x, c = f // 4, (f // 2) % 2, f % 2
        return ((y + steps * (2 * c - 1)) % high * 2 + (x + other) % 2) * 2 + (c if half else 0)

    def places(index, *which):
        table = np.array([[place(f, *w) for w in which] for f in range(count)], np.int32)
        return lax.dynamic_index_in_dim(jnp.asarray(table), index, 0, keepdims=False)

    def join(v):
        return lax.all_gather(v, "fsdp", axis=0, tiled=True, axis_index_groups=core_pairs)

    def on_device(tokens, norm_gain, gate_weight, up_weight):
        index = lax.axis_index("fsdp")
        gain = norm_gain[:, None]
        own = jnp.concatenate([gate_weight * gain, up_weight * gain], axis=1).astype(jnp.bfloat16)
        depth, wide = own.shape
        half = lax.bitwise_and(index, 1) * depth
        chip, late = lax.optimization_barrier((join(own), tokens))

        rows = tokens.shape[0]
        sums = jax.ShapeDtypeStruct((rows, wide), jnp.float32)

        a1 = along(chip)
        b1 = slant(chip)
        others = swap(late)
        b0 = across(own)
        a2 = along(a1)
        b2 = along(b1)
        a3 = along(a2)
        total, partial, scale = call(
            first_kernel,
            places(index, (0, 0, True), (0, 1, True), (1, 0), (1, 1), (2, 0)),
            [tokens, others],
            [own, b0, a1, b1, a2],
            (sums, sums, jax.ShapeDtypeStruct((rows, 1), jnp.float32)),
        )
        b2, total = lax.optimization_barrier((b2, total))
        b3 = along(b2)
        a4 = along(lax.dynamic_slice_in_dim(a3, half, depth, 0))
        total, partial = call(
            next_kernel,
            places(index, (2, 1), (3, 0)),
            [tokens, others, total, partial],
            [b2, a3],
            (sums, sums),
        )
        b3, total = lax.optimization_barrier((b3, total))
        b4 = along(lax.dynamic_slice_in_dim(b3, half, depth, 0))
        return call(
            last_kernel,
            places(index, (3, 1), (-3, 1), (4, 0), (4, 1)),
            [tokens, total, swap(partial), scale],
            [b3, swap(b3), join(a4), join(b4)],
            jax.ShapeDtypeStruct((rows, wide // 2), jnp.bfloat16),
            [pltpu.VMEM((rows, wide), jnp.float32)],
        )

    return on_device


def solution(mesh):
    return jax.shard_map(
        make_on_device(mesh.shape["fsdp"]),
        mesh=mesh,
        in_specs=(P("fsdp", None), P("fsdp"), P("fsdp", "tensor"), P("fsdp", "tensor")),
        out_specs=P("fsdp", "tensor"),
        check_vma=False,
    )
```

time: 98.8 us -> 95.5 us (0.967)
  starting transfers between devices: 42.3 us -> 33.7 us
  local copies, waits for them, and re-layouts: 2.15 us -> 7.09 us
  waiting for transfers between devices: 25.8 us -> 23.3 us
  blocking collectives: 17.1 us -> 19.3 us
    ppermute x15 -> x12, starting transfers between devices: 42.3 us -> 33.7 us  [move(): return lambda v: lax.ppermute(v, 'fsdp', pairs)]
    unnamed x2 -> x14, local copies, waits for them, and re-layouts: 0.01 us -> 2.9 us
    ppermute x15 -> x12, waiting for transfers between devices: 25.8 us -> 23.3 us  [move(): return lambda v: lax.ppermute(v, 'fsdp', pairs)]
    all_gather x3, blocking collectives: 17.1 us -> 19.3 us  [join(): lax.all_gather(v, 'fsdp', axis=0, tiled=True, axis_index_groups=core_pairs)]
    dynamic_slice x2, local copies, waits for them, and re-layouts: 0.05 us -> 2.09 us  [the longest x1 1.09 us: on_device(): a4 = along(lax.dynamic_slice_in_dim(a3, half, depth, 0))]
  transfers between devices with their start and end apart: 15 -> 12, of which waited for: 5 -> 4; matrix products, arithmetic and copies ran while one was open for 2% -> 4% of each run, Pallas kernels for 7% -> 7%
where the time goes in v2:
time: 95.5 us; the launch traced here: 94.7 us
  starting transfers between devices  33.7 us (35%)
  waiting for transfers between devices  23.3 us (24%)
  blocking collectives  19.3 us (20%)
  Pallas kernels  9.83 us (10%)
  local copies, waits for them, and re-layouts  7.09 us (7%)
  other arithmetic  1.28 us (1%)
    ppermute x12, starting transfers between devices, move(): return lambda v: lax.ppermute(v, 'fsdp', pairs)  33.7 us
    ppermute x12, waiting for transfers between devices, move(): return lambda v: lax.ppermute(v, 'fsdp', pairs)  23.3 us
    all_gather x3, blocking collectives, join(): lax.all_gather(v, 'fsdp', axis=0, tiled=True, axis_index_groups=core_pairs)  19.3 us
    pallas_call x3, Pallas kernels, call(): pl.pallas_call(functools.partial(kernel, n), out_shape=out_shape, in_spec...  9.83 us
    unnamed x14, local copies, waits for them, and re-layouts  2.9 us
    squeeze x3, local copies, waits for them, and re-layouts, places(): lax.dynamic_index_in_dim(jnp.asarray(table), index, 0, keepdims=False)  2.1 us
  transfers between devices with their start and end apart: 12, of which 4 were waited for; matrix products, arithmetic and copies ran while one was open for 4% of the time, Pallas kernels for 7%

profile of v2, /device:TPU:1, one launch (start us, length us, event | category | flops | bytes accessed | tf_op | source)
XLA Modules:
  0.0 94.7 jit_solution(10168555677460226958)
XLA Ops:
  0.0 1.3 %multiply_convert_fusion.1 = (bf16[128,640]{1,0:T(8,128)(2,1)S(1)}, bf16[128,640]{1,0:T(8,128)(2,1)S(1)}) fusion(bf16[128,640]{1,0:T(8,128)(2,1)} %param.9, f32[128]{0:T(128)} %param.8, bf16[128,640]{1,0:T(8,128)(2,1)} %param.10), kind=kLoop, calls=%fused_computation.2 | loop fusion | flops 491520 | bytes 655872 | tf_op jit(solution)/shard_map/convert
  1.3 12.4 %all_gather.9 = bf16[256,1280]{1,0:T(8,128)(2,1)S(1)} all-gather(bf16[128,1280]{1,0:T(8,128)(2,1)S(1)} %pad_maximum_fusion.refs_0_), channel_id=1, replica_groups={{0,24},{48,72},{96,120},{144,168},{192,216},{240,264},{288,312},{336,36..., dimensions={0}, use_global_device_ids=true | all-gather | bytes 983040 | tf_op jit(solution)/shard_map/all_gather | solution.py:111
  13.7 2.3 %collective-permute-start.2 = (bf16[192,4096]{1,0:T(8,128)(2,1)S(1)}, bf16[192,4096]{1,0:T(8,128)(2,1)S(1)}, u32[]{:S(2)}, u32[]{:S(2)}) collective-permute-start(bf16[192,4096]{1,0:T(8,128)(2,1)S(1)} %copy-done), channel_id=1, source_target_pairs={{0,24},{24,0},{48,72},{72,48},{96,120},{120,96},{144,168},{168,144... | collective-permute-start | bytes 4718600 | tf_op jit(solution)/shard_map/ppermute | solution.py:94
  16.0 1.9 %collective-permute-start.4 = (bf16[256,1280]{1,0:T(8,128)(2,1)S(1)}, bf16[256,1280]{1,0:T(8,128)(2,1)S(1)}, u32[]{:S(2)}, u32[]{:S(2)}) collective-permute-start(bf16[256,1280]{1,0:T(8,128)(2,1)S(1)} %all_gather.9), channel_id=1, source_target_pairs={{0,96},{24,696},{48,144},{72,744},{96,192},{120,24},{144,240},{168... | collective-permute-start | bytes 1966088 | tf_op jit(solution)/shard_map/ppermute | solution.py:94
  17.9 1.9 %collective-permute-start = (bf16[256,1280]{1,0:T(8,128)(2,1)S(1)}, bf16[256,1280]{1,0:T(8,128)(2,1)}, u32[]{:S(2)}, u32[]{:S(2)}) collective-permute-start(bf16[256,1280]{1,0:T(8,128)(2,1)S(1)} %all_gather.9), channel_id=1, source_target_pairs={{0,144},{24,744},{48,96},{72,696},{96,240},{120,72},{144,192},{168... | collective-permute-start | bytes 1966088 | tf_op jit(solution)/shard_map/ppermute | solution.py:94
  19.9 7.9 %collective-permute-done.4.refs_2_ = bf16[256,1280]{1,0:T(8,128)(2,1)S(1)} collective-permute-done((bf16[256,1280]{1,0:T(8,128)(2,1)S(1)}, bf16[256,1280]{1,0:T(8,128)(2,1)S(1)}, u32[]{:S(2)}, u32[]{:S(2)}) %collective-permute-start.4) | collective-permute-done | bytes 655392 | tf_op jit(solution)/shard_map/ppermute | solution.py:94
  27.7 3.1 %collective-permute-start.5 = (bf16[256,1280]{1,0:T(8,128)(2,1)S(1)}, bf16[256,1280]{1,0:T(8,128)(2,1)}, u32[]{:S(2)}, u32[]{:S(2)}) collective-permute-start(bf16[256,1280]{1,0:T(8,128)(2,1)S(1)} %collective-permute-done.4.refs_2_), channel_id=1, source_target_pairs={{0,96},{24,696},{48,144},{72,744},{96,192},{120,24},{144,240},{168... | collective-permute-start | bytes 1966088 | tf_op jit(solution)/shard_map/ppermute | solution.py:94
  31.7 7.1 %collective-permute-done.refs_3_ = bf16[256,1280]{1,0:T(8,128)(2,1)} collective-permute-done((bf16[256,1280]{1,0:T(8,128)(2,1)S(1)}, bf16[256,1280]{1,0:T(8,128)(2,1)}, u32[]{:S(2)}, u32[]{:S(2)}) %collective-permute-start) | collective-permute-done | bytes 655392 | tf_op jit(solution)/shard_map/ppermute | solution.py:94
  38.8 1.9 %collective-permute-start.1 = (bf16[256,1280]{1,0:T(8,128)(2,1)}, bf16[256,1280]{1,0:T(8,128)(2,1)}, u32[]{:S(2)}, u32[]{:S(2)}) collective-permute-start(bf16[256,1280]{1,0:T(8,128)(2,1)} %collective-permute-done.refs_3_), channel_id=1, source_target_pairs={{0,96},{24,696},{48,144},{72,744},{96,192},{120,24},{144,240},{168... | collective-permute-start | bytes 1966088 | tf_op jit(solution)/shard_map/ppermute | solution.py:94
  40.7 7.3 %collective-permute-start.3 = (bf16[128,1280]{1,0:T(8,128)(2,1)S(1)}, bf16[128,1280]{1,0:T(8,128)(2,1)}, u32[]{:S(2)}, u32[]{:S(2)}) collective-permute-start(bf16[128,1280]{1,0:T(8,128)(2,1)S(1)} %pad_maximum_fusion.refs_0_), channel_id=1, source_target_pairs={{0,48},{24,72},{48,0},{72,24},{96,144},{120,168},{144,96},{168,120... | collective-permute-start | bytes 983048 | tf_op jit(solution)/shard_map/ppermute | solution.py:94
  48.0 1.9 %collective-permute-start.7 = (bf16[256,1280]{1,0:T(8,128)(2,1)}, bf16[256,1280]{1,0:T(8,128)(2,1)}, u32[]{:S(2)}, u32[]{:S(2)}) collective-permute-start(bf16[256,1280]{1,0:T(8,128)(2,1)} %collective-permute-done.5.refs_4_), channel_id=1, source_target_pairs={{0,96},{24,696},{48,144},{72,744},{96,192},{120,24},{144,240},{168... | collective-permute-start | bytes 1966088 | tf_op jit(solution)/shard_map/ppermute | solution.py:94
  50.6 5.2 %collective-permute-done.3.refs_1_ = bf16[128,1280]{1,0:T(8,128)(2,1)} collective-permute-done((bf16[128,1280]{1,0:T(8,128)(2,1)S(1)}, bf16[128,1280]{1,0:T(8,128)(2,1)}, u32[]{:S(2)}, u32[]{:S(2)}) %collective-permute-start.3) | collective-permute-done | bytes 327712 | tf_op jit(solution)/shard_map/ppermute | solution.py:94
  55.9 1.1 %copy-done.4 = bf16[256,1280]{1,0:T(8,128)(2,1)S(1)} copy-done((bf16[256,1280]{1,0:T(8,128)(2,1)S(1)}, bf16[256,1280]{1,0:T(8,128)(2,1)}, u32[]{:S(2)}) %copy-start.4) | copy-done | bytes 655384
  57.0 3.0 %shard_map.73 = (f32[192,1280]{1,0:T(8,128)S(1)}, f32[192,1280]{1,0:T(8,128)S(1)}, f32[192,1]{1,0:T(8,128)S(1)}) custom-call(s32[5]{0:T(128)S(1)} %fusion.1.places, bf16[192,4096]{1,0:T(8,128)(2,1)S(1)} %copy-done, bf16[192,4096]{1,0:T(8,128)(2,1)S(1)} %collective-permute-done.2.others, bf16[128,1280]{1,0:T(8,128)(2,1)S(1)} %pad_maximum_fusion.refs_0_, ...), custom_call_target="tpu_custom_call" | custom-call | flops 1006632960 | bytes 6553600 | tf_op jit(solution)/shard_map/pallas_call | solution.py:73
  60.0 1.9 %collective-permute-start.6 = (bf16[256,1280]{1,0:T(8,128)(2,1)}, bf16[256,1280]{1,0:T(8,128)(2,1)}, u32[]{:S(2)}, u32[]{:S(2)}) collective-permute-start(bf16[256,1280]{1,0:T(8,128)(2,1)} %collective-permute-done.1.refs_0_), channel_id=1, source_target_pairs={{0,96},{24,696},{48,144},{72,744},{96,192},{120,24},{144,240},{168... | collective-permute-start | bytes 1966088 | tf_op jit(solution)/shard_map/ppermute | solution.py:94
  62.7 3.4 %shard_map.74 = (f32[192,1280]{1,0:T(8,128)S(1)}, f32[192,1280]{1,0:T(8,128)}) custom-call(s32[2]{0:T(128)S(1)} %fusion.2.places, bf16[192,4096]{1,0:T(8,128)(2,1)S(1)} %copy-done, bf16[192,4096]{1,0:T(8,128)(2,1)S(1)} %collective-permute-done.2.others, f32[192,1280]{1,0:T(8,128)S(1)} %get-tuple-element.20.total_before, ...), custom_call_target="tpu_custom_call" | custom-call | flops 503316480 | bytes 5242880 | tf_op jit(solution)/shard_map/pallas_call | solution.py:73
  67.0 2.8 %collective-permute-start.8 = (f32[192,1280]{1,0:T(8,128)}, f32[192,1280]{1,0:T(8,128)S(1)}, u32[]{:S(2)}, u32[]{:S(2)}) collective-permute-start(f32[192,1280]{1,0:T(8,128)} %get-tuple-element.24), channel_id=1, source_target_pairs={{0,24},{24,0},{48,72},{72,48},{96,120},{120,96},{144,168},{168,144... | collective-permute-start | bytes 2949128 | tf_op jit(solution)/shard_map/ppermute | solution.py:94
  70.9 4.8 %collective-permute-start.10 = (bf16[128,1280]{1,0:T(8,128)(2,1)S(1)}, bf16[128,1280]{1,0:T(8,128)(2,1)S(1)}, u32[]{:S(2)}, u32[]{:S(2)}) collective-permute-start(bf16[128,1280]{1,0:T(8,128)(2,1)S(1)} %constant_dynamic-slice_fusion.1), channel_id=1, source_target_pairs={{0,96},{24,696},{48,144},{72,744},{96,192},{120,24},{144,240},{168... | collective-permute-start | bytes 983048 | tf_op jit(solution)/shard_map/ppermute | solution.py:94
  75.8 1.9 %collective-permute-start.9 = (bf16[256,1280]{1,0:T(8,128)(2,1)}, bf16[256,1280]{1,0:T(8,128)(2,1)S(1)}, u32[]{:S(2)}, u32[]{:S(2)}) collective-permute-start(bf16[256,1280]{1,0:T(8,128)(2,1)} %collective-permute-done.6.refs_0_), channel_id=1, source_target_pairs={{0,24},{24,0},{48,72},{72,48},{96,120},{120,96},{144,168},{168,144... | collective-permute-start | bytes 1966088 | tf_op jit(solution)/shard_map/ppermute | solution.py:94
  78.7 1.9 %collective-permute-start.11 = (bf16[128,1280]{1,0:T(8,128)(2,1)S(1)}, bf16[128,1280]{1,0:T(8,128)(2,1)S(1)}, u32[]{:S(2)}, u32[]{:S(2)}) collective-permute-start(bf16[128,1280]{1,0:T(8,128)(2,1)S(1)} %constant_dynamic-slice_fusion), channel_id=1, source_target_pairs={{0,96},{24,696},{48,144},{72,744},{96,192},{120,24},{144,240},{168... | collective-permute-start | bytes 983048 | tf_op jit(solution)/shard_map/ppermute | solution.py:94
  81.3 2.4 %all_gather.10.refs_2_ = bf16[256,1280]{1,0:T(8,128)(2,1)S(1)} all-gather(bf16[128,1280]{1,0:T(8,128)(2,1)S(1)} %collective-permute-done.10), channel_id=1, replica_groups={{0,24},{48,72},{96,120},{144,168},{192,216},{240,264},{288,312},{336,36..., dimensions={0}, use_global_device_ids=true | all-gather | bytes 983040 | tf_op jit(solution)/shard_map/all_gather | solution.py:111
  83.7 3.1 %collective-permute-done.11 = bf16[128,1280]{1,0:T(8,128)(2,1)S(1)} collective-permute-done((bf16[128,1280]{1,0:T(8,128)(2,1)S(1)}, bf16[128,1280]{1,0:T(8,128)(2,1)S(1)}, u32[]{:S(2)}, u32[]{:S(2)}) %collective-permute-start.11) | collective-permute-done | bytes 327712 | tf_op jit(solution)/shard_map/ppermute | solution.py:94
  86.8 4.5 %all_gather.11.refs_3_ = bf16[256,1280]{1,0:T(8,128)(2,1)S(1)} all-gather(bf16[128,1280]{1,0:T(8,128)(2,1)S(1)} %collective-permute-done.11), channel_id=1, replica_groups={{0,24},{48,72},{96,120},{144,168},{192,216},{240,264},{288,312},{336,36..., dimensions={0}, use_global_device_ids=true | all-gather | bytes 983040 | tf_op jit(solution)/shard_map/all_gather | solution.py:111
  91.3 3.4 %shard_map.75 = bf16[192,640]{1,0:T(8,128)(2,1)} custom-call(s32[4]{0:T(128)S(1)} %fusion.places, bf16[192,4096]{1,0:T(8,128)(2,1)S(1)} %copy-done, f32[192,1280]{1,0:T(8,128)S(1)} %copy-done.2, f32[192,1280]{1,0:T(8,128)S(1)} %collective-permute-done.8.partial_arrived, f32[192,1]{1,0:T(8,128)S(1)} %copy-done.6, ...), custom_call_target="tpu_custom_call" | custom-call | flops 1006632960 | bytes 6553600 | tf_op jit(solution)/shard_map/pallas_call | solution.py:73
  (27 shorter events, 6.0 us)
Async XLA Ops:
  0.0 13.7 %copy-start = (bf16[192,4096]{1,0:T(8,128)(2,1)S(1)}, bf16[192,4096]{1,0:T(8,128)(2,1)}, u32[]{:S(2)}) copy-start(bf16[192,4096]{1,0:T(8,128)(2,1)} %tokens.5) | copy-start | bytes 4718596
  13.7 42.2 %collective-permute-start.2 = (bf16[192,4096]{1,0:T(8,128)(2,1)S(1)}, bf16[192,4096]{1,0:T(8,128)(2,1)S(1)}, u32[]{:S(2)}, u32[]{:S(2)}) collective-permute-start(bf16[192,4096]{1,0:T(8,128)(2,1)S(1)} %copy-done), channel_id=1, source_target_pairs={{0,24},{24,0},{48,72},{72,48},{96,120},{120,96},{144,168},{168,144... | collective-permute-start | bytes 4718600 | tf_op jit(solution)/shard_map/ppermute | solution.py:94
  16.0 11.7 %collective-permute-start.4 = (bf16[256,1280]{1,0:T(8,128)(2,1)S(1)}, bf16[256,1280]{1,0:T(8,128)(2,1)S(1)}, u32[]{:S(2)}, u32[]{:S(2)}) collective-permute-start(bf16[256,1280]{1,0:T(8,128)(2,1)S(1)} %all_gather.9), channel_id=1, source_target_pairs={{0,96},{24,696},{48,144},{72,744},{96,192},{120,24},{144,240},{168... | collective-permute-start | bytes 1966088 | tf_op jit(solution)/shard_map/ppermute | solution.py:94
  17.9 20.9 %collective-permute-start = (bf16[256,1280]{1,0:T(8,128)(2,1)S(1)}, bf16[256,1280]{1,0:T(8,128)(2,1)}, u32[]{:S(2)}, u32[]{:S(2)}) collective-permute-start(bf16[256,1280]{1,0:T(8,128)(2,1)S(1)} %all_gather.9), channel_id=1, source_target_pairs={{0,144},{24,744},{48,96},{72,696},{96,240},{120,72},{144,192},{168... | collective-permute-start | bytes 1966088 | tf_op jit(solution)/shard_map/ppermute | solution.py:94
  27.7 20.3 %collective-permute-start.5 = (bf16[256,1280]{1,0:T(8,128)(2,1)S(1)}, bf16[256,1280]{1,0:T(8,128)(2,1)}, u32[]{:S(2)}, u32[]{:S(2)}) collective-permute-start(bf16[256,1280]{1,0:T(8,128)(2,1)S(1)} %collective-permute-done.4.refs_2_), channel_id=1, source_target_pairs={{0,96},{24,696},{48,144},{72,744},{96,192},{120,24},{144,240},{168... | collective-permute-start | bytes 1966088 | tf_op jit(solution)/shard_map/ppermute | solution.py:94
  30.9 0.8 copy-start.3
  38.8 21.2 %collective-permute-start.1 = (bf16[256,1280]{1,0:T(8,128)(2,1)}, bf16[256,1280]{1,0:T(8,128)(2,1)}, u32[]{:S(2)}, u32[]{:S(2)}) collective-permute-start(bf16[256,1280]{1,0:T(8,128)(2,1)} %collective-permute-done.refs_3_), channel_id=1, source_target_pairs={{0,96},{24,696},{48,144},{72,744},{96,192},{120,24},{144,240},{168... | collective-permute-start | bytes 1966088 | tf_op jit(solution)/shard_map/ppermute | solution.py:94
  40.7 15.2 %collective-permute-start.3 = (bf16[128,1280]{1,0:T(8,128)(2,1)S(1)}, bf16[128,1280]{1,0:T(8,128)(2,1)}, u32[]{:S(2)}, u32[]{:S(2)}) collective-permute-start(bf16[128,1280]{1,0:T(8,128)(2,1)S(1)} %pad_maximum_fusion.refs_0_), channel_id=1, source_target_pairs={{0,48},{24,72},{48,0},{72,24},{96,144},{120,168},{144,96},{168,120... | collective-permute-start | bytes 983048 | tf_op jit(solution)/shard_map/ppermute | solution.py:94
  48.0 14.7 %collective-permute-start.7 = (bf16[256,1280]{1,0:T(8,128)(2,1)}, bf16[256,1280]{1,0:T(8,128)(2,1)}, u32[]{:S(2)}, u32[]{:S(2)}) collective-permute-start(bf16[256,1280]{1,0:T(8,128)(2,1)} %collective-permute-done.5.refs_4_), channel_id=1, source_target_pairs={{0,96},{24,696},{48,144},{72,744},{96,192},{120,24},{144,240},{168... | collective-permute-start | bytes 1966088 | tf_op jit(solution)/shard_map/ppermute | solution.py:94
  55.9 1.1 %copy-start.4 = (bf16[256,1280]{1,0:T(8,128)(2,1)S(1)}, bf16[256,1280]{1,0:T(8,128)(2,1)}, u32[]{:S(2)}) copy-start(bf16[256,1280]{1,0:T(8,128)(2,1)} %copy-done.3) | copy-start | bytes 1966084
  60.0 6.0 %copy-start.5 = (f32[192,1]{1,0:T(8,128)}, f32[192,1]{1,0:T(8,128)S(1)}, u32[]{:S(2)}) copy-start(f32[192,1]{1,0:T(8,128)S(1)} %get-tuple-element.25.scale) | copy-start | bytes 2308
  60.0 15.7 %collective-permute-start.6 = (bf16[256,1280]{1,0:T(8,128)(2,1)}, bf16[256,1280]{1,0:T(8,128)(2,1)}, u32[]{:S(2)}, u32[]{:S(2)}) collective-permute-start(bf16[256,1280]{1,0:T(8,128)(2,1)} %collective-permute-done.1.refs_0_), channel_id=1, source_target_pairs={{0,96},{24,696},{48,144},{72,744},{96,192},{120,24},{144,240},{168... | collective-permute-start | bytes 1966088 | tf_op jit(solution)/shard_map/ppermute | solution.py:94
  66.1 1.0 %copy-start.1 = (f32[192,1280]{1,0:T(8,128)}, f32[192,1280]{1,0:T(8,128)S(1)}, u32[]{:S(2)}) copy-start(f32[192,1280]{1,0:T(8,128)S(1)} %get-tuple-element.23.total_before) | copy-start | bytes 2949124
  67.0 24.3 %collective-permute-start.8 = (f32[192,1280]{1,0:T(8,128)}, f32[192,1280]{1,0:T(8,128)S(1)}, u32[]{:S(2)}, u32[]{:S(2)}) collective-permute-start(f32[192,1280]{1,0:T(8,128)} %get-tuple-element.24), channel_id=1, source_target_pairs={{0,24},{24,0},{48,72},{72,48},{96,120},{120,96},{144,168},{168,144... | collective-permute-start | bytes 2949128 | tf_op jit(solution)/shard_map/ppermute | solution.py:94
  69.8 21.5 %copy-start.2 = (f32[192,1280]{1,0:T(8,128)S(1)}, f32[192,1280]{1,0:T(8,128)}, u32[]{:S(2)}) copy-start(f32[192,1280]{1,0:T(8,128)} %copy-done.1) | copy-start | bytes 2949124
  69.8 21.5 %copy-start.6 = (f32[192,1]{1,0:T(8,128)S(1)}, f32[192,1]{1,0:T(8,128)}, u32[]{:S(2)}) copy-start(f32[192,1]{1,0:T(8,128)} %copy-done.5) | copy-start | bytes 2308
  70.9 10.4 %collective-permute-start.10 = (bf16[128,1280]{1,0:T(8,128)(2,1)S(1)}, bf16[128,1280]{1,0:T(8,128)(2,1)S(1)}, u32[]{:S(2)}, u32[]{:S(2)}) collective-permute-start(bf16[128,1280]{1,0:T(8,128)(2,1)S(1)} %constant_dynamic-slice_fusion.1), channel_id=1, source_target_pairs={{0,96},{24,696},{48,144},{72,744},{96,192},{120,24},{144,240},{168... | collective-permute-start | bytes 983048 | tf_op jit(solution)/shard_map/ppermute | solution.py:94
  75.8 15.5 %collective-permute-start.9 = (bf16[256,1280]{1,0:T(8,128)(2,1)}, bf16[256,1280]{1,0:T(8,128)(2,1)S(1)}, u32[]{:S(2)}, u32[]{:S(2)}) collective-permute-start(bf16[256,1280]{1,0:T(8,128)(2,1)} %collective-permute-done.6.refs_0_), channel_id=1, source_target_pairs={{0,24},{24,0},{48,72},{72,48},{96,120},{120,96},{144,168},{168,144... | collective-permute-start | bytes 1966088 | tf_op jit(solution)/shard_map/ppermute | solution.py:94
  78.7 8.1 %collective-permute-start.11 = (bf16[128,1280]{1,0:T(8,128)(2,1)S(1)}, bf16[128,1280]{1,0:T(8,128)(2,1)S(1)}, u32[]{:S(2)}, u32[]{:S(2)}) collective-permute-start(bf16[128,1280]{1,0:T(8,128)(2,1)S(1)} %constant_dynamic-slice_fusion), channel_id=1, source_target_pairs={{0,96},{24,696},{48,144},{72,744},{96,192},{120,24},{144,240},{168... | collective-permute-start | bytes 983048 | tf_op jit(solution)/shard_map/ppermute | solution.py:94

commit v3 on v2

v3 whole, which is shorter than its diff:
```python
import functools

import jax
import jax.numpy as jnp
from jax import lax
from jax.experimental import pallas as pl
from jax.experimental.pallas import tpu as pltpu
from jax.sharding import PartitionSpec as P

epsilon = 1e-05
vmem_bytes = 16 * 1024 * 1024


def column(spec, high):
    steps, other, half = spec
    index = lax.axis_index("fsdp")
    core = lax.rem(index, 2)
    x = lax.rem(lax.div(index, 2), 2)
    y = lax.rem(lax.div(index, 4) + (steps * (2 * core - 1) + high), high)
    return (y * 2 + (1 - x if other else x)) * 2 + (core if half else 0)


def add_blocks(specs, high, blocks, pairs):
    for spec, block in zip(specs, blocks):
        depth = block.shape[0]
        unit = depth if spec[2] else depth // 2
        start = pl.multiple_of(column(spec, high) * unit, unit)
        for tokens, total in pairs:
            total[...] += jnp.dot(tokens[:, pl.ds(start, depth)], block[...], preferred_element_type=jnp.float32)


def first_kernel(add, n, tokens, others, *refs):
    blocks, (total, partial, scale) = refs[:n], refs[n:]
    values = tokens[...].astype(jnp.float32)
    scale[...] = lax.rsqrt(jnp.mean(values * values, axis=1, keepdims=True) + epsilon)
    total[...] = jnp.zeros_like(total)
    partial[...] = jnp.zeros_like(partial)
    add(blocks, [(tokens, total), (others, partial)])


def second_kernel(add, n, tokens, others, total_before, partial_before, *refs):
    blocks, (total, partial) = refs[:n], refs[n:]
    total[...] = total_before[...]
    partial[...] = partial_before[...]
    add(blocks, [(tokens, total), (others, partial)])


def third_kernel(add, n, tokens, total_before, partial_arrived, *refs):
    blocks, (total,) = refs[:n], refs[n:]
    total[...] = total_before[...] + partial_arrived[...]
    add(blocks, [(tokens, total)])


def last_kernel(add, n, tokens, total_before, scale, *refs):
    blocks, (hidden, total) = refs[:n], refs[n:]
    total[...] = total_before[...]
    add(blocks, [(tokens, total)])
    wide = hidden.shape[1]
    gate = total[:, :wide] * scale[...]
    up = total[:, wide:] * scale[...]
    hidden[...] = (gate / (1.0 + jnp.exp(-gate)) * up).astype(hidden.dtype)


def call(kernel, *, high, specs, arrays, blocks, out_shape, scratch=()):
    n = len(blocks)
    depth, wide = sum(b.shape[0] for b in blocks), blocks[0].shape[1]
    rows = arrays[0].shape[0]
    vmem = pl.BlockSpec(memory_space=pltpu.VMEM)
    return pl.pallas_call(
        functools.partial(kernel, functools.partial(add_blocks, specs, high), n),
        out_shape=out_shape,
        in_specs=[vmem] * (len(arrays) + n),
        out_specs=jax.tree.map(lambda _: vmem, out_shape),
        scratch_shapes=list(scratch),
        compiler_params=pltpu.CompilerParams(vmem_limit_bytes=vmem_bytes),
        cost_estimate=pl.CostEstimate(
            flops=4 * rows * depth * wide, bytes_accessed=2 * depth * wide + 16 * rows * wide, transcendentals=0
        ),
    )(*arrays, *blocks)


def make_on_device(count):
    high = count // 4

    def move(where):
        pairs = []
        for f in range(count):
            y, x, c = where(f // 4, (f // 2) % 2, f % 2)
            pairs.append((f, (y % high) * 4 + (x % 2) * 2 + c % 2))
        return lambda v: lax.ppermute(v, "fsdp", pairs)

    along = move(lambda y, x, c: (y + 1 - 2 * c, x, c))
    slant = move(lambda y, x, c: (y + 1 - 2 * c, x + 1, c))
    across = move(lambda y, x, c: (y, x + 1, c))
    swap = move(lambda y, x, c: (y, x, c + 1))
    core_pairs = [[f, f + 1] for f in range(0, count, 2)]

    def join(v):
        return lax.all_gather(v, "fsdp", axis=0, tiled=True, axis_index_groups=core_pairs)

    def on_device(tokens, norm_gain, gate_weight, up_weight):
        index = lax.axis_index("fsdp")
        gain = norm_gain[:, None]
        own = jnp.concatenate([gate_weight * gain, up_weight * gain], axis=1).astype(jnp.bfloat16)
        depth, wide = own.shape
        half = lax.bitwise_and(index, 1) * depth
        chip = join(own)
        rows = tokens.shape[0]
        sums = jax.ShapeDtypeStruct((rows, wide), jnp.float32)
        step = functools.partial(call, high=high)

        late0 = tokens
        a1 = along(chip)
        b1 = slant(chip)
        others = swap(late0)
        a2 = along(a1)
        b2 = along(b1)
        a3 = along(a2)
        total, partial, scale = step(
            first_kernel,
            specs=[(0, 0, 1), (1, 0, 0), (1, 1, 0), (2, 0, 0)],
            arrays=[tokens, others],
            blocks=[own, a1, b1, a2],
            out_shape=(sums, sums, jax.ShapeDtypeStruct((rows, 1), jnp.float32)),
        )
        b2, total = lax.optimization_barrier((b2, total))
        b2, chip = lax.optimization_barrier((b2, chip))
        b0 = across(chip)
        b3 = along(b2)
        a4 = along(lax.dynamic_slice_in_dim(a3, half, depth, 0))
        total, partial = step(
            second_kernel,
            specs=[(2, 1, 0), (3, 0, 0)],
            arrays=[tokens, others, total, partial],
            blocks=[b2, a3],
            out_shape=(sums, sums),
        )
        b3, total = lax.optimization_barrier((b3, total))
        bs = lax.dynamic_slice_in_dim(b3, half, depth, 0)
        b4 = along(bs)
        a4, late = lax.optimization_barrier((a4, b3))
        partial = swap(partial)
        total = step(
            third_kernel,
            specs=[(0, 1, 0), (3, 1, 0), (-3, 1, 0), (4, 0, 0)],
            arrays=[tokens, total, partial],
            blocks=[b0, b3, swap(late), join(a4)],
            out_shape=sums,
        )
        b4, total = lax.optimization_barrier((b4, total))
        return step(
            last_kernel,
            specs=[(4, 1, 0)],
            arrays=[tokens, total, scale],
            blocks=[join(b4)],
            out_shape=jax.ShapeDtypeStruct((rows, wide // 2), jnp.bfloat16),
            scratch=[pltpu.VMEM((rows, wide), jnp.float32)],
        )

    return on_device


def solution(mesh):
    return jax.shard_map(
        make_on_device(mesh.shape["fsdp"]),
        mesh=mesh,
        in_specs=(P("fsdp", None), P("fsdp"), P("fsdp", "tensor"), P("fsdp", "tensor")),
        out_specs=P("fsdp", "tensor"),
        check_vma=False,
    )
```

time: 95.5 us -> 96 us (level)
  waiting for transfers between devices: 23.3 us -> 27.9 us
  Pallas kernels: 9.83 us -> 7.41 us
  blocking collectives: 19.3 us -> 17.6 us
    ppermute x12, waiting for transfers between devices: 23.3 us -> 27.9 us  [move(): return lambda v: lax.ppermute(v, 'fsdp', pairs)]
    pallas_call x3 -> x4, Pallas kernels: 9.83 us -> 7.41 us  [call(): pl.pallas_call(functools.partial(kernel, functools.partial(add_blocks, sp...]
    squeeze x3 -> x0, local copies, waits for them, and re-layouts: 2.1 us -> none  [places(): lax.dynamic_index_in_dim(jnp.asarray(table), index, 0, keepdims=False)]
    all_gather x3, blocking collectives: 19.3 us -> 17.6 us  [join(): lax.all_gather(v, 'fsdp', axis=0, tiled=True, axis_index_groups=core_pairs)]
    unnamed x14, local copies, waits for them, and re-layouts: 2.9 us -> 4.36 us
  transfers between devices with their start and end apart: 12 -> 12, of which waited for: 4 -> 6; matrix products, arithmetic and copies ran while one was open for 4% -> 2% of each run, Pallas kernels for 7% -> 7%
where the time goes in v3:
time: 96 us; the launch traced here: 95.3 us
  starting transfers between devices  34.6 us (36%)
  waiting for transfers between devices  27.9 us (29%)
  blocking collectives  17.6 us (18%)
  Pallas kernels  7.41 us (8%)
  local copies, waits for them, and re-layouts  6.35 us (7%)
  other arithmetic  1.28 us (1%)
    ppermute x12, starting transfers between devices, move(): return lambda v: lax.ppermute(v, 'fsdp', pairs)  34.6 us
    ppermute x12, waiting for transfers between devices, move(): return lambda v: lax.ppermute(v, 'fsdp', pairs)  27.9 us
    all_gather x3, blocking collectives, join(): lax.all_gather(v, 'fsdp', axis=0, tiled=True, axis_index_groups=core_pairs)  17.6 us
    pallas_call x4, Pallas kernels, call(): pl.pallas_call(functools.partial(kernel, functools.partial(add_blocks, sp...  7.41 us
    unnamed x14, local copies, waits for them, and re-layouts  4.36 us
  transfers between devices with their start and end apart: 12, of which 6 were waited for; matrix products, arithmetic and copies ran while one was open for 2% of the time, Pallas kernels for 7%

profile of v3, /device:TPU:1, one launch (start us, length us, event | category | flops | bytes accessed | tf_op | source)
XLA Modules:
  0.0 95.3 jit_solution(4418739807471088837)
XLA Ops:
  0.0 1.3 %multiply_convert_fusion.1 = (bf16[128,640]{1,0:T(8,128)(2,1)S(1)}, bf16[128,640]{1,0:T(8,128)(2,1)S(1)}) fusion(bf16[128,640]{1,0:T(8,128)(2,1)} %param.6, f32[128]{0:T(128)} %param.5, bf16[128,640]{1,0:T(8,128)(2,1)} %param.7), kind=kLoop, calls=%fused_computation.2 | loop fusion | flops 491520 | bytes 655872 | tf_op jit(solution)/shard_map/convert
  1.3 12.4 %all_gather.9 = bf16[256,1280]{1,0:T(8,128)(2,1)S(1)} all-gather(bf16[128,1280]{1,0:T(8,128)(2,1)S(1)} %pad_maximum_fusion.refs_0_), channel_id=1, replica_groups={{0,24},{48,72},{96,120},{144,168},{192,216},{240,264},{288,312},{336,36..., dimensions={0}, use_global_device_ids=true | all-gather | bytes 983040 | tf_op jit(solution)/shard_map/all_gather | solution.py:99
  13.7 1.9 %collective-permute-start.3 = (bf16[256,1280]{1,0:T(8,128)(2,1)S(1)}, bf16[256,1280]{1,0:T(8,128)(2,1)S(1)}, u32[]{:S(2)}, u32[]{:S(2)}) collective-permute-start(bf16[256,1280]{1,0:T(8,128)(2,1)S(1)} %all_gather.9), channel_id=1, source_target_pairs={{0,96},{24,696},{48,144},{72,744},{96,192},{120,24},{144,240},{168... | collective-permute-start | bytes 1966088 | tf_op jit(solution)/shard_map/ppermute | solution.py:90
  15.6 2.3 %collective-permute-start.2 = (bf16[192,4096]{1,0:T(8,128)(2,1)S(1)}, bf16[192,4096]{1,0:T(8,128)(2,1)S(1)}, u32[]{:S(2)}, u32[]{:S(2)}) collective-permute-start(bf16[192,4096]{1,0:T(8,128)(2,1)S(1)} %copy-done), channel_id=1, source_target_pairs={{0,24},{24,0},{48,72},{72,48},{96,120},{120,96},{144,168},{168,144... | collective-permute-start | bytes 4718600 | tf_op jit(solution)/shard_map/ppermute | solution.py:90
  17.9 1.9 %collective-permute-start = (bf16[256,1280]{1,0:T(8,128)(2,1)S(1)}, bf16[256,1280]{1,0:T(8,128)(2,1)S(1)}, u32[]{:S(2)}, u32[]{:S(2)}) collective-permute-start(bf16[256,1280]{1,0:T(8,128)(2,1)S(1)} %all_gather.9), channel_id=1, source_target_pairs={{0,144},{24,744},{48,96},{72,696},{96,240},{120,72},{144,192},{168... | collective-permute-start | bytes 1966088 | tf_op jit(solution)/shard_map/ppermute | solution.py:90
  19.9 5.5 %collective-permute-done.3.refs_1_ = bf16[256,1280]{1,0:T(8,128)(2,1)S(1)} collective-permute-done((bf16[256,1280]{1,0:T(8,128)(2,1)S(1)}, bf16[256,1280]{1,0:T(8,128)(2,1)S(1)}, u32[]{:S(2)}, u32[]{:S(2)}) %collective-permute-start.3) | collective-permute-done | bytes 655392 | tf_op jit(solution)/shard_map/ppermute | solution.py:90
  25.3 2.8 %collective-permute-start.4 = (bf16[256,1280]{1,0:T(8,128)(2,1)S(1)}, bf16[256,1280]{1,0:T(8,128)(2,1)}, u32[]{:S(2)}, u32[]{:S(2)}) collective-permute-start(bf16[256,1280]{1,0:T(8,128)(2,1)S(1)} %collective-permute-done.3.refs_1_), channel_id=1, source_target_pairs={{0,96},{24,696},{48,144},{72,744},{96,192},{120,24},{144,240},{168... | collective-permute-start | bytes 1966088 | tf_op jit(solution)/shard_map/ppermute | solution.py:90
  28.2 10.5 %collective-permute-done.refs_2_ = bf16[256,1280]{1,0:T(8,128)(2,1)S(1)} collective-permute-done((bf16[256,1280]{1,0:T(8,128)(2,1)S(1)}, bf16[256,1280]{1,0:T(8,128)(2,1)S(1)}, u32[]{:S(2)}, u32[]{:S(2)}) %collective-permute-start) | collective-permute-done | bytes 655392 | tf_op jit(solution)/shard_map/ppermute | solution.py:90
  38.7 3.9 %collective-permute-start.1 = (bf16[256,1280]{1,0:T(8,128)(2,1)S(1)}, bf16[256,1280]{1,0:T(8,128)(2,1)}, u32[]{:S(2)}, u32[]{:S(2)}) collective-permute-start(bf16[256,1280]{1,0:T(8,128)(2,1)S(1)} %collective-permute-done.refs_2_), channel_id=1, source_target_pairs={{0,96},{24,696},{48,144},{72,744},{96,192},{120,24},{144,240},{168... | collective-permute-start | bytes 1966088 | tf_op jit(solution)/shard_map/ppermute | solution.py:90
  42.6 2.3 %collective-permute-done.4.refs_3_ = bf16[256,1280]{1,0:T(8,128)(2,1)} collective-permute-done((bf16[256,1280]{1,0:T(8,128)(2,1)S(1)}, bf16[256,1280]{1,0:T(8,128)(2,1)}, u32[]{:S(2)}, u32[]{:S(2)}) %collective-permute-start.4) | collective-permute-done | bytes 655392 | tf_op jit(solution)/shard_map/ppermute | solution.py:90
  44.9 1.9 %collective-permute-start.6 = (bf16[256,1280]{1,0:T(8,128)(2,1)}, bf16[256,1280]{1,0:T(8,128)(2,1)}, u32[]{:S(2)}, u32[]{:S(2)}) collective-permute-start(bf16[256,1280]{1,0:T(8,128)(2,1)} %collective-permute-done.4.refs_3_), channel_id=1, source_target_pairs={{0,96},{24,696},{48,144},{72,744},{96,192},{120,24},{144,240},{168... | collective-permute-start | bytes 1966088 | tf_op jit(solution)/shard_map/ppermute | solution.py:90
  46.9 2.5 %shard_map.46 = (f32[192,1280]{1,0:T(8,128)S(1)}, f32[192,1280]{1,0:T(8,128)S(1)}, f32[192,1]{1,0:T(8,128)S(1)}) custom-call(bf16[192,4096]{1,0:T(8,128)(2,1)S(1)} %copy-done, bf16[192,4096]{1,0:T(8,128)(2,1)S(1)} %collective-permute-done.2.others, bf16[128,1280]{1,0:T(8,128)(2,1)S(1)} %pad_maximum_fusion.refs_0_, ...), custom_call_target="tpu_custom_call" | custom-call | flops 880803840 | bytes 6225920 | tf_op jit(solution)/shard_map/pallas_call | solution.py:69
  52.2 3.0 %collective-permute-start.5 = (bf16[256,1280]{1,0:T(8,128)(2,1)}, bf16[256,1280]{1,0:T(8,128)(2,1)}, u32[]{:S(2)}, u32[]{:S(2)}) collective-permute-start(bf16[256,1280]{1,0:T(8,128)(2,1)} %collective-permute-done.1.refs_0_), channel_id=1, source_target_pairs={{0,96},{24,696},{48,144},{72,744},{96,192},{120,24},{144,240},{168... | collective-permute-start | bytes 1966088 | tf_op jit(solution)/shard_map/ppermute | solution.py:90
  55.3 4.0 %collective-permute-done.6.refs_1_ = bf16[256,1280]{1,0:T(8,128)(2,1)} collective-permute-done((bf16[256,1280]{1,0:T(8,128)(2,1)}, bf16[256,1280]{1,0:T(8,128)(2,1)}, u32[]{:S(2)}, u32[]{:S(2)}) %collective-permute-start.6) | collective-permute-done | bytes 655392 | tf_op jit(solution)/shard_map/ppermute | solution.py:90
  60.2 3.1 %collective-permute-start.10 = (bf16[128,1280]{1,0:T(8,128)(2,1)S(1)}, bf16[128,1280]{1,0:T(8,128)(2,1)S(1)}, u32[]{:S(2)}, u32[]{:S(2)}) collective-permute-start(bf16[128,1280]{1,0:T(8,128)(2,1)S(1)} %constant_dynamic-slice_fusion), channel_id=1, source_target_pairs={{0,96},{24,696},{48,144},{72,744},{96,192},{120,24},{144,240},{168... | collective-permute-start | bytes 983048 | tf_op jit(solution)/shard_map/ppermute | solution.py:90
  65.7 2.0 %shard_map.47 = (f32[192,1280]{1,0:T(8,128)S(1)}, f32[192,1280]{1,0:T(8,128)S(1)}) custom-call(bf16[192,4096]{1,0:T(8,128)(2,1)S(1)} %copy-done, bf16[192,4096]{1,0:T(8,128)(2,1)S(1)} %collective-permute-done.2.others, f32[192,1280]{1,0:T(8,128)S(1)} %copy-done.2, f32[192,1280]{1,0:T(8,128)S(1)} %copy-done.4, ...), custom_call_target="tpu_custom_call" | custom-call | flops 503316480 | bytes 5242880 | tf_op jit(solution)/shard_map/pallas_call | solution.py:69
  67.7 2.2 %collective-permute-start.8 = (f32[192,1280]{1,0:T(8,128)S(1)}, f32[192,1280]{1,0:T(8,128)S(1)}, u32[]{:S(2)}, u32[]{:S(2)}) collective-permute-start(f32[192,1280]{1,0:T(8,128)S(1)} %get-tuple-element.28), channel_id=1, source_target_pairs={{0,24},{24,0},{48,72},{72,48},{96,120},{120,96},{144,168},{168,144... | collective-permute-start | bytes 2949128 | tf_op jit(solution)/shard_map/ppermute | solution.py:90
  70.0 4.4 %collective-permute-start.9 = (bf16[256,1280]{1,0:T(8,128)(2,1)S(1)}, bf16[256,1280]{1,0:T(8,128)(2,1)S(1)}, u32[]{:S(2)}, u32[]{:S(2)}) collective-permute-start(bf16[256,1280]{1,0:T(8,128)(2,1)S(1)} %copy-done.6), channel_id=1, source_target_pairs={{0,48},{24,72},{48,0},{72,24},{96,144},{120,168},{144,96},{168,120... | collective-permute-start | bytes 1966088 | tf_op jit(solution)/shard_map/ppermute | solution.py:90
  74.4 2.2 %collective-permute-start.11 = (bf16[256,1280]{1,0:T(8,128)(2,1)}, bf16[256,1280]{1,0:T(8,128)(2,1)S(1)}, u32[]{:S(2)}, u32[]{:S(2)}) collective-permute-start(bf16[256,1280]{1,0:T(8,128)(2,1)} %collective-permute-done.5.refs_1_), channel_id=1, source_target_pairs={{0,24},{24,0},{48,72},{72,48},{96,120},{120,96},{144,168},{168,144... | collective-permute-start | bytes 1966088 | tf_op jit(solution)/shard_map/ppermute | solution.py:90
  77.6 4.9 %collective-permute-start.7 = (bf16[128,1280]{1,0:T(8,128)(2,1)S(1)}, bf16[128,1280]{1,0:T(8,128)(2,1)S(1)}, u32[]{:S(2)}, u32[]{:S(2)}) collective-permute-start(bf16[128,1280]{1,0:T(8,128)(2,1)S(1)} %constant_dynamic-slice_fusion.1), channel_id=1, source_target_pairs={{0,96},{24,696},{48,144},{72,744},{96,192},{120,24},{144,240},{168... | collective-permute-start | bytes 983048 | tf_op jit(solution)/shard_map/ppermute | solution.py:90
  82.5 2.3 %all_gather.10.refs_3_ = bf16[256,1280]{1,0:T(8,128)(2,1)S(1)} all-gather(bf16[128,1280]{1,0:T(8,128)(2,1)S(1)} %collective-permute-done.10), channel_id=1, replica_groups={{0,24},{48,72},{96,120},{144,168},{192,216},{240,264},{288,312},{336,36..., dimensions={0}, use_global_device_ids=true | all-gather | bytes 983040 | tf_op jit(solution)/shard_map/all_gather | solution.py:99
  84.8 4.7 %collective-permute-done.9.refs_0_ = bf16[256,1280]{1,0:T(8,128)(2,1)S(1)} collective-permute-done((bf16[256,1280]{1,0:T(8,128)(2,1)S(1)}, bf16[256,1280]{1,0:T(8,128)(2,1)S(1)}, u32[]{:S(2)}, u32[]{:S(2)}) %collective-permute-start.9) | collective-permute-done | bytes 655392 | tf_op jit(solution)/shard_map/ppermute | solution.py:90
  89.5 1.8 %shard_map.48.total_before = f32[192,1280]{1,0:T(8,128)S(1)} custom-call(bf16[192,4096]{1,0:T(8,128)(2,1)S(1)} %copy-done, f32[192,1280]{1,0:T(8,128)S(1)} %get-tuple-element.27.total_before, f32[192,1280]{1,0:T(8,128)S(1)} %collective-permute-done.8.partial_arrived, bf16[256,1280]{1,0:T(8,128)(2,1)S(1)} %collective-permute-done.9.refs_0_, ...), custom_call_target="tpu_custom_call" | custom-call | flops 1006632960 | bytes 6553600 | tf_op jit(solution)/shard_map/pallas_call | solution.py:69
  91.3 2.9 %all_gather.11.refs_0_ = bf16[256,1280]{1,0:T(8,128)(2,1)S(1)} all-gather(bf16[128,1280]{1,0:T(8,128)(2,1)S(1)} %collective-permute-done.7), channel_id=1, replica_groups={{0,24},{48,72},{96,120},{144,168},{192,216},{240,264},{288,312},{336,36..., dimensions={0}, use_global_device_ids=true | all-gather | bytes 983040 | tf_op jit(solution)/shard_map/all_gather | solution.py:99
  (25 shorter events, 8.3 us)
Async XLA Ops:
  0.0 15.6 %copy-start = (bf16[192,4096]{1,0:T(8,128)(2,1)S(1)}, bf16[192,4096]{1,0:T(8,128)(2,1)}, u32[]{:S(2)}) copy-start(bf16[192,4096]{1,0:T(8,128)(2,1)} %tokens.7) | copy-start | bytes 4718596
  13.7 33.1 %copy-start.5 = (bf16[256,1280]{1,0:T(8,128)(2,1)}, bf16[256,1280]{1,0:T(8,128)(2,1)S(1)}, u32[]{:S(2)}) copy-start(bf16[256,1280]{1,0:T(8,128)(2,1)S(1)} %all_gather.9) | copy-start | bytes 1966084
  13.7 11.6 %collective-permute-start.3 = (bf16[256,1280]{1,0:T(8,128)(2,1)S(1)}, bf16[256,1280]{1,0:T(8,128)(2,1)S(1)}, u32[]{:S(2)}, u32[]{:S(2)}) collective-permute-start(bf16[256,1280]{1,0:T(8,128)(2,1)S(1)} %all_gather.9), channel_id=1, source_target_pairs={{0,96},{24,696},{48,144},{72,744},{96,192},{120,24},{144,240},{168... | collective-permute-start | bytes 1966088 | tf_op jit(solution)/shard_map/ppermute | solution.py:90
  15.6 31.2 %collective-permute-start.2 = (bf16[192,4096]{1,0:T(8,128)(2,1)S(1)}, bf16[192,4096]{1,0:T(8,128)(2,1)S(1)}, u32[]{:S(2)}, u32[]{:S(2)}) collective-permute-start(bf16[192,4096]{1,0:T(8,128)(2,1)S(1)} %copy-done), channel_id=1, source_target_pairs={{0,24},{24,0},{48,72},{72,48},{96,120},{120,96},{144,168},{168,144... | collective-permute-start | bytes 4718600 | tf_op jit(solution)/shard_map/ppermute | solution.py:90
  17.9 20.8 %collective-permute-start = (bf16[256,1280]{1,0:T(8,128)(2,1)S(1)}, bf16[256,1280]{1,0:T(8,128)(2,1)S(1)}, u32[]{:S(2)}, u32[]{:S(2)}) collective-permute-start(bf16[256,1280]{1,0:T(8,128)(2,1)S(1)} %all_gather.9), channel_id=1, source_target_pairs={{0,144},{24,744},{48,96},{72,696},{96,240},{120,72},{144,192},{168... | collective-permute-start | bytes 1966088 | tf_op jit(solution)/shard_map/ppermute | solution.py:90
  25.3 19.6 %collective-permute-start.4 = (bf16[256,1280]{1,0:T(8,128)(2,1)S(1)}, bf16[256,1280]{1,0:T(8,128)(2,1)}, u32[]{:S(2)}, u32[]{:S(2)}) collective-permute-start(bf16[256,1280]{1,0:T(8,128)(2,1)S(1)} %collective-permute-done.3.refs_1_), channel_id=1, source_target_pairs={{0,96},{24,696},{48,144},{72,744},{96,192},{120,24},{144,240},{168... | collective-permute-start | bytes 1966088 | tf_op jit(solution)/shard_map/ppermute | solution.py:90
  38.7 13.5 %collective-permute-start.1 = (bf16[256,1280]{1,0:T(8,128)(2,1)S(1)}, bf16[256,1280]{1,0:T(8,128)(2,1)}, u32[]{:S(2)}, u32[]{:S(2)}) collective-permute-start(bf16[256,1280]{1,0:T(8,128)(2,1)S(1)} %collective-permute-done.refs_2_), channel_id=1, source_target_pairs={{0,96},{24,696},{48,144},{72,744},{96,192},{120,24},{144,240},{168... | collective-permute-start | bytes 1966088 | tf_op jit(solution)/shard_map/ppermute | solution.py:90
  44.9 14.3 %collective-permute-start.6 = (bf16[256,1280]{1,0:T(8,128)(2,1)}, bf16[256,1280]{1,0:T(8,128)(2,1)}, u32[]{:S(2)}, u32[]{:S(2)}) collective-permute-start(bf16[256,1280]{1,0:T(8,128)(2,1)} %collective-permute-done.4.refs_3_), channel_id=1, source_target_pairs={{0,96},{24,696},{48,144},{72,744},{96,192},{120,24},{144,240},{168... | collective-permute-start | bytes 1966088 | tf_op jit(solution)/shard_map/ppermute | solution.py:90
  49.4 1.0 %copy-start.1 = (f32[192,1280]{1,0:T(8,128)}, f32[192,1280]{1,0:T(8,128)S(1)}, u32[]{:S(2)}) copy-start(f32[192,1280]{1,0:T(8,128)S(1)} %get-tuple-element.23.total_before) | copy-start | bytes 2949124
  50.4 1.0 %copy-start.3 = (f32[192,1280]{1,0:T(8,128)}, f32[192,1280]{1,0:T(8,128)S(1)}, u32[]{:S(2)}) copy-start(f32[192,1280]{1,0:T(8,128)S(1)} %get-tuple-element.24.partial_before) | copy-start | bytes 2949124
  52.2 22.2 %collective-permute-start.5 = (bf16[256,1280]{1,0:T(8,128)(2,1)}, bf16[256,1280]{1,0:T(8,128)(2,1)}, u32[]{:S(2)}, u32[]{:S(2)}) collective-permute-start(bf16[256,1280]{1,0:T(8,128)(2,1)} %collective-permute-done.1.refs_0_), channel_id=1, source_target_pairs={{0,96},{24,696},{48,144},{72,744},{96,192},{120,24},{144,240},{168... | collective-permute-start | bytes 1966088 | tf_op jit(solution)/shard_map/ppermute | solution.py:90
  60.2 14.2 %collective-permute-start.10 = (bf16[128,1280]{1,0:T(8,128)(2,1)S(1)}, bf16[128,1280]{1,0:T(8,128)(2,1)S(1)}, u32[]{:S(2)}, u32[]{:S(2)}) collective-permute-start(bf16[128,1280]{1,0:T(8,128)(2,1)S(1)} %constant_dynamic-slice_fusion), channel_id=1, source_target_pairs={{0,96},{24,696},{48,144},{72,744},{96,192},{120,24},{144,240},{168... | collective-permute-start | bytes 983048 | tf_op jit(solution)/shard_map/ppermute | solution.py:90
  63.3 1.2 %copy-start.2 = (f32[192,1280]{1,0:T(8,128)S(1)}, f32[192,1280]{1,0:T(8,128)}, u32[]{:S(2)}) copy-start(f32[192,1280]{1,0:T(8,128)} %copy-done.1) | copy-start | bytes 2949124
  64.5 1.2 %copy-start.4 = (f32[192,1280]{1,0:T(8,128)S(1)}, f32[192,1280]{1,0:T(8,128)}, u32[]{:S(2)}) copy-start(f32[192,1280]{1,0:T(8,128)} %copy-done.3) | copy-start | bytes 2949124
  65.7 4.3 %copy-start.6 = (bf16[256,1280]{1,0:T(8,128)(2,1)S(1)}, bf16[256,1280]{1,0:T(8,128)(2,1)}, u32[]{:S(2)}) copy-start(bf16[256,1280]{1,0:T(8,128)(2,1)} %copy-done.5) | copy-start | bytes 1966084
  67.7 21.8 %collective-permute-start.8 = (f32[192,1280]{1,0:T(8,128)S(1)}, f32[192,1280]{1,0:T(8,128)S(1)}, u32[]{:S(2)}, u32[]{:S(2)}) collective-permute-start(f32[192,1280]{1,0:T(8,128)S(1)} %get-tuple-element.28), channel_id=1, source_target_pairs={{0,24},{24,0},{48,72},{72,48},{96,120},{120,96},{144,168},{168,144... | collective-permute-start | bytes 2949128 | tf_op jit(solution)/shard_map/ppermute | solution.py:90
  70.0 19.5 %collective-permute-start.9 = (bf16[256,1280]{1,0:T(8,128)(2,1)S(1)}, bf16[256,1280]{1,0:T(8,128)(2,1)S(1)}, u32[]{:S(2)}, u32[]{:S(2)}) collective-permute-start(bf16[256,1280]{1,0:T(8,128)(2,1)S(1)} %copy-done.6), channel_id=1, source_target_pairs={{0,48},{24,72},{48,0},{72,24},{96,144},{120,168},{144,96},{168,120... | collective-permute-start | bytes 1966088 | tf_op jit(solution)/shard_map/ppermute | solution.py:90
  74.4 15.1 %collective-permute-start.11 = (bf16[256,1280]{1,0:T(8,128)(2,1)}, bf16[256,1280]{1,0:T(8,128)(2,1)S(1)}, u32[]{:S(2)}, u32[]{:S(2)}) collective-permute-start(bf16[256,1280]{1,0:T(8,128)(2,1)} %collective-permute-done.5.refs_1_), channel_id=1, source_target_pairs={{0,24},{24,0},{48,72},{72,48},{96,120},{120,96},{144,168},{168,144... | collective-permute-start | bytes 1966088 | tf_op jit(solution)/shard_map/ppermute | solution.py:90
  77.6 13.7 %collective-permute-start.7 = (bf16[128,1280]{1,0:T(8,128)(2,1)S(1)}, bf16[128,1280]{1,0:T(8,128)(2,1)S(1)}, u32[]{:S(2)}, u32[]{:S(2)}) collective-permute-start(bf16[128,1280]{1,0:T(8,128)(2,1)S(1)} %constant_dynamic-slice_fusion.1), channel_id=1, source_target_pairs={{0,96},{24,696},{48,144},{72,744},{96,192},{120,24},{144,240},{168... | collective-permute-start | bytes 983048 | tf_op jit(solution)/shard_map/ppermute | solution.py:90

commit v4 on v3

--- a/solution.py
+++ b/solution.py
@@ -45,17 +45,23 @@
     add(blocks, [(tokens, total), (others, partial)])
 
 
-def third_kernel(add, n, tokens, total_before, partial_arrived, *refs):
-    blocks, (total,) = refs[:n], refs[n:]
-    total[...] = total_before[...] + partial_arrived[...]
-    add(blocks, [(tokens, total)])
+def third_kernel(add, n, tokens, others, total_before, partial_before, *refs):
+    blocks, (total, gate, up, sums) = refs[:n], refs[n:]
+    total[...] = total_before[...]
+    sums[...] = partial_before[...]
+    add(blocks, [(tokens, total), (others, sums)])
+    wide = gate.shape[1]
+    gate[...] = sums[:, :wide]
+    up[...] = sums[:, wide:]
 
 
-def last_kernel(add, n, tokens, total_before, scale, *refs):
+def last_kernel(add, n, tokens, total_before, gate_arrived, up_arrived, scale, *refs):
     blocks, (hidden, total) = refs[:n], refs[n:]
-    total[...] = total_before[...]
+    rows, wide = hidden.shape
+    theirs = pl.ds(pl.multiple_of((1 - lax.rem(lax.axis_index("fsdp"), 2)) * rows, rows), rows)
+    total[:, :wide] = total_before[:, :wide] + gate_arrived[theirs, :]
+    total[:, wide:] = total_before[:, wide:] + up_arrived[theirs, :]
     add(blocks, [(tokens, total)])
-    wide = hidden.shape[1]
     gate = total[:, :wide] * scale[...]
     up = total[:, wide:] * scale[...]
     hidden[...] = (gate / (1.0 + jnp.exp(-gate)) * up).astype(hidden.dtype)
@@ -109,10 +115,9 @@
         sums = jax.ShapeDtypeStruct((rows, wide), jnp.float32)
         step = functools.partial(call, high=high)
 
-        late0 = tokens
         a1 = along(chip)
         b1 = slant(chip)
-        others = swap(late0)
+        others = swap(tokens)
         a2 = along(a1)
         b2 = along(b1)
         a3 = along(a2)
@@ -123,35 +128,33 @@
             blocks=[own, a1, b1, a2],
             out_shape=(sums, sums, jax.ShapeDtypeStruct((rows, 1), jnp.float32)),
         )
-        b2, total = lax.optimization_barrier((b2, total))
-        b2, chip = lax.optimization_barrier((b2, chip))
-        b0 = across(chip)
+        b2, total, late = lax.optimization_barrier((b2, total, own))
         b3 = along(b2)
         a4 = along(lax.dynamic_slice_in_dim(a3, half, depth, 0))
+        b0 = across(late)
         total, partial = step(
             second_kernel,
-            specs=[(2, 1, 0), (3, 0, 0)],
+            specs=[(0, 1, 1), (2, 1, 0), (3, 0, 0)],
             arrays=[tokens, others, total, partial],
-            blocks=[b2, a3],
+            blocks=[b0, b2, a3],
             out_shape=(sums, sums),
         )
         b3, total = lax.optimization_barrier((b3, total))
-        bs = lax.dynamic_slice_in_dim(b3, half, depth, 0)
-        b4 = along(bs)
-        a4, late = lax.optimization_barrier((a4, b3))
-        partial = swap(partial)
-        total = step(
+        b4 = along(lax.dynamic_slice_in_dim(b3, half, depth, 0))
+        narrow = jax.ShapeDtypeStruct((rows, wide // 2), jnp.float32)
+        total, *partial = step(
             third_kernel,
-            specs=[(0, 1, 0), (3, 1, 0), (-3, 1, 0), (4, 0, 0)],
-            arrays=[tokens, total, partial],
-            blocks=[b0, b3, swap(late), join(a4)],
-            out_shape=sums,
+            specs=[(3, 1, 0), (4, 0, 1)],
+            arrays=[tokens, others, total, partial],
+            blocks=[b3, a4],
+            out_shape=(sums, narrow, narrow),
+            scratch=[pltpu.VMEM((rows, wide), jnp.float32)],
         )
-        b4, total = lax.optimization_barrier((b4, total))
+        partial = [join(v) for v in partial]
         return step(
             last_kernel,
             specs=[(4, 1, 0)],
-            arrays=[tokens, total, scale],
+            arrays=[tokens, total, *partial, scale],
             blocks=[join(b4)],
             out_shape=jax.ShapeDtypeStruct((rows, wide // 2), jnp.bfloat16),
             scratch=[pltpu.VMEM((rows, wide), jnp.float32)],

time: 96 us -> 89.7 us (0.934)
  blocking collectives: 17.6 us -> 12.2 us
  starting transfers between devices: 34.6 us -> 33.2 us
    all_gather x3 -> x4, blocking collectives: 17.6 us -> 12.2 us  [join(): lax.all_gather(v, 'fsdp', axis=0, tiled=True, axis_index_groups=core_pairs)]
    ppermute x12 -> x10, starting transfers between devices: 34.6 us -> 33.2 us  [move(): return lambda v: lax.ppermute(v, 'fsdp', pairs)]
    ppermute x12 -> x10, waiting for transfers between devices: 27.9 us -> 27.6 us  [move(): return lambda v: lax.ppermute(v, 'fsdp', pairs)]
  transfers between devices with their start and end apart: 12 -> 10, of which waited for: 6 -> 5; matrix products, arithmetic and copies ran while one was open for 2% -> 4% of each run, Pallas kernels for 7% -> 7%
where the time goes in v4:
time: 89.7 us; the launch traced here: 89 us
  starting transfers between devices  33.2 us (37%)
  waiting for transfers between devices  27.6 us (31%)
  blocking collectives  12.2 us (14%)
  Pallas kernels  7.7 us (9%)
  local copies, waits for them, and re-layouts  6.99 us (8%)
  other arithmetic  1.16 us (1%)
    ppermute x10, starting transfers between devices, move(): return lambda v: lax.ppermute(v, 'fsdp', pairs)  33.2 us
    ppermute x10, waiting for transfers between devices, move(): return lambda v: lax.ppermute(v, 'fsdp', pairs)  27.6 us
    all_gather x4, blocking collectives, join(): lax.all_gather(v, 'fsdp', axis=0, tiled=True, axis_index_groups=core_pairs)  12.2 us
    pallas_call x4, Pallas kernels, call(): pl.pallas_call(functools.partial(kernel, functools.partial(add_blocks, sp...  7.7 us
    unnamed x14, local copies, waits for them, and re-layouts  4.99 us
  transfers between devices with their start and end apart: 10, of which 5 were waited for; matrix products, arithmetic and copies ran while one was open for 4% of the time, Pallas kernels for 7%

profile of v4, /device:TPU:1, one launch (start us, length us, event | category | flops | bytes accessed | tf_op | source)
XLA Modules:
  0.0 89.0 jit_solution(4480708877470577241)
XLA Ops:
  0.0 12.5 %collective-permute-start = (bf16[192,4096]{1,0:T(8,128)(2,1)}, bf16[192,4096]{1,0:T(8,128)(2,1)S(1)}, u32[]{:S(2)}, u32[]{:S(2)}) collective-permute-start(bf16[192,4096]{1,0:T(8,128)(2,1)} %tokens.7), channel_id=1, source_target_pairs={{0,24},{24,0},{48,72},{72,48},{96,120},{120,96},{144,168},{168,144... | collective-permute-start | bytes 4718600 | tf_op jit(solution)/shard_map/ppermute | solution.py:96
  12.6 1.1 %multiply_convert_fusion.1 = (bf16[128,640]{1,0:T(8,128)(2,1)S(1)}, bf16[128,640]{1,0:T(8,128)(2,1)S(1)}) fusion(bf16[128,640]{1,0:T(8,128)(2,1)} %param.6, f32[128]{0:T(128)} %param.5, bf16[128,640]{1,0:T(8,128)(2,1)} %param.7), kind=kLoop, calls=%fused_computation.2 | loop fusion | flops 491520 | bytes 655872 | tf_op jit(solution)/shard_map/convert
  13.7 2.3 %all_gather.12 = bf16[256,1280]{1,0:T(8,128)(2,1)S(1)} all-gather(bf16[128,1280]{1,0:T(8,128)(2,1)S(1)} %pad_maximum_fusion.refs_0_), channel_id=1, replica_groups={{0,24},{48,72},{96,120},{144,168},{192,216},{240,264},{288,312},{336,36..., dimensions={0}, use_global_device_ids=true | all-gather | bytes 983040 | tf_op jit(solution)/shard_map/all_gather | solution.py:105
  16.0 1.9 %collective-permute-start.3 = (bf16[256,1280]{1,0:T(8,128)(2,1)S(1)}, bf16[256,1280]{1,0:T(8,128)(2,1)S(1)}, u32[]{:S(2)}, u32[]{:S(2)}) collective-permute-start(bf16[256,1280]{1,0:T(8,128)(2,1)S(1)} %all_gather.12), channel_id=1, source_target_pairs={{0,96},{24,696},{48,144},{72,744},{96,192},{120,24},{144,240},{168... | collective-permute-start | bytes 1966088 | tf_op jit(solution)/shard_map/ppermute | solution.py:96
  18.0 1.9 %collective-permute-start.1 = (bf16[256,1280]{1,0:T(8,128)(2,1)S(1)}, bf16[256,1280]{1,0:T(8,128)(2,1)S(1)}, u32[]{:S(2)}, u32[]{:S(2)}) collective-permute-start(bf16[256,1280]{1,0:T(8,128)(2,1)S(1)} %all_gather.12), channel_id=1, source_target_pairs={{0,144},{24,744},{48,96},{72,696},{96,240},{120,72},{144,192},{168... | collective-permute-start | bytes 1966088 | tf_op jit(solution)/shard_map/ppermute | solution.py:96
  19.9 7.8 %collective-permute-done.3.refs_1_ = bf16[256,1280]{1,0:T(8,128)(2,1)S(1)} collective-permute-done((bf16[256,1280]{1,0:T(8,128)(2,1)S(1)}, bf16[256,1280]{1,0:T(8,128)(2,1)S(1)}, u32[]{:S(2)}, u32[]{:S(2)}) %collective-permute-start.3) | collective-permute-done | bytes 655392 | tf_op jit(solution)/shard_map/ppermute | solution.py:96
  27.7 3.1 %collective-permute-start.4 = (bf16[256,1280]{1,0:T(8,128)(2,1)S(1)}, bf16[256,1280]{1,0:T(8,128)(2,1)}, u32[]{:S(2)}, u32[]{:S(2)}) collective-permute-start(bf16[256,1280]{1,0:T(8,128)(2,1)S(1)} %collective-permute-done.3.refs_1_), channel_id=1, source_target_pairs={{0,96},{24,696},{48,144},{72,744},{96,192},{120,24},{144,240},{168... | collective-permute-start | bytes 1966088 | tf_op jit(solution)/shard_map/ppermute | solution.py:96
  30.8 7.9 %collective-permute-done.1.refs_2_ = bf16[256,1280]{1,0:T(8,128)(2,1)S(1)} collective-permute-done((bf16[256,1280]{1,0:T(8,128)(2,1)S(1)}, bf16[256,1280]{1,0:T(8,128)(2,1)S(1)}, u32[]{:S(2)}, u32[]{:S(2)}) %collective-permute-start.1) | collective-permute-done | bytes 655392 | tf_op jit(solution)/shard_map/ppermute | solution.py:96
  38.7 1.9 %collective-permute-start.2 = (bf16[256,1280]{1,0:T(8,128)(2,1)S(1)}, bf16[256,1280]{1,0:T(8,128)(2,1)}, u32[]{:S(2)}, u32[]{:S(2)}) collective-permute-start(bf16[256,1280]{1,0:T(8,128)(2,1)S(1)} %collective-permute-done.1.refs_2_), channel_id=1, source_target_pairs={{0,96},{24,696},{48,144},{72,744},{96,192},{120,24},{144,240},{168... | collective-permute-start | bytes 1966088 | tf_op jit(solution)/shard_map/ppermute | solution.py:96
  40.6 6.9 %collective-permute-done.4.refs_3_ = bf16[256,1280]{1,0:T(8,128)(2,1)} collective-permute-done((bf16[256,1280]{1,0:T(8,128)(2,1)S(1)}, bf16[256,1280]{1,0:T(8,128)(2,1)}, u32[]{:S(2)}, u32[]{:S(2)}) %collective-permute-start.4) | collective-permute-done | bytes 655392 | tf_op jit(solution)/shard_map/ppermute | solution.py:96
  47.5 1.9 %collective-permute-start.7 = (bf16[256,1280]{1,0:T(8,128)(2,1)}, bf16[256,1280]{1,0:T(8,128)(2,1)}, u32[]{:S(2)}, u32[]{:S(2)}) collective-permute-start(bf16[256,1280]{1,0:T(8,128)(2,1)} %collective-permute-done.4.refs_3_), channel_id=1, source_target_pairs={{0,96},{24,696},{48,144},{72,744},{96,192},{120,24},{144,240},{168... | collective-permute-start | bytes 1966088 | tf_op jit(solution)/shard_map/ppermute | solution.py:96
  49.4 2.5 %shard_map.46 = (f32[192,1280]{1,0:T(8,128)S(1)}, f32[192,1280]{1,0:T(8,128)S(1)}, f32[192,1]{1,0:T(8,128)S(1)}) custom-call(bf16[192,4096]{1,0:T(8,128)(2,1)S(1)} %copy-done, bf16[192,4096]{1,0:T(8,128)(2,1)S(1)} %collective-permute-done.others, bf16[128,1280]{1,0:T(8,128)(2,1)S(1)} %pad_maximum_fusion.refs_0_, ...), custom_call_target="tpu_custom_call" | custom-call | flops 880803840 | bytes 6225920 | tf_op jit(solution)/shard_map/pallas_call | solution.py:75
  54.5 1.9 %collective-permute-start.5 = (bf16[256,1280]{1,0:T(8,128)(2,1)}, bf16[256,1280]{1,0:T(8,128)(2,1)}, u32[]{:S(2)}, u32[]{:S(2)}) collective-permute-start(bf16[256,1280]{1,0:T(8,128)(2,1)} %collective-permute-done.2.refs_1_), channel_id=1, source_target_pairs={{0,96},{24,696},{48,144},{72,744},{96,192},{120,24},{144,240},{168... | collective-permute-start | bytes 1966088 | tf_op jit(solution)/shard_map/ppermute | solution.py:96
  56.5 4.1 %collective-permute-start.6 = (bf16[128,1280]{1,0:T(8,128)(2,1)S(1)}, bf16[128,1280]{1,0:T(8,128)(2,1)}, u32[]{:S(2)}, u32[]{:S(2)}) collective-permute-start(bf16[128,1280]{1,0:T(8,128)(2,1)S(1)} %pad_maximum_fusion.refs_0_), channel_id=1, source_target_pairs={{0,48},{24,72},{48,0},{72,24},{96,144},{120,168},{144,96},{168,120... | collective-permute-start | bytes 983048 | tf_op jit(solution)/shard_map/ppermute | solution.py:96
  62.5 1.9 %collective-permute-start.8 = (bf16[128,1280]{1,0:T(8,128)(2,1)S(1)}, bf16[128,1280]{1,0:T(8,128)(2,1)S(1)}, u32[]{:S(2)}, u32[]{:S(2)}) collective-permute-start(bf16[128,1280]{1,0:T(8,128)(2,1)S(1)} %constant_dynamic-slice_fusion.1), channel_id=1, source_target_pairs={{0,96},{24,696},{48,144},{72,744},{96,192},{120,24},{144,240},{168... | collective-permute-start | bytes 983048 | tf_op jit(solution)/shard_map/ppermute | solution.py:96
  64.5 4.1 %collective-permute-done.6.refs_0_ = bf16[128,1280]{1,0:T(8,128)(2,1)} collective-permute-done((bf16[128,1280]{1,0:T(8,128)(2,1)S(1)}, bf16[128,1280]{1,0:T(8,128)(2,1)}, u32[]{:S(2)}, u32[]{:S(2)}) %collective-permute-start.6) | collective-permute-done | bytes 327712 | tf_op jit(solution)/shard_map/ppermute | solution.py:96
  68.5 1.2 %copy-done.2 = f32[192,1280]{1,0:T(8,128)S(1)} copy-done((f32[192,1280]{1,0:T(8,128)S(1)}, f32[192,1280]{1,0:T(8,128)}, u32[]{:S(2)}) %copy-start.2) | copy-done | bytes 983064
  69.7 1.2 %copy-done.4 = f32[192,1280]{1,0:T(8,128)S(1)} copy-done((f32[192,1280]{1,0:T(8,128)S(1)}, f32[192,1280]{1,0:T(8,128)}, u32[]{:S(2)}) %copy-start.4) | copy-done | bytes 983064
  70.9 2.3 %shard_map.47 = (f32[192,1280]{1,0:T(8,128)S(1)}, f32[192,1280]{1,0:T(8,128)S(1)}) custom-call(bf16[192,4096]{1,0:T(8,128)(2,1)S(1)} %copy-done, bf16[192,4096]{1,0:T(8,128)(2,1)S(1)} %collective-permute-done.others, f32[192,1280]{1,0:T(8,128)S(1)} %copy-done.2, f32[192,1280]{1,0:T(8,128)S(1)} %copy-done.4, ...), custom_call_target="tpu_custom_call" | custom-call | flops 629145600 | bytes 5570560 | tf_op jit(solution)/shard_map/pallas_call | solution.py:75
  74.3 1.9 %collective-permute-start.9 = (bf16[128,1280]{1,0:T(8,128)(2,1)S(1)}, bf16[128,1280]{1,0:T(8,128)(2,1)S(1)}, u32[]{:S(2)}, u32[]{:S(2)}) collective-permute-start(bf16[128,1280]{1,0:T(8,128)(2,1)S(1)} %constant_dynamic-slice_fusion), channel_id=1, source_target_pairs={{0,96},{24,696},{48,144},{72,744},{96,192},{120,24},{144,240},{168... | collective-permute-start | bytes 983048 | tf_op jit(solution)/shard_map/ppermute | solution.py:96
  76.2 1.8 %shard_map.48 = (f32[192,1280]{1,0:T(8,128)S(1)}, f32[192,640]{1,0:T(8,128)S(1)}, f32[192,640]{1,0:T(8,128)S(1)}) custom-call(bf16[192,4096]{1,0:T(8,128)(2,1)S(1)} %copy-done, bf16[192,4096]{1,0:T(8,128)(2,1)S(1)} %collective-permute-done.others, f32[192,1280]{1,0:T(8,128)S(1)} %get-tuple-element.24.total_before, ...), custom_call_target="tpu_custom_call" | custom-call | flops 377487360 | bytes 4915200 | tf_op jit(solution)/shard_map/pallas_call | solution.py:75
  78.0 3.7 %all_gather.13.gate_arrived = f32[384,640]{1,0:T(8,128)S(1)} all-gather(f32[192,640]{1,0:T(8,128)S(1)} %get-tuple-element.28), channel_id=1, replica_groups={{0,24},{48,72},{96,120},{144,168},{192,216},{240,264},{288,312},{336,36..., dimensions={0}, use_global_device_ids=true | all-gather | bytes 1474560 | tf_op jit(solution)/shard_map/all_gather | solution.py:105
  81.7 2.6 %all_gather.14.up_arrived = f32[384,640]{1,0:T(8,128)S(1)} all-gather(f32[192,640]{1,0:T(8,128)S(1)} %get-tuple-element.29), channel_id=1, replica_groups={{0,24},{48,72},{96,120},{144,168},{192,216},{240,264},{288,312},{336,36..., dimensions={0}, use_global_device_ids=true | all-gather | bytes 1474560 | tf_op jit(solution)/shard_map/all_gather | solution.py:105
  84.3 3.6 %all_gather.15.refs_0_ = bf16[256,1280]{1,0:T(8,128)(2,1)S(1)} all-gather(bf16[128,1280]{1,0:T(8,128)(2,1)S(1)} %collective-permute-done.9), channel_id=1, replica_groups={{0,24},{48,72},{96,120},{144,168},{192,216},{240,264},{288,312},{336,36..., dimensions={0}, use_global_device_ids=true | all-gather | bytes 983040 | tf_op jit(solution)/shard_map/all_gather | solution.py:105
  (22 shorter events, 6.7 us)
Async XLA Ops:
  0.0 49.4 %copy-start = (bf16[192,4096]{1,0:T(8,128)(2,1)S(1)}, bf16[192,4096]{1,0:T(8,128)(2,1)}, u32[]{:S(2)}) copy-start(bf16[192,4096]{1,0:T(8,128)(2,1)} %tokens.7) | copy-start | bytes 4718596
  0.0 49.4 %collective-permute-start = (bf16[192,4096]{1,0:T(8,128)(2,1)}, bf16[192,4096]{1,0:T(8,128)(2,1)S(1)}, u32[]{:S(2)}, u32[]{:S(2)}) collective-permute-start(bf16[192,4096]{1,0:T(8,128)(2,1)} %tokens.7), channel_id=1, source_target_pairs={{0,24},{24,0},{48,72},{72,48},{96,120},{120,96},{144,168},{168,144... | collective-permute-start | bytes 4718600 | tf_op jit(solution)/shard_map/ppermute | solution.py:96
  16.0 11.6 %collective-permute-start.3 = (bf16[256,1280]{1,0:T(8,128)(2,1)S(1)}, bf16[256,1280]{1,0:T(8,128)(2,1)S(1)}, u32[]{:S(2)}, u32[]{:S(2)}) collective-permute-start(bf16[256,1280]{1,0:T(8,128)(2,1)S(1)} %all_gather.12), channel_id=1, source_target_pairs={{0,96},{24,696},{48,144},{72,744},{96,192},{120,24},{144,240},{168... | collective-permute-start | bytes 1966088 | tf_op jit(solution)/shard_map/ppermute | solution.py:96
  18.0 20.8 %collective-permute-start.1 = (bf16[256,1280]{1,0:T(8,128)(2,1)S(1)}, bf16[256,1280]{1,0:T(8,128)(2,1)S(1)}, u32[]{:S(2)}, u32[]{:S(2)}) collective-permute-start(bf16[256,1280]{1,0:T(8,128)(2,1)S(1)} %all_gather.12), channel_id=1, source_target_pairs={{0,144},{24,744},{48,96},{72,696},{96,240},{120,72},{144,192},{168... | collective-permute-start | bytes 1966088 | tf_op jit(solution)/shard_map/ppermute | solution.py:96
  27.7 19.8 %collective-permute-start.4 = (bf16[256,1280]{1,0:T(8,128)(2,1)S(1)}, bf16[256,1280]{1,0:T(8,128)(2,1)}, u32[]{:S(2)}, u32[]{:S(2)}) collective-permute-start(bf16[256,1280]{1,0:T(8,128)(2,1)S(1)} %collective-permute-done.3.refs_1_), channel_id=1, source_target_pairs={{0,96},{24,696},{48,144},{72,744},{96,192},{120,24},{144,240},{168... | collective-permute-start | bytes 1966088 | tf_op jit(solution)/shard_map/ppermute | solution.py:96
  38.7 15.8 %collective-permute-start.2 = (bf16[256,1280]{1,0:T(8,128)(2,1)S(1)}, bf16[256,1280]{1,0:T(8,128)(2,1)}, u32[]{:S(2)}, u32[]{:S(2)}) collective-permute-start(bf16[256,1280]{1,0:T(8,128)(2,1)S(1)} %collective-permute-done.1.refs_2_), channel_id=1, source_target_pairs={{0,96},{24,696},{48,144},{72,744},{96,192},{120,24},{144,240},{168... | collective-permute-start | bytes 1966088 | tf_op jit(solution)/shard_map/ppermute | solution.py:96
  47.5 14.0 %collective-permute-start.7 = (bf16[256,1280]{1,0:T(8,128)(2,1)}, bf16[256,1280]{1,0:T(8,128)(2,1)}, u32[]{:S(2)}, u32[]{:S(2)}) collective-permute-start(bf16[256,1280]{1,0:T(8,128)(2,1)} %collective-permute-done.4.refs_3_), channel_id=1, source_target_pairs={{0,96},{24,696},{48,144},{72,744},{96,192},{120,24},{144,240},{168... | collective-permute-start | bytes 1966088 | tf_op jit(solution)/shard_map/ppermute | solution.py:96
  51.9 1.0 %copy-start.1 = (f32[192,1280]{1,0:T(8,128)}, f32[192,1280]{1,0:T(8,128)S(1)}, u32[]{:S(2)}) copy-start(f32[192,1280]{1,0:T(8,128)S(1)} %get-tuple-element.20.total_before) | copy-start | bytes 2949124
  52.9 1.0 %copy-start.3 = (f32[192,1280]{1,0:T(8,128)}, f32[192,1280]{1,0:T(8,128)S(1)}, u32[]{:S(2)}) copy-start(f32[192,1280]{1,0:T(8,128)S(1)} %get-tuple-element.21.partial_before) | copy-start | bytes 2949124
  53.9 0.6 copy-start.5
  54.5 18.7 %collective-permute-start.5 = (bf16[256,1280]{1,0:T(8,128)(2,1)}, bf16[256,1280]{1,0:T(8,128)(2,1)}, u32[]{:S(2)}, u32[]{:S(2)}) collective-permute-start(bf16[256,1280]{1,0:T(8,128)(2,1)} %collective-permute-done.2.refs_1_), channel_id=1, source_target_pairs={{0,96},{24,696},{48,144},{72,744},{96,192},{120,24},{144,240},{168... | collective-permute-start | bytes 1966088 | tf_op jit(solution)/shard_map/ppermute | solution.py:96
  56.5 12.1 %collective-permute-start.6 = (bf16[128,1280]{1,0:T(8,128)(2,1)S(1)}, bf16[128,1280]{1,0:T(8,128)(2,1)}, u32[]{:S(2)}, u32[]{:S(2)}) collective-permute-start(bf16[128,1280]{1,0:T(8,128)(2,1)S(1)} %pad_maximum_fusion.refs_0_), channel_id=1, source_target_pairs={{0,48},{24,72},{48,0},{72,24},{96,144},{120,168},{144,96},{168,120... | collective-permute-start | bytes 983048 | tf_op jit(solution)/shard_map/ppermute | solution.py:96
  62.5 13.7 %collective-permute-start.8 = (bf16[128,1280]{1,0:T(8,128)(2,1)S(1)}, bf16[128,1280]{1,0:T(8,128)(2,1)S(1)}, u32[]{:S(2)}, u32[]{:S(2)}) collective-permute-start(bf16[128,1280]{1,0:T(8,128)(2,1)S(1)} %constant_dynamic-slice_fusion.1), channel_id=1, source_target_pairs={{0,96},{24,696},{48,144},{72,744},{96,192},{120,24},{144,240},{168... | collective-permute-start | bytes 983048 | tf_op jit(solution)/shard_map/ppermute | solution.py:96
  68.5 1.2 %copy-start.2 = (f32[192,1280]{1,0:T(8,128)S(1)}, f32[192,1280]{1,0:T(8,128)}, u32[]{:S(2)}) copy-start(f32[192,1280]{1,0:T(8,128)} %copy-done.1) | copy-start | bytes 2949124
  69.7 1.2 %copy-start.4 = (f32[192,1280]{1,0:T(8,128)S(1)}, f32[192,1280]{1,0:T(8,128)}, u32[]{:S(2)}) copy-start(f32[192,1280]{1,0:T(8,128)} %copy-done.3) | copy-start | bytes 2949124
  74.3 10.0 %collective-permute-start.9 = (bf16[128,1280]{1,0:T(8,128)(2,1)S(1)}, bf16[128,1280]{1,0:T(8,128)(2,1)S(1)}, u32[]{:S(2)}, u32[]{:S(2)}) collective-permute-start(bf16[128,1280]{1,0:T(8,128)(2,1)S(1)} %constant_dynamic-slice_fusion), channel_id=1, source_target_pairs={{0,96},{24,696},{48,144},{72,744},{96,192},{120,24},{144,240},{168... | collective-permute-start | bytes 983048 | tf_op jit(solution)/shard_map/ppermute | solution.py:96
  81.7 6.2 %copy-start.6 = (f32[192,1]{1,0:T(8,128)S(1)}, f32[192,1]{1,0:T(8,128)}, u32[]{:S(2)}) copy-start(f32[192,1]{1,0:T(8,128)} %copy-done.5) | copy-start | bytes 2308

commit v5 on v4

--- a/solution.py
+++ b/solution.py
@@ -67,6 +67,27 @@
     hidden[...] = (gate / (1.0 + jnp.exp(-gate)) * up).astype(hidden.dtype)
 
 
+def cut_kernel(depth, block, out, sem):
+    start = pl.multiple_of(lax.rem(lax.axis_index("fsdp"), 2) * depth, depth)
+    copy = pltpu.make_async_copy(block.at[pl.ds(start, depth)], out, sem)
+    copy.start()
+    copy.wait()
+
+
+def cut(block):
+    depth, wide = block.shape[0] // 2, block.shape[1]
+    anywhere = pl.BlockSpec(memory_space=pl.ANY)
+    return pl.pallas_call(
+        functools.partial(cut_kernel, depth),
+        out_shape=jax.ShapeDtypeStruct((depth, wide), block.dtype),
+        in_specs=[anywhere],
+        out_specs=anywhere,
+        scratch_shapes=[pltpu.SemaphoreType.DMA],
+        compiler_params=pltpu.CompilerParams(vmem_limit_bytes=vmem_bytes // 16),
+        cost_estimate=pl.CostEstimate(flops=0, bytes_accessed=4 * depth * wide, transcendentals=0),
+    )(block)
+
+
 def call(kernel, *, high, specs, arrays, blocks, out_shape, scratch=()):
     n = len(blocks)
     depth, wide = sum(b.shape[0] for b in blocks), blocks[0].shape[1]
@@ -96,7 +117,6 @@
         return lambda v: lax.ppermute(v, "fsdp", pairs)
 
     along = move(lambda y, x, c: (y + 1 - 2 * c, x, c))
-    slant = move(lambda y, x, c: (y + 1 - 2 * c, x + 1, c))
     across = move(lambda y, x, c: (y, x + 1, c))
     swap = move(lambda y, x, c: (y, x, c + 1))
     core_pairs = [[f, f + 1] for f in range(0, count, 2)]
@@ -105,19 +125,18 @@
         return lax.all_gather(v, "fsdp", axis=0, tiled=True, axis_index_groups=core_pairs)
 
     def on_device(tokens, norm_gain, gate_weight, up_weight):
-        index = lax.axis_index("fsdp")
         gain = norm_gain[:, None]
         own = jnp.concatenate([gate_weight * gain, up_weight * gain], axis=1).astype(jnp.bfloat16)
-        depth, wide = own.shape
-        half = lax.bitwise_and(index, 1) * depth
-        chip = join(own)
+        wide = own.shape[1]
+        b0 = across(own)
+        chip, late = join(own), tokens
         rows = tokens.shape[0]
         sums = jax.ShapeDtypeStruct((rows, wide), jnp.float32)
         step = functools.partial(call, high=high)
 
         a1 = along(chip)
-        b1 = slant(chip)
-        others = swap(tokens)
+        b1 = along(join(b0))
+        others = swap(late)
         a2 = along(a1)
         b2 = along(b1)
         a3 = along(a2)
@@ -128,10 +147,9 @@
             blocks=[own, a1, b1, a2],
             out_shape=(sums, sums, jax.ShapeDtypeStruct((rows, 1), jnp.float32)),
         )
-        b2, total, late = lax.optimization_barrier((b2, total, own))
+        b2, total = lax.optimization_barrier((b2, total))
         b3 = along(b2)
-        a4 = along(lax.dynamic_slice_in_dim(a3, half, depth, 0))
-        b0 = across(late)
+        a4 = along(cut(a3))
         total, partial = step(
             second_kernel,
             specs=[(0, 1, 1), (2, 1, 0), (3, 0, 0)],
@@ -140,7 +158,7 @@
             out_shape=(sums, sums),
         )
         b3, total = lax.optimization_barrier((b3, total))
-        b4 = along(lax.dynamic_slice_in_dim(b3, half, depth, 0))
+        b4 = along(cut(b3))
         narrow = jax.ShapeDtypeStruct((rows, wide // 2), jnp.float32)
         total, *partial = step(
             third_kernel,

time: 89.7 us -> 82 us (0.914)
  local copies, waits for them, and re-layouts: 6.99 us -> 0.01 us
  waiting for transfers between devices: 27.6 us -> 21 us
  blocking collectives: 12.2 us -> 17 us
  starting transfers between devices: 33.2 us -> 37.8 us
  Pallas kernels: 7.7 us -> 4.34 us
    ppermute x10, waiting for transfers between devices: 27.6 us -> 21 us  [move(): return lambda v: lax.ppermute(v, 'fsdp', pairs)]
    unnamed x14 -> x2, local copies, waits for them, and re-layouts: 4.99 us -> 0.01 us
    all_gather x4 -> x5, blocking collectives: 12.2 us -> 17 us  [join(): lax.all_gather(v, 'fsdp', axis=0, tiled=True, axis_index_groups=core_pairs)]
    ppermute x10, starting transfers between devices: 33.2 us -> 37.8 us  [move(): return lambda v: lax.ppermute(v, 'fsdp', pairs)]
    pallas_call x4, Pallas kernels: 7.7 us -> 4.13 us  [call(): pl.pallas_call(functools.partial(kernel, functools.partial(add_blocks, sp...]
    dynamic_slice x2 -> x0, local copies, waits for them, and re-layouts: 2 us -> none  [the longest x1 1 us: on_device(): b4 = along(lax.dynamic_slice_in_dim(b3, half, depth, 0))]
  transfers between devices with their start and end apart: 10 -> 10, of which waited for: 5 -> 7; matrix products, arithmetic and copies ran while one was open for 4% -> 0% of each run, Pallas kernels for 7% -> 4%
where the time goes in v5:
time: 82 us; the launch traced here: 81.6 us
  starting transfers between devices  37.8 us (46%)
  waiting for transfers between devices  21 us (26%)
  blocking collectives  17 us (21%)
  Pallas kernels  4.34 us (5%)
  other arithmetic  1.28 us (2%)
    ppermute x10, starting transfers between devices, move(): return lambda v: lax.ppermute(v, 'fsdp', pairs)  37.8 us
    ppermute x10, waiting for transfers between devices, move(): return lambda v: lax.ppermute(v, 'fsdp', pairs)  21 us
    all_gather x5, blocking collectives, join(): lax.all_gather(v, 'fsdp', axis=0, tiled=True, axis_index_groups=core_pairs)  17 us
    pallas_call x4, Pallas kernels, call(): pl.pallas_call(functools.partial(kernel, functools.partial(add_blocks, sp...  4.13 us
  transfers between devices with their start and end apart: 10, of which 7 were waited for; matrix products, arithmetic and copies ran while one was open for 0% of the time, Pallas kernels for 4%

profile of v5, /device:TPU:1, one launch (start us, length us, event | category | flops | bytes accessed | tf_op | source)
XLA Modules:
  0.0 81.6 jit_solution(829262905602791949)
XLA Ops:
  0.0 1.3 %multiply_convert_fusion.1 = (bf16[128,640]{1,0:T(8,128)(2,1)S(1)}, bf16[128,640]{1,0:T(8,128)(2,1)S(1)}) fusion(bf16[128,640]{1,0:T(8,128)(2,1)} %param.6, f32[128]{0:T(128)} %param.5, bf16[128,640]{1,0:T(8,128)(2,1)} %param.7), kind=kLoop, calls=%fused_computation.2 | loop fusion | flops 491520 | bytes 655872 | tf_op jit(solution)/shard_map/convert
  1.3 5.5 %collective-permute-start.1 = (bf16[128,1280]{1,0:T(8,128)(2,1)S(1)}, bf16[128,1280]{1,0:T(8,128)(2,1)S(1)}, u32[]{:S(2)}, u32[]{:S(2)}) collective-permute-start(bf16[128,1280]{1,0:T(8,128)(2,1)S(1)} %pad_maximum_fusion.refs_0_), channel_id=1, source_target_pairs={{0,48},{24,72},{48,0},{72,24},{96,144},{120,168},{144,96},{168,120... | collective-permute-start | bytes 983048 | tf_op jit(solution)/shard_map/ppermute | solution.py:117
  6.8 8.9 %collective-permute-start = (bf16[192,4096]{1,0:T(8,128)(2,1)}, bf16[192,4096]{1,0:T(8,128)(2,1)S(1)}, u32[]{:S(2)}, u32[]{:S(2)}) collective-permute-start(bf16[192,4096]{1,0:T(8,128)(2,1)} %tokens.7), channel_id=1, source_target_pairs={{0,24},{24,0},{48,72},{72,48},{96,120},{120,96},{144,168},{168,144... | collective-permute-start | bytes 4718600 | tf_op jit(solution)/shard_map/ppermute | solution.py:117
  15.7 3.5 %all_gather.16 = bf16[256,1280]{1,0:T(8,128)(2,1)S(1)} all-gather(bf16[128,1280]{1,0:T(8,128)(2,1)S(1)} %pad_maximum_fusion.refs_0_), channel_id=1, replica_groups={{0,24},{48,72},{96,120},{144,168},{192,216},{240,264},{288,312},{336,36..., dimensions={0}, use_global_device_ids=true | all-gather | bytes 983040 | tf_op jit(solution)/shard_map/all_gather | solution.py:125
  19.1 1.9 %collective-permute-start.4 = (bf16[256,1280]{1,0:T(8,128)(2,1)S(1)}, bf16[256,1280]{1,0:T(8,128)(2,1)S(1)}, u32[]{:S(2)}, u32[]{:S(2)}) collective-permute-start(bf16[256,1280]{1,0:T(8,128)(2,1)S(1)} %all_gather.16), channel_id=1, source_target_pairs={{0,96},{24,696},{48,144},{72,744},{96,192},{120,24},{144,240},{168... | collective-permute-start | bytes 1966088 | tf_op jit(solution)/shard_map/ppermute | solution.py:117
  21.1 3.1 %all_gather.15 = bf16[256,1280]{1,0:T(8,128)(2,1)S(1)} all-gather(bf16[128,1280]{1,0:T(8,128)(2,1)S(1)} %collective-permute-done.1.refs_0_), channel_id=1, replica_groups={{0,24},{48,72},{96,120},{144,168},{192,216},{240,264},{288,312},{336,36..., dimensions={0}, use_global_device_ids=true | all-gather | bytes 983040 | tf_op jit(solution)/shard_map/all_gather | solution.py:125
  24.2 4.0 %collective-permute-start.2 = (bf16[256,1280]{1,0:T(8,128)(2,1)S(1)}, bf16[256,1280]{1,0:T(8,128)(2,1)S(1)}, u32[]{:S(2)}, u32[]{:S(2)}) collective-permute-start(bf16[256,1280]{1,0:T(8,128)(2,1)S(1)} %all_gather.15), channel_id=1, source_target_pairs={{0,96},{24,696},{48,144},{72,744},{96,192},{120,24},{144,240},{168... | collective-permute-start | bytes 1966088 | tf_op jit(solution)/shard_map/ppermute | solution.py:117
  28.2 2.6 %collective-permute-done.4.refs_1_ = bf16[256,1280]{1,0:T(8,128)(2,1)S(1)} collective-permute-done((bf16[256,1280]{1,0:T(8,128)(2,1)S(1)}, bf16[256,1280]{1,0:T(8,128)(2,1)S(1)}, u32[]{:S(2)}, u32[]{:S(2)}) %collective-permute-start.4) | collective-permute-done | bytes 655392 | tf_op jit(solution)/shard_map/ppermute | solution.py:117
  30.8 2.8 %collective-permute-start.5 = (bf16[256,1280]{1,0:T(8,128)(2,1)S(1)}, bf16[256,1280]{1,0:T(8,128)(2,1)S(1)}, u32[]{:S(2)}, u32[]{:S(2)}) collective-permute-start(bf16[256,1280]{1,0:T(8,128)(2,1)S(1)} %collective-permute-done.4.refs_1_), channel_id=1, source_target_pairs={{0,96},{24,696},{48,144},{72,744},{96,192},{120,24},{144,240},{168... | collective-permute-start | bytes 1966088 | tf_op jit(solution)/shard_map/ppermute | solution.py:117
  33.6 4.2 %collective-permute-done.2.refs_2_ = bf16[256,1280]{1,0:T(8,128)(2,1)S(1)} collective-permute-done((bf16[256,1280]{1,0:T(8,128)(2,1)S(1)}, bf16[256,1280]{1,0:T(8,128)(2,1)S(1)}, u32[]{:S(2)}, u32[]{:S(2)}) %collective-permute-start.2) | collective-permute-done | bytes 655392 | tf_op jit(solution)/shard_map/ppermute | solution.py:117
  37.8 2.9 %collective-permute-start.3 = (bf16[256,1280]{1,0:T(8,128)(2,1)S(1)}, bf16[256,1280]{1,0:T(8,128)(2,1)S(1)}, u32[]{:S(2)}, u32[]{:S(2)}) collective-permute-start(bf16[256,1280]{1,0:T(8,128)(2,1)S(1)} %collective-permute-done.2.refs_2_), channel_id=1, source_target_pairs={{0,96},{24,696},{48,144},{72,744},{96,192},{120,24},{144,240},{168... | collective-permute-start | bytes 1966088 | tf_op jit(solution)/shard_map/ppermute | solution.py:117
  40.7 4.1 %collective-permute-done.5.refs_3_ = bf16[256,1280]{1,0:T(8,128)(2,1)S(1)} collective-permute-done((bf16[256,1280]{1,0:T(8,128)(2,1)S(1)}, bf16[256,1280]{1,0:T(8,128)(2,1)S(1)}, u32[]{:S(2)}, u32[]{:S(2)}) %collective-permute-start.5) | collective-permute-done | bytes 655392 | tf_op jit(solution)/shard_map/ppermute | solution.py:117
  44.8 2.9 %collective-permute-start.7 = (bf16[256,1280]{1,0:T(8,128)(2,1)S(1)}, bf16[256,1280]{1,0:T(8,128)(2,1)S(1)}, u32[]{:S(2)}, u32[]{:S(2)}) collective-permute-start(bf16[256,1280]{1,0:T(8,128)(2,1)S(1)} %collective-permute-done.5.refs_3_), channel_id=1, source_target_pairs={{0,96},{24,696},{48,144},{72,744},{96,192},{120,24},{144,240},{168... | collective-permute-start | bytes 1966088 | tf_op jit(solution)/shard_map/ppermute | solution.py:117
  47.8 1.4 %shard_map.46 = (f32[192,1280]{1,0:T(8,128)S(1)}, f32[192,1280]{1,0:T(8,128)S(1)}, f32[192,1]{1,0:T(8,128)S(1)}) custom-call(bf16[192,4096]{1,0:T(8,128)(2,1)S(1)} %copy-done, bf16[192,4096]{1,0:T(8,128)(2,1)S(1)} %collective-permute-done.others, bf16[128,1280]{1,0:T(8,128)(2,1)S(1)} %pad_maximum_fusion.refs_0_, ...), custom_call_target="tpu_custom_call" | custom-call | flops 880803840 | bytes 6225920 | tf_op jit(solution)/shard_map/pallas_call | solution.py:96
  49.2 2.7 %collective-permute-done.3.refs_1_ = bf16[256,1280]{1,0:T(8,128)(2,1)S(1)} collective-permute-done((bf16[256,1280]{1,0:T(8,128)(2,1)S(1)}, bf16[256,1280]{1,0:T(8,128)(2,1)S(1)}, u32[]{:S(2)}, u32[]{:S(2)}) %collective-permute-start.3) | collective-permute-done | bytes 655392 | tf_op jit(solution)/shard_map/ppermute | solution.py:117
  51.8 2.9 %collective-permute-start.6 = (bf16[256,1280]{1,0:T(8,128)(2,1)S(1)}, bf16[256,1280]{1,0:T(8,128)(2,1)S(1)}, u32[]{:S(2)}, u32[]{:S(2)}) collective-permute-start(bf16[256,1280]{1,0:T(8,128)(2,1)S(1)} %collective-permute-done.3.refs_1_), channel_id=1, source_target_pairs={{0,96},{24,696},{48,144},{72,744},{96,192},{120,24},{144,240},{168... | collective-permute-start | bytes 1966088 | tf_op jit(solution)/shard_map/ppermute | solution.py:117
  54.8 4.1 %collective-permute-done.7.refs_2_.block = bf16[256,1280]{1,0:T(8,128)(2,1)S(1)} collective-permute-done((bf16[256,1280]{1,0:T(8,128)(2,1)S(1)}, bf16[256,1280]{1,0:T(8,128)(2,1)S(1)}, u32[]{:S(2)}, u32[]{:S(2)}) %collective-permute-start.7) | collective-permute-done | bytes 655392 | tf_op jit(solution)/shard_map/ppermute | solution.py:117
  59.0 3.0 %collective-permute-start.8 = (bf16[128,1280]{1,0:T(8,128)(2,1)S(1)}, bf16[128,1280]{1,0:T(8,128)(2,1)S(1)}, u32[]{:S(2)}, u32[]{:S(2)}) collective-permute-start(bf16[128,1280]{1,0:T(8,128)(2,1)S(1)} %shard_map.48), channel_id=1, source_target_pairs={{0,96},{24,696},{48,144},{72,744},{96,192},{120,24},{144,240},{168... | collective-permute-start | bytes 983048 | tf_op jit(solution)/shard_map/ppermute | solution.py:117
  62.8 3.0 %collective-permute-done.6.refs_0_.block = bf16[256,1280]{1,0:T(8,128)(2,1)S(1)} collective-permute-done((bf16[256,1280]{1,0:T(8,128)(2,1)S(1)}, bf16[256,1280]{1,0:T(8,128)(2,1)S(1)}, u32[]{:S(2)}, u32[]{:S(2)}) %collective-permute-start.6) | collective-permute-done | bytes 655392 | tf_op jit(solution)/shard_map/ppermute | solution.py:117
  66.0 3.0 %collective-permute-start.9 = (bf16[128,1280]{1,0:T(8,128)(2,1)S(1)}, bf16[128,1280]{1,0:T(8,128)(2,1)S(1)}, u32[]{:S(2)}, u32[]{:S(2)}) collective-permute-start(bf16[128,1280]{1,0:T(8,128)(2,1)S(1)} %shard_map.50), channel_id=1, source_target_pairs={{0,96},{24,696},{48,144},{72,744},{96,192},{120,24},{144,240},{168... | collective-permute-start | bytes 983048 | tf_op jit(solution)/shard_map/ppermute | solution.py:117
  70.1 4.6 %all_gather.17.gate_arrived = f32[384,640]{1,0:T(8,128)S(1)} all-gather(f32[192,640]{1,0:T(8,128)S(1)} %get-tuple-element.26), channel_id=1, replica_groups={{0,24},{48,72},{96,120},{144,168},{192,216},{240,264},{288,312},{336,36..., dimensions={0}, use_global_device_ids=true | all-gather | bytes 1474560 | tf_op jit(solution)/shard_map/all_gather | solution.py:125
  74.6 2.5 %all_gather.18.up_arrived = f32[384,640]{1,0:T(8,128)S(1)} all-gather(f32[192,640]{1,0:T(8,128)S(1)} %get-tuple-element.27), channel_id=1, replica_groups={{0,24},{48,72},{96,120},{144,168},{192,216},{240,264},{288,312},{336,36..., dimensions={0}, use_global_device_ids=true | all-gather | bytes 1474560 | tf_op jit(solution)/shard_map/all_gather | solution.py:125
  77.1 3.3 %all_gather.19.refs_0_ = bf16[256,1280]{1,0:T(8,128)(2,1)S(1)} all-gather(bf16[128,1280]{1,0:T(8,128)(2,1)S(1)} %collective-permute-done.9), channel_id=1, replica_groups={{0,24},{48,72},{96,120},{144,168},{192,216},{240,264},{288,312},{336,36..., dimensions={0}, use_global_device_ids=true | all-gather | bytes 983040 | tf_op jit(solution)/shard_map/all_gather | solution.py:125
  80.5 1.1 %shard_map.51 = bf16[192,640]{1,0:T(8,128)(2,1)} custom-call(bf16[192,4096]{1,0:T(8,128)(2,1)S(1)} %copy-done, f32[192,1280]{1,0:T(8,128)S(1)} %get-tuple-element.25.total_before, f32[384,640]{1,0:T(8,128)S(1)} %all_gather.17.gate_arrived, f32[384,640]{1,0:T(8,128)S(1)} %all_gather.18.up_arrived, f32[192,1]{1,0:T(8,128)S(1)} %get-tuple-element.28.scale, ...), custom_call_target="tpu_custom_call" | custom-call | flops 251658240 | bytes 4587520 | tf_op jit(solution)/shard_map/pallas_call | solution.py:96
  (11 shorter events, 2.3 us)
Async XLA Ops:
  0.0 47.8 %copy-start = (bf16[192,4096]{1,0:T(8,128)(2,1)S(1)}, bf16[192,4096]{1,0:T(8,128)(2,1)}, u32[]{:S(2)}) copy-start(bf16[192,4096]{1,0:T(8,128)(2,1)} %tokens.7) | copy-start | bytes 4718596
  1.3 19.8 %collective-permute-start.1 = (bf16[128,1280]{1,0:T(8,128)(2,1)S(1)}, bf16[128,1280]{1,0:T(8,128)(2,1)S(1)}, u32[]{:S(2)}, u32[]{:S(2)}) collective-permute-start(bf16[128,1280]{1,0:T(8,128)(2,1)S(1)} %pad_maximum_fusion.refs_0_), channel_id=1, source_target_pairs={{0,48},{24,72},{48,0},{72,24},{96,144},{120,168},{144,96},{168,120... | collective-permute-start | bytes 983048 | tf_op jit(solution)/shard_map/ppermute | solution.py:117
  6.8 41.0 %collective-permute-start = (bf16[192,4096]{1,0:T(8,128)(2,1)}, bf16[192,4096]{1,0:T(8,128)(2,1)S(1)}, u32[]{:S(2)}, u32[]{:S(2)}) collective-permute-start(bf16[192,4096]{1,0:T(8,128)(2,1)} %tokens.7), channel_id=1, source_target_pairs={{0,24},{24,0},{48,72},{72,48},{96,120},{120,96},{144,168},{168,144... | collective-permute-start | bytes 4718600 | tf_op jit(solution)/shard_map/ppermute | solution.py:117
  19.1 11.6 %collective-permute-start.4 = (bf16[256,1280]{1,0:T(8,128)(2,1)S(1)}, bf16[256,1280]{1,0:T(8,128)(2,1)S(1)}, u32[]{:S(2)}, u32[]{:S(2)}) collective-permute-start(bf16[256,1280]{1,0:T(8,128)(2,1)S(1)} %all_gather.16), channel_id=1, source_target_pairs={{0,96},{24,696},{48,144},{72,744},{96,192},{120,24},{144,240},{168... | collective-permute-start | bytes 1966088 | tf_op jit(solution)/shard_map/ppermute | solution.py:117
  24.2 13.6 %collective-permute-start.2 = (bf16[256,1280]{1,0:T(8,128)(2,1)S(1)}, bf16[256,1280]{1,0:T(8,128)(2,1)S(1)}, u32[]{:S(2)}, u32[]{:S(2)}) collective-permute-start(bf16[256,1280]{1,0:T(8,128)(2,1)S(1)} %all_gather.15), channel_id=1, source_target_pairs={{0,96},{24,696},{48,144},{72,744},{96,192},{120,24},{144,240},{168... | collective-permute-start | bytes 1966088 | tf_op jit(solution)/shard_map/ppermute | solution.py:117
  30.8 14.0 %collective-permute-start.5 = (bf16[256,1280]{1,0:T(8,128)(2,1)S(1)}, bf16[256,1280]{1,0:T(8,128)(2,1)S(1)}, u32[]{:S(2)}, u32[]{:S(2)}) collective-permute-start(bf16[256,1280]{1,0:T(8,128)(2,1)S(1)} %collective-permute-done.4.refs_1_), channel_id=1, source_target_pairs={{0,96},{24,696},{48,144},{72,744},{96,192},{120,24},{144,240},{168... | collective-permute-start | bytes 1966088 | tf_op jit(solution)/shard_map/ppermute | solution.py:117
  37.8 14.0 %collective-permute-start.3 = (bf16[256,1280]{1,0:T(8,128)(2,1)S(1)}, bf16[256,1280]{1,0:T(8,128)(2,1)S(1)}, u32[]{:S(2)}, u32[]{:S(2)}) collective-permute-start(bf16[256,1280]{1,0:T(8,128)(2,1)S(1)} %collective-permute-done.2.refs_2_), channel_id=1, source_target_pairs={{0,96},{24,696},{48,144},{72,744},{96,192},{120,24},{144,240},{168... | collective-permute-start | bytes 1966088 | tf_op jit(solution)/shard_map/ppermute | solution.py:117
  44.8 14.0 %collective-permute-start.7 = (bf16[256,1280]{1,0:T(8,128)(2,1)S(1)}, bf16[256,1280]{1,0:T(8,128)(2,1)S(1)}, u32[]{:S(2)}, u32[]{:S(2)}) collective-permute-start(bf16[256,1280]{1,0:T(8,128)(2,1)S(1)} %collective-permute-done.5.refs_3_), channel_id=1, source_target_pairs={{0,96},{24,696},{48,144},{72,744},{96,192},{120,24},{144,240},{168... | collective-permute-start | bytes 1966088 | tf_op jit(solution)/shard_map/ppermute | solution.py:117
  51.8 14.0 %collective-permute-start.6 = (bf16[256,1280]{1,0:T(8,128)(2,1)S(1)}, bf16[256,1280]{1,0:T(8,128)(2,1)S(1)}, u32[]{:S(2)}, u32[]{:S(2)}) collective-permute-start(bf16[256,1280]{1,0:T(8,128)(2,1)S(1)} %collective-permute-done.3.refs_1_), channel_id=1, source_target_pairs={{0,96},{24,696},{48,144},{72,744},{96,192},{120,24},{144,240},{168... | collective-permute-start | bytes 1966088 | tf_op jit(solution)/shard_map/ppermute | solution.py:117
  59.0 10.4 %collective-permute-start.8 = (bf16[128,1280]{1,0:T(8,128)(2,1)S(1)}, bf16[128,1280]{1,0:T(8,128)(2,1)S(1)}, u32[]{:S(2)}, u32[]{:S(2)}) collective-permute-start(bf16[128,1280]{1,0:T(8,128)(2,1)S(1)} %shard_map.48), channel_id=1, source_target_pairs={{0,96},{24,696},{48,144},{72,744},{96,192},{120,24},{144,240},{168... | collective-permute-start | bytes 983048 | tf_op jit(solution)/shard_map/ppermute | solution.py:117
  66.0 11.2 %collective-permute-start.9 = (bf16[128,1280]{1,0:T(8,128)(2,1)S(1)}, bf16[128,1280]{1,0:T(8,128)(2,1)S(1)}, u32[]{:S(2)}, u32[]{:S(2)}) collective-permute-start(bf16[128,1280]{1,0:T(8,128)(2,1)S(1)} %shard_map.50), channel_id=1, source_target_pairs={{0,96},{24,696},{48,144},{72,744},{96,192},{120,24},{144,240},{168... | collective-permute-start | bytes 983048 | tf_op jit(solution)/shard_map/ppermute | solution.py:117

commit v6 on v5

--- a/solution.py
+++ b/solution.py
@@ -17,7 +17,7 @@
     core = lax.rem(index, 2)
     x = lax.rem(lax.div(index, 2), 2)
     y = lax.rem(lax.div(index, 4) + (steps * (2 * core - 1) + high), high)
-    return (y * 2 + (1 - x if other else x)) * 2 + (core if half else 0)
+    return (y * 2 + (1 - x if other else x)) * 2 + (0, core, 1 - core)[half]
 
 
 def add_blocks(specs, high, blocks, pairs):
@@ -67,18 +67,18 @@
     hidden[...] = (gate / (1.0 + jnp.exp(-gate)) * up).astype(hidden.dtype)
 
 
-def cut_kernel(depth, block, out, sem):
-    start = pl.multiple_of(lax.rem(lax.axis_index("fsdp"), 2) * depth, depth)
+def cut_kernel(flip, depth, block, out, sem):
+    start = pl.multiple_of(lax.rem(lax.axis_index("fsdp") + flip, 2) * depth, depth)
     copy = pltpu.make_async_copy(block.at[pl.ds(start, depth)], out, sem)
     copy.start()
     copy.wait()
 
 
-def cut(block):
+def cut(block, flip=0):
     depth, wide = block.shape[0] // 2, block.shape[1]
     anywhere = pl.BlockSpec(memory_space=pl.ANY)
     return pl.pallas_call(
-        functools.partial(cut_kernel, depth),
+        functools.partial(cut_kernel, flip, depth),
         out_shape=jax.ShapeDtypeStruct((depth, wide), block.dtype),
         in_specs=[anywhere],
         out_specs=anywhere,
@@ -129,13 +129,14 @@
         own = jnp.concatenate([gate_weight * gain, up_weight * gain], axis=1).astype(jnp.bfloat16)
         wide = own.shape[1]
         b0 = across(own)
-        chip, late = join(own), tokens
+        chip = join(own)
         rows = tokens.shape[0]
         sums = jax.ShapeDtypeStruct((rows, wide), jnp.float32)
         step = functools.partial(call, high=high)
 
         a1 = along(chip)
-        b1 = along(join(b0))
+        beside, late = lax.optimization_barrier((join(b0), tokens))
+        b1 = along(beside)
         others = swap(late)
         a2 = along(a1)
         b2 = along(b1)
@@ -148,7 +149,8 @@
             out_shape=(sums, sums, jax.ShapeDtypeStruct((rows, 1), jnp.float32)),
         )
         b2, total = lax.optimization_barrier((b2, total))
-        b3 = along(b2)
+        b3 = along(cut(b2))
+        b3_rest = along(cut(b2, 1))
         a4 = along(cut(a3))
         total, partial = step(
             second_kernel,
@@ -158,13 +160,13 @@
             out_shape=(sums, sums),
         )
         b3, total = lax.optimization_barrier((b3, total))
-        b4 = along(cut(b3))
+        b4 = along(b3)
         narrow = jax.ShapeDtypeStruct((rows, wide // 2), jnp.float32)
         total, *partial = step(
             third_kernel,
-            specs=[(3, 1, 0), (4, 0, 1)],
+            specs=[(3, 1, 1), (3, 1, 2), (4, 0, 1)],
             arrays=[tokens, others, total, partial],
-            blocks=[b3, a4],
+            blocks=[b3, b3_rest, a4],
             out_shape=(sums, narrow, narrow),
             scratch=[pltpu.VMEM((rows, wide), jnp.float32)],
         )

time: 82 us -> 81.3 us (level)
  starting transfers between devices: 37.8 us -> 29.2 us
  blocking collectives: 17 us -> 24.6 us
    ppermute x10 -> x11, starting transfers between devices: 37.8 us -> 29.2 us  [move(): return lambda v: lax.ppermute(v, 'fsdp', pairs)]
    all_gather x5, blocking collectives: 17 us -> 24.6 us  [join(): lax.all_gather(v, 'fsdp', axis=0, tiled=True, axis_index_groups=core_pairs)]
    ppermute x10 -> x11, waiting for transfers between devices: 21 us -> 20.9 us  [move(): return lambda v: lax.ppermute(v, 'fsdp', pairs)]
  transfers between devices with their start and end apart: 10 -> 11, of which waited for: 7 -> 6; matrix products, arithmetic and copies ran while one was open for 0% -> 0% of each run, Pallas kernels for 4% -> 4%
where the time goes in v6:
time: 81.3 us; the launch traced here: 80.8 us
  starting transfers between devices  29.2 us (36%)
  blocking collectives  24.6 us (30%)
  waiting for transfers between devices  20.9 us (26%)
  Pallas kernels  4.69 us (6%)
  other arithmetic  1.28 us (2%)
    ppermute x11, starting transfers between devices, move(): return lambda v: lax.ppermute(v, 'fsdp', pairs)  29.2 us
    all_gather x5, blocking collectives, join(): lax.all_gather(v, 'fsdp', axis=0, tiled=True, axis_index_groups=core_pairs)  24.6 us
    ppermute x11, waiting for transfers between devices, move(): return lambda v: lax.ppermute(v, 'fsdp', pairs)  20.9 us
    pallas_call x4, Pallas kernels, call(): pl.pallas_call(functools.partial(kernel, functools.partial(add_blocks, sp...  4.35 us
  transfers between devices with their start and end apart: 11, of which 6 were waited for; matrix products, arithmetic and copies ran while one was open for 0% of the time, Pallas kernels for 4%

profile of v6, /device:TPU:1, one launch (start us, length us, event | category | flops | bytes accessed | tf_op | source)
XLA Modules:
  0.0 80.8 jit_solution(8183021883356772362)
XLA Ops:
  0.0 1.3 %multiply_convert_fusion.1 = (bf16[128,640]{1,0:T(8,128)(2,1)S(1)}, bf16[128,640]{1,0:T(8,128)(2,1)S(1)}) fusion(bf16[128,640]{1,0:T(8,128)(2,1)} %param.6, f32[128]{0:T(128)} %param.5, bf16[128,640]{1,0:T(8,128)(2,1)} %param.7), kind=kLoop, calls=%fused_computation.2 | loop fusion | flops 491520 | bytes 655872 | tf_op jit(solution)/shard_map/convert
  1.3 5.5 %collective-permute-start = (bf16[128,1280]{1,0:T(8,128)(2,1)S(1)}, bf16[128,1280]{1,0:T(8,128)(2,1)S(1)}, u32[]{:S(2)}, u32[]{:S(2)}) collective-permute-start(bf16[128,1280]{1,0:T(8,128)(2,1)S(1)} %pad_maximum_fusion.refs_0_), channel_id=1, source_target_pairs={{0,48},{24,72},{48,0},{72,24},{96,144},{120,168},{144,96},{168,120... | collective-permute-start | bytes 983048 | tf_op jit(solution)/shard_map/ppermute | solution.py:117
  6.8 8.9 %all_gather.16 = bf16[256,1280]{1,0:T(8,128)(2,1)S(1)} all-gather(bf16[128,1280]{1,0:T(8,128)(2,1)S(1)} %pad_maximum_fusion.refs_0_), channel_id=1, replica_groups={{0,24},{48,72},{96,120},{144,168},{192,216},{240,264},{288,312},{336,36..., dimensions={0}, use_global_device_ids=true | all-gather | bytes 983040 | tf_op jit(solution)/shard_map/all_gather | solution.py:125
  15.6 1.9 %collective-permute-start.4 = (bf16[256,1280]{1,0:T(8,128)(2,1)S(1)}, bf16[256,1280]{1,0:T(8,128)(2,1)S(1)}, u32[]{:S(2)}, u32[]{:S(2)}) collective-permute-start(bf16[256,1280]{1,0:T(8,128)(2,1)S(1)} %all_gather.16), channel_id=1, source_target_pairs={{0,96},{24,696},{48,144},{72,744},{96,192},{120,24},{144,240},{168... | collective-permute-start | bytes 1966088 | tf_op jit(solution)/shard_map/ppermute | solution.py:117
  17.6 6.6 %all_gather.15 = bf16[256,1280]{1,0:T(8,128)(2,1)S(1)} all-gather(bf16[128,1280]{1,0:T(8,128)(2,1)S(1)} %collective-permute-done.refs_0_), channel_id=1, replica_groups={{0,24},{48,72},{96,120},{144,168},{192,216},{240,264},{288,312},{336,36..., dimensions={0}, use_global_device_ids=true | all-gather | bytes 983040 | tf_op jit(solution)/shard_map/all_gather | solution.py:125
  24.2 2.3 %collective-permute-start.1 = (bf16[192,4096]{1,0:T(8,128)(2,1)S(1)}, bf16[192,4096]{1,0:T(8,128)(2,1)S(1)}, u32[]{:S(2)}, u32[]{:S(2)}) collective-permute-start(bf16[192,4096]{1,0:T(8,128)(2,1)S(1)} %copy-done), channel_id=1, source_target_pairs={{0,24},{24,0},{48,72},{72,48},{96,120},{120,96},{144,168},{168,144... | collective-permute-start | bytes 4718600 | tf_op jit(solution)/shard_map/ppermute | solution.py:117
  26.5 1.9 %collective-permute-start.2 = (bf16[256,1280]{1,0:T(8,128)(2,1)S(1)}, bf16[256,1280]{1,0:T(8,128)(2,1)S(1)}, u32[]{:S(2)}, u32[]{:S(2)}) collective-permute-start(bf16[256,1280]{1,0:T(8,128)(2,1)S(1)} %all_gather.15), channel_id=1, source_target_pairs={{0,96},{24,696},{48,144},{72,744},{96,192},{120,24},{144,240},{168... | collective-permute-start | bytes 1966088 | tf_op jit(solution)/shard_map/ppermute | solution.py:117
  28.4 1.9 %collective-permute-start.5 = (bf16[256,1280]{1,0:T(8,128)(2,1)S(1)}, bf16[256,1280]{1,0:T(8,128)(2,1)S(1)}, u32[]{:S(2)}, u32[]{:S(2)}) collective-permute-start(bf16[256,1280]{1,0:T(8,128)(2,1)S(1)} %collective-permute-done.4.refs_1_), channel_id=1, source_target_pairs={{0,96},{24,696},{48,144},{72,744},{96,192},{120,24},{144,240},{168... | collective-permute-start | bytes 1966088 | tf_op jit(solution)/shard_map/ppermute | solution.py:117
  30.3 7.8 %collective-permute-done.2.refs_2_ = bf16[256,1280]{1,0:T(8,128)(2,1)S(1)} collective-permute-done((bf16[256,1280]{1,0:T(8,128)(2,1)S(1)}, bf16[256,1280]{1,0:T(8,128)(2,1)S(1)}, u32[]{:S(2)}, u32[]{:S(2)}) %collective-permute-start.2) | collective-permute-done | bytes 655392 | tf_op jit(solution)/shard_map/ppermute | solution.py:117
  38.1 2.8 %collective-permute-start.3 = (bf16[256,1280]{1,0:T(8,128)(2,1)S(1)}, bf16[256,1280]{1,0:T(8,128)(2,1)S(1)}, u32[]{:S(2)}, u32[]{:S(2)}) collective-permute-start(bf16[256,1280]{1,0:T(8,128)(2,1)S(1)} %collective-permute-done.2.refs_2_), channel_id=1, source_target_pairs={{0,96},{24,696},{48,144},{72,744},{96,192},{120,24},{144,240},{168... | collective-permute-start | bytes 1966088 | tf_op jit(solution)/shard_map/ppermute | solution.py:117
  40.9 4.2 %collective-permute-done.5.refs_3_ = bf16[256,1280]{1,0:T(8,128)(2,1)S(1)} collective-permute-done((bf16[256,1280]{1,0:T(8,128)(2,1)S(1)}, bf16[256,1280]{1,0:T(8,128)(2,1)S(1)}, u32[]{:S(2)}, u32[]{:S(2)}) %collective-permute-start.5) | collective-permute-done | bytes 655392 | tf_op jit(solution)/shard_map/ppermute | solution.py:117
  45.1 2.8 %collective-permute-start.7 = (bf16[256,1280]{1,0:T(8,128)(2,1)S(1)}, bf16[256,1280]{1,0:T(8,128)(2,1)S(1)}, u32[]{:S(2)}, u32[]{:S(2)}) collective-permute-start(bf16[256,1280]{1,0:T(8,128)(2,1)S(1)} %collective-permute-done.5.refs_3_), channel_id=1, source_target_pairs={{0,96},{24,696},{48,144},{72,744},{96,192},{120,24},{144,240},{168... | collective-permute-start | bytes 1966088 | tf_op jit(solution)/shard_map/ppermute | solution.py:117
  47.9 1.4 %shard_map.46 = (f32[192,1280]{1,0:T(8,128)S(1)}, f32[192,1280]{1,0:T(8,128)S(1)}, f32[192,1]{1,0:T(8,128)S(1)}) custom-call(bf16[192,4096]{1,0:T(8,128)(2,1)S(1)} %copy-done, bf16[192,4096]{1,0:T(8,128)(2,1)S(1)} %collective-permute-done.1.others, bf16[128,1280]{1,0:T(8,128)(2,1)S(1)} %pad_maximum_fusion.refs_0_, ...), custom_call_target="tpu_custom_call" | custom-call | flops 880803840 | bytes 6225920 | tf_op jit(solution)/shard_map/pallas_call | solution.py:96
  49.3 2.8 %collective-permute-done.3.block.refs_1_ = bf16[256,1280]{1,0:T(8,128)(2,1)S(1)} collective-permute-done((bf16[256,1280]{1,0:T(8,128)(2,1)S(1)}, bf16[256,1280]{1,0:T(8,128)(2,1)S(1)}, u32[]{:S(2)}, u32[]{:S(2)}) %collective-permute-start.3) | collective-permute-done | bytes 655392 | tf_op jit(solution)/shard_map/ppermute | solution.py:117
  52.2 2.8 %collective-permute-start.6 = (bf16[128,1280]{1,0:T(8,128)(2,1)S(1)}, bf16[128,1280]{1,0:T(8,128)(2,1)S(1)}, u32[]{:S(2)}, u32[]{:S(2)}) collective-permute-start(bf16[128,1280]{1,0:T(8,128)(2,1)S(1)} %shard_map.47), channel_id=1, source_target_pairs={{0,96},{24,696},{48,144},{72,744},{96,192},{120,24},{144,240},{168... | collective-permute-start | bytes 983048 | tf_op jit(solution)/shard_map/ppermute | solution.py:117
  55.2 1.9 %collective-permute-start.8 = (bf16[128,1280]{1,0:T(8,128)(2,1)S(1)}, bf16[128,1280]{1,0:T(8,128)(2,1)S(1)}, u32[]{:S(2)}, u32[]{:S(2)}) collective-permute-start(bf16[128,1280]{1,0:T(8,128)(2,1)S(1)} %shard_map.49), channel_id=1, source_target_pairs={{0,96},{24,696},{48,144},{72,744},{96,192},{120,24},{144,240},{168... | collective-permute-start | bytes 983048 | tf_op jit(solution)/shard_map/ppermute | solution.py:117
  57.2 2.0 %collective-permute-done.7.refs_2_.block = bf16[256,1280]{1,0:T(8,128)(2,1)S(1)} collective-permute-done((bf16[256,1280]{1,0:T(8,128)(2,1)S(1)}, bf16[256,1280]{1,0:T(8,128)(2,1)S(1)}, u32[]{:S(2)}, u32[]{:S(2)}) %collective-permute-start.7) | collective-permute-done | bytes 655392 | tf_op jit(solution)/shard_map/ppermute | solution.py:117
  59.3 2.8 %collective-permute-start.9 = (bf16[128,1280]{1,0:T(8,128)(2,1)S(1)}, bf16[128,1280]{1,0:T(8,128)(2,1)S(1)}, u32[]{:S(2)}, u32[]{:S(2)}) collective-permute-start(bf16[128,1280]{1,0:T(8,128)(2,1)S(1)} %shard_map.50), channel_id=1, source_target_pairs={{0,96},{24,696},{48,144},{72,744},{96,192},{120,24},{144,240},{168... | collective-permute-start | bytes 983048 | tf_op jit(solution)/shard_map/ppermute | solution.py:117
  63.0 2.4 %collective-permute-start.10 = (bf16[128,1280]{1,0:T(8,128)(2,1)S(1)}, bf16[128,1280]{1,0:T(8,128)(2,1)S(1)}, u32[]{:S(2)}, u32[]{:S(2)}) collective-permute-start(bf16[128,1280]{1,0:T(8,128)(2,1)S(1)} %collective-permute-done.6.refs_0_), channel_id=1, source_target_pairs={{0,96},{24,696},{48,144},{72,744},{96,192},{120,24},{144,240},{168... | collective-permute-start | bytes 983048 | tf_op jit(solution)/shard_map/ppermute | solution.py:117
  66.2 3.5 %collective-permute-done.9.refs_2_ = bf16[128,1280]{1,0:T(8,128)(2,1)S(1)} collective-permute-done((bf16[128,1280]{1,0:T(8,128)(2,1)S(1)}, bf16[128,1280]{1,0:T(8,128)(2,1)S(1)}, u32[]{:S(2)}, u32[]{:S(2)}) %collective-permute-start.9) | collective-permute-done | bytes 327712 | tf_op jit(solution)/shard_map/ppermute | solution.py:117
  70.6 4.3 %all_gather.17.gate_arrived = f32[384,640]{1,0:T(8,128)S(1)} all-gather(f32[192,640]{1,0:T(8,128)S(1)} %get-tuple-element.30), channel_id=1, replica_groups={{0,24},{48,72},{96,120},{144,168},{192,216},{240,264},{288,312},{336,36..., dimensions={0}, use_global_device_ids=true | all-gather | bytes 1474560 | tf_op jit(solution)/shard_map/all_gather | solution.py:125
  74.9 2.5 %all_gather.18.up_arrived = f32[384,640]{1,0:T(8,128)S(1)} all-gather(f32[192,640]{1,0:T(8,128)S(1)} %get-tuple-element.31), channel_id=1, replica_groups={{0,24},{48,72},{96,120},{144,168},{192,216},{240,264},{288,312},{336,36..., dimensions={0}, use_global_device_ids=true | all-gather | bytes 1474560 | tf_op jit(solution)/shard_map/all_gather | solution.py:125
  77.4 2.3 %all_gather.19.refs_0_ = bf16[256,1280]{1,0:T(8,128)(2,1)S(1)} all-gather(bf16[128,1280]{1,0:T(8,128)(2,1)S(1)} %collective-permute-done.10), channel_id=1, replica_groups={{0,24},{48,72},{96,120},{144,168},{192,216},{240,264},{288,312},{336,36..., dimensions={0}, use_global_device_ids=true | all-gather | bytes 983040 | tf_op jit(solution)/shard_map/all_gather | solution.py:125
  79.7 1.1 %shard_map.52 = bf16[192,640]{1,0:T(8,128)(2,1)} custom-call(bf16[192,4096]{1,0:T(8,128)(2,1)S(1)} %copy-done, f32[192,1280]{1,0:T(8,128)S(1)} %get-tuple-element.29.total_before, f32[384,640]{1,0:T(8,128)S(1)} %all_gather.17.gate_arrived, f32[384,640]{1,0:T(8,128)S(1)} %all_gather.18.up_arrived, f32[192,1]{1,0:T(8,128)S(1)} %get-tuple-element.32.scale, ...), custom_call_target="tpu_custom_call" | custom-call | flops 251658240 | bytes 4587520 | tf_op jit(solution)/shard_map/pallas_call | solution.py:96
  (14 shorter events, 2.9 us)
Async XLA Ops:
  0.0 24.2 %copy-start = (bf16[192,4096]{1,0:T(8,128)(2,1)S(1)}, bf16[192,4096]{1,0:T(8,128)(2,1)}, u32[]{:S(2)}) copy-start(bf16[192,4096]{1,0:T(8,128)(2,1)} %tokens.7) | copy-start | bytes 4718596
  1.3 16.3 %collective-permute-start = (bf16[128,1280]{1,0:T(8,128)(2,1)S(1)}, bf16[128,1280]{1,0:T(8,128)(2,1)S(1)}, u32[]{:S(2)}, u32[]{:S(2)}) collective-permute-start(bf16[128,1280]{1,0:T(8,128)(2,1)S(1)} %pad_maximum_fusion.refs_0_), channel_id=1, source_target_pairs={{0,48},{24,72},{48,0},{72,24},{96,144},{120,168},{144,96},{168,120... | collective-permute-start | bytes 983048 | tf_op jit(solution)/shard_map/ppermute | solution.py:117
  15.6 12.7 %collective-permute-start.4 = (bf16[256,1280]{1,0:T(8,128)(2,1)S(1)}, bf16[256,1280]{1,0:T(8,128)(2,1)S(1)}, u32[]{:S(2)}, u32[]{:S(2)}) collective-permute-start(bf16[256,1280]{1,0:T(8,128)(2,1)S(1)} %all_gather.16), channel_id=1, source_target_pairs={{0,96},{24,696},{48,144},{72,744},{96,192},{120,24},{144,240},{168... | collective-permute-start | bytes 1966088 | tf_op jit(solution)/shard_map/ppermute | solution.py:117
  24.2 23.8 %collective-permute-start.1 = (bf16[192,4096]{1,0:T(8,128)(2,1)S(1)}, bf16[192,4096]{1,0:T(8,128)(2,1)S(1)}, u32[]{:S(2)}, u32[]{:S(2)}) collective-permute-start(bf16[192,4096]{1,0:T(8,128)(2,1)S(1)} %copy-done), channel_id=1, source_target_pairs={{0,24},{24,0},{48,72},{72,48},{96,120},{120,96},{144,168},{168,144... | collective-permute-start | bytes 4718600 | tf_op jit(solution)/shard_map/ppermute | solution.py:117
  26.5 11.6 %collective-permute-start.2 = (bf16[256,1280]{1,0:T(8,128)(2,1)S(1)}, bf16[256,1280]{1,0:T(8,128)(2,1)S(1)}, u32[]{:S(2)}, u32[]{:S(2)}) collective-permute-start(bf16[256,1280]{1,0:T(8,128)(2,1)S(1)} %all_gather.15), channel_id=1, source_target_pairs={{0,96},{24,696},{48,144},{72,744},{96,192},{120,24},{144,240},{168... | collective-permute-start | bytes 1966088 | tf_op jit(solution)/shard_map/ppermute | solution.py:117
  28.4 16.7 %collective-permute-start.5 = (bf16[256,1280]{1,0:T(8,128)(2,1)S(1)}, bf16[256,1280]{1,0:T(8,128)(2,1)S(1)}, u32[]{:S(2)}, u32[]{:S(2)}) collective-permute-start(bf16[256,1280]{1,0:T(8,128)(2,1)S(1)} %collective-permute-done.4.refs_1_), channel_id=1, source_target_pairs={{0,96},{24,696},{48,144},{72,744},{96,192},{120,24},{144,240},{168... | collective-permute-start | bytes 1966088 | tf_op jit(solution)/shard_map/ppermute | solution.py:117
  38.1 14.0 %collective-permute-start.3 = (bf16[256,1280]{1,0:T(8,128)(2,1)S(1)}, bf16[256,1280]{1,0:T(8,128)(2,1)S(1)}, u32[]{:S(2)}, u32[]{:S(2)}) collective-permute-start(bf16[256,1280]{1,0:T(8,128)(2,1)S(1)} %collective-permute-done.2.refs_2_), channel_id=1, source_target_pairs={{0,96},{24,696},{48,144},{72,744},{96,192},{120,24},{144,240},{168... | collective-permute-start | bytes 1966088 | tf_op jit(solution)/shard_map/ppermute | solution.py:117
  45.1 14.0 %collective-permute-start.7 = (bf16[256,1280]{1,0:T(8,128)(2,1)S(1)}, bf16[256,1280]{1,0:T(8,128)(2,1)S(1)}, u32[]{:S(2)}, u32[]{:S(2)}) collective-permute-start(bf16[256,1280]{1,0:T(8,128)(2,1)S(1)} %collective-permute-done.5.refs_3_), channel_id=1, source_target_pairs={{0,96},{24,696},{48,144},{72,744},{96,192},{120,24},{144,240},{168... | collective-permute-start | bytes 1966088 | tf_op jit(solution)/shard_map/ppermute | solution.py:117
  52.2 10.8 %collective-permute-start.6 = (bf16[128,1280]{1,0:T(8,128)(2,1)S(1)}, bf16[128,1280]{1,0:T(8,128)(2,1)S(1)}, u32[]{:S(2)}, u32[]{:S(2)}) collective-permute-start(bf16[128,1280]{1,0:T(8,128)(2,1)S(1)} %shard_map.47), channel_id=1, source_target_pairs={{0,96},{24,696},{48,144},{72,744},{96,192},{120,24},{144,240},{168... | collective-permute-start | bytes 983048 | tf_op jit(solution)/shard_map/ppermute | solution.py:117
  55.2 10.9 %collective-permute-start.8 = (bf16[128,1280]{1,0:T(8,128)(2,1)S(1)}, bf16[128,1280]{1,0:T(8,128)(2,1)S(1)}, u32[]{:S(2)}, u32[]{:S(2)}) collective-permute-start(bf16[128,1280]{1,0:T(8,128)(2,1)S(1)} %shard_map.49), channel_id=1, source_target_pairs={{0,96},{24,696},{48,144},{72,744},{96,192},{120,24},{144,240},{168... | collective-permute-start | bytes 983048 | tf_op jit(solution)/shard_map/ppermute | solution.py:117
  59.3 10.4 %collective-permute-start.9 = (bf16[128,1280]{1,0:T(8,128)(2,1)S(1)}, bf16[128,1280]{1,0:T(8,128)(2,1)S(1)}, u32[]{:S(2)}, u32[]{:S(2)}) collective-permute-start(bf16[128,1280]{1,0:T(8,128)(2,1)S(1)} %shard_map.50), channel_id=1, source_target_pairs={{0,96},{24,696},{48,144},{72,744},{96,192},{120,24},{144,240},{168... | collective-permute-start | bytes 983048 | tf_op jit(solution)/shard_map/ppermute | solution.py:117
  63.0 14.4 %collective-permute-start.10 = (bf16[128,1280]{1,0:T(8,128)(2,1)S(1)}, bf16[128,1280]{1,0:T(8,128)(2,1)S(1)}, u32[]{:S(2)}, u32[]{:S(2)}) collective-permute-start(bf16[128,1280]{1,0:T(8,128)(2,1)S(1)} %collective-permute-done.6.refs_0_), channel_id=1, source_target_pairs={{0,96},{24,696},{48,144},{72,744},{96,192},{120,24},{144,240},{168... | collective-permute-start | bytes 983048 | tf_op jit(solution)/shard_map/ppermute | solution.py:117

commit v7 on v6

--- a/solution.py
+++ b/solution.py
@@ -39,31 +39,28 @@
 
 
 def second_kernel(add, n, tokens, others, total_before, partial_before, *refs):
-    blocks, (total, partial) = refs[:n], refs[n:]
+    blocks, (total, gate, up, partial) = refs[:n], refs[n:]
     total[...] = total_before[...]
     partial[...] = partial_before[...]
     add(blocks, [(tokens, total), (others, partial)])
+    wide = gate.shape[1]
+    gate[...] = partial[:, :wide]
+    up[...] = partial[:, wide:]
 
 
-def third_kernel(add, n, tokens, others, total_before, partial_before, *refs):
-    blocks, (total, gate, up, sums) = refs[:n], refs[n:]
+def third_kernel(add, n, tokens, others, total_before, *refs):
+    blocks, (total, leaving, partial) = refs[:n], refs[n:]
     total[...] = total_before[...]
-    sums[...] = partial_before[...]
-    add(blocks, [(tokens, total), (others, sums)])
-    wide = gate.shape[1]
-    gate[...] = sums[:, :wide]
-    up[...] = sums[:, wide:]
+    partial[...] = jnp.zeros_like(partial)
+    add(blocks, [(tokens, total), (others, partial)])
+    leaving[...] = partial[...].astype(leaving.dtype)
 
 
-def last_kernel(add, n, tokens, total_before, gate_arrived, up_arrived, scale, *refs):
-    blocks, (hidden, total) = refs[:n], refs[n:]
+def last_kernel(add, n, total, gate_arrived, up_arrived, late, scale, hidden):
     rows, wide = hidden.shape
     theirs = pl.ds(pl.multiple_of((1 - lax.rem(lax.axis_index("fsdp"), 2)) * rows, rows), rows)
-    total[:, :wide] = total_before[:, :wide] + gate_arrived[theirs, :]
-    total[:, wide:] = total_before[:, wide:] + up_arrived[theirs, :]
-    add(blocks, [(tokens, total)])
-    gate = total[:, :wide] * scale[...]
-    up = total[:, wide:] * scale[...]
+    gate = (total[:, :wide] + gate_arrived[theirs, :] + late[theirs, :wide].astype(jnp.float32)) * scale[...]
+    up = (total[:, wide:] + up_arrived[theirs, :] + late[theirs, wide:].astype(jnp.float32)) * scale[...]
     hidden[...] = (gate / (1.0 + jnp.exp(-gate)) * up).astype(hidden.dtype)
 
 
@@ -88,10 +85,10 @@
     )(block)
 
 
-def call(kernel, *, high, specs, arrays, blocks, out_shape, scratch=()):
+def call(kernel, *, high, sum_width, specs, arrays, blocks, out_shape, scratch=()):
     n = len(blocks)
-    depth, wide = sum(b.shape[0] for b in blocks), blocks[0].shape[1]
-    rows = arrays[0].shape[0]
+    depth = sum(b.shape[0] for b in blocks)
+    rows, wide = arrays[0].shape[0], sum_width
     vmem = pl.BlockSpec(memory_space=pltpu.VMEM)
     return pl.pallas_call(
         functools.partial(kernel, functools.partial(add_blocks, specs, high), n),
@@ -132,7 +129,7 @@
         chip = join(own)
         rows = tokens.shape[0]
         sums = jax.ShapeDtypeStruct((rows, wide), jnp.float32)
-        step = functools.partial(call, high=high)
+        step = functools.partial(call, high=high, sum_width=wide)
 
         a1 = along(chip)
         beside, late = lax.optimization_barrier((join(b0), tokens))
@@ -152,32 +149,31 @@
         b3 = along(cut(b2))
         b3_rest = along(cut(b2, 1))
         a4 = along(cut(a3))
-        total, partial = step(
+        narrow = jax.ShapeDtypeStruct((rows, wide // 2), jnp.float32)
+        total, gate, up = step(
             second_kernel,
             specs=[(0, 1, 1), (2, 1, 0), (3, 0, 0)],
             arrays=[tokens, others, total, partial],
             blocks=[b0, b2, a3],
-            out_shape=(sums, sums),
+            out_shape=(sums, narrow, narrow),
+            scratch=[pltpu.VMEM((rows, wide), jnp.float32)],
         )
         b3, total = lax.optimization_barrier((b3, total))
         b4 = along(b3)
-        narrow = jax.ShapeDtypeStruct((rows, wide // 2), jnp.float32)
-        total, *partial = step(
+        total, late = step(
             third_kernel,
-            specs=[(3, 1, 1), (3, 1, 2), (4, 0, 1)],
-            arrays=[tokens, others, total, partial],
-            blocks=[b3, b3_rest, a4],
-            out_shape=(sums, narrow, narrow),
+            specs=[(3, 1, 1), (3, 1, 2), (4, 0, 1), (4, 1, 1)],
+            arrays=[tokens, others, total],
+            blocks=[b3, b3_rest, a4, b4],
+            out_shape=(sums, jax.ShapeDtypeStruct((rows, wide), jnp.bfloat16)),
             scratch=[pltpu.VMEM((rows, wide), jnp.float32)],
         )
-        partial = [join(v) for v in partial]
         return step(
             last_kernel,
-            specs=[(4, 1, 0)],
-            arrays=[tokens, total, *partial, scale],
-            blocks=[join(b4)],
+            specs=[],
+            arrays=[total, join(gate), join(up), join(late), scale],
+            blocks=[],
             out_shape=jax.ShapeDtypeStruct((rows, wide // 2), jnp.bfloat16),
-            scratch=[pltpu.VMEM((rows, wide), jnp.float32)],
         )
 
     return on_device

time: 81.3 us -> 80.1 us (0.985)
  waiting for transfers between devices: 20.9 us -> 18.5 us
  blocking collectives: 24.6 us -> 25.7 us
    ppermute x11, waiting for transfers between devices: 20.9 us -> 18.5 us  [move(): return lambda v: lax.ppermute(v, 'fsdp', pairs)]
    all_gather x5, blocking collectives: 24.6 us -> 25.7 us  [join(): lax.all_gather(v, 'fsdp', axis=0, tiled=True, axis_index_groups=core_pairs)]
  transfers between devices with their start and end apart: 11 -> 11, of which waited for: 6 -> 5; matrix products, arithmetic and copies ran while one was open for 0% -> 0% of each run, Pallas kernels for 4% -> 3%
where the time goes in v7:
time: 80.1 us; the launch traced here: 79.7 us
  starting transfers between devices  29.2 us (36%)
  blocking collectives  25.7 us (32%)
  waiting for transfers between devices  18.5 us (23%)
  Pallas kernels  4.81 us (6%)
  other arithmetic  1.28 us (2%)
    ppermute x11, starting transfers between devices, move(): return lambda v: lax.ppermute(v, 'fsdp', pairs)  29.2 us
    all_gather x5, blocking collectives, join(): lax.all_gather(v, 'fsdp', axis=0, tiled=True, axis_index_groups=core_pairs)  25.7 us
    ppermute x11, waiting for transfers between devices, move(): return lambda v: lax.ppermute(v, 'fsdp', pairs)  18.5 us
    pallas_call x4, Pallas kernels, call(): pl.pallas_call(functools.partial(kernel, functools.partial(add_blocks, sp...  4.46 us
  transfers between devices with their start and end apart: 11, of which 5 were waited for; matrix products, arithmetic and copies ran while one was open for 0% of the time, Pallas kernels for 3%

profile of v7, /device:TPU:1, one launch (start us, length us, event | category | flops | bytes accessed | tf_op | source)
XLA Modules:
  0.0 79.7 jit_solution(17404551550982783917)
XLA Ops:
  0.0 1.3 %multiply_convert_fusion.1 = (bf16[128,640]{1,0:T(8,128)(2,1)S(1)}, bf16[128,640]{1,0:T(8,128)(2,1)S(1)}) fusion(bf16[128,640]{1,0:T(8,128)(2,1)} %param.6, f32[128]{0:T(128)} %param.5, bf16[128,640]{1,0:T(8,128)(2,1)} %param.7), kind=kLoop, calls=%fused_computation.2 | loop fusion | flops 491520 | bytes 655872 | tf_op jit(solution)/shard_map/convert
  1.3 5.5 %collective-permute-start = (bf16[128,1280]{1,0:T(8,128)(2,1)S(1)}, bf16[128,1280]{1,0:T(8,128)(2,1)S(1)}, u32[]{:S(2)}, u32[]{:S(2)}) collective-permute-start(bf16[128,1280]{1,0:T(8,128)(2,1)S(1)} %pad_maximum_fusion.refs_0_), channel_id=1, source_target_pairs={{0,48},{24,72},{48,0},{72,24},{96,144},{120,168},{144,96},{168,120... | collective-permute-start | bytes 983048 | tf_op jit(solution)/shard_map/ppermute | solution.py:114
  6.8 8.9 %all_gather.16 = bf16[256,1280]{1,0:T(8,128)(2,1)S(1)} all-gather(bf16[128,1280]{1,0:T(8,128)(2,1)S(1)} %pad_maximum_fusion.refs_0_), channel_id=1, replica_groups={{0,24},{48,72},{96,120},{144,168},{192,216},{240,264},{288,312},{336,36..., dimensions={0}, use_global_device_ids=true | all-gather | bytes 983040 | tf_op jit(solution)/shard_map/all_gather | solution.py:122
  15.6 1.9 %collective-permute-start.4 = (bf16[256,1280]{1,0:T(8,128)(2,1)S(1)}, bf16[256,1280]{1,0:T(8,128)(2,1)S(1)}, u32[]{:S(2)}, u32[]{:S(2)}) collective-permute-start(bf16[256,1280]{1,0:T(8,128)(2,1)S(1)} %all_gather.16), channel_id=1, source_target_pairs={{0,96},{24,696},{48,144},{72,744},{96,192},{120,24},{144,240},{168... | collective-permute-start | bytes 1966088 | tf_op jit(solution)/shard_map/ppermute | solution.py:114
  17.6 6.6 %all_gather.15 = bf16[256,1280]{1,0:T(8,128)(2,1)S(1)} all-gather(bf16[128,1280]{1,0:T(8,128)(2,1)S(1)} %collective-permute-done.refs_0_), channel_id=1, replica_groups={{0,24},{48,72},{96,120},{144,168},{192,216},{240,264},{288,312},{336,36..., dimensions={0}, use_global_device_ids=true | all-gather | bytes 983040 | tf_op jit(solution)/shard_map/all_gather | solution.py:122
  24.2 2.3 %collective-permute-start.1 = (bf16[192,4096]{1,0:T(8,128)(2,1)S(1)}, bf16[192,4096]{1,0:T(8,128)(2,1)S(1)}, u32[]{:S(2)}, u32[]{:S(2)}) collective-permute-start(bf16[192,4096]{1,0:T(8,128)(2,1)S(1)} %copy-done), channel_id=1, source_target_pairs={{0,24},{24,0},{48,72},{72,48},{96,120},{120,96},{144,168},{168,144... | collective-permute-start | bytes 4718600 | tf_op jit(solution)/shard_map/ppermute | solution.py:114
  26.5 1.9 %collective-permute-start.2 = (bf16[256,1280]{1,0:T(8,128)(2,1)S(1)}, bf16[256,1280]{1,0:T(8,128)(2,1)S(1)}, u32[]{:S(2)}, u32[]{:S(2)}) collective-permute-start(bf16[256,1280]{1,0:T(8,128)(2,1)S(1)} %all_gather.15), channel_id=1, source_target_pairs={{0,96},{24,696},{48,144},{72,744},{96,192},{120,24},{144,240},{168... | collective-permute-start | bytes 1966088 | tf_op jit(solution)/shard_map/ppermute | solution.py:114
  28.4 1.9 %collective-permute-start.5 = (bf16[256,1280]{1,0:T(8,128)(2,1)S(1)}, bf16[256,1280]{1,0:T(8,128)(2,1)S(1)}, u32[]{:S(2)}, u32[]{:S(2)}) collective-permute-start(bf16[256,1280]{1,0:T(8,128)(2,1)S(1)} %collective-permute-done.4.refs_1_), channel_id=1, source_target_pairs={{0,96},{24,696},{48,144},{72,744},{96,192},{120,24},{144,240},{168... | collective-permute-start | bytes 1966088 | tf_op jit(solution)/shard_map/ppermute | solution.py:114
  30.3 7.8 %collective-permute-done.2.refs_2_ = bf16[256,1280]{1,0:T(8,128)(2,1)S(1)} collective-permute-done((bf16[256,1280]{1,0:T(8,128)(2,1)S(1)}, bf16[256,1280]{1,0:T(8,128)(2,1)S(1)}, u32[]{:S(2)}, u32[]{:S(2)}) %collective-permute-start.2) | collective-permute-done | bytes 655392 | tf_op jit(solution)/shard_map/ppermute | solution.py:114
  38.1 2.8 %collective-permute-start.3 = (bf16[256,1280]{1,0:T(8,128)(2,1)S(1)}, bf16[256,1280]{1,0:T(8,128)(2,1)S(1)}, u32[]{:S(2)}, u32[]{:S(2)}) collective-permute-start(bf16[256,1280]{1,0:T(8,128)(2,1)S(1)} %collective-permute-done.2.refs_2_), channel_id=1, source_target_pairs={{0,96},{24,696},{48,144},{72,744},{96,192},{120,24},{144,240},{168... | collective-permute-start | bytes 1966088 | tf_op jit(solution)/shard_map/ppermute | solution.py:114
  40.9 4.2 %collective-permute-done.5.refs_3_ = bf16[256,1280]{1,0:T(8,128)(2,1)S(1)} collective-permute-done((bf16[256,1280]{1,0:T(8,128)(2,1)S(1)}, bf16[256,1280]{1,0:T(8,128)(2,1)S(1)}, u32[]{:S(2)}, u32[]{:S(2)}) %collective-permute-start.5) | collective-permute-done | bytes 655392 | tf_op jit(solution)/shard_map/ppermute | solution.py:114
  45.1 2.8 %collective-permute-start.7 = (bf16[256,1280]{1,0:T(8,128)(2,1)S(1)}, bf16[256,1280]{1,0:T(8,128)(2,1)S(1)}, u32[]{:S(2)}, u32[]{:S(2)}) collective-permute-start(bf16[256,1280]{1,0:T(8,128)(2,1)S(1)} %collective-permute-done.5.refs_3_), channel_id=1, source_target_pairs={{0,96},{24,696},{48,144},{72,744},{96,192},{120,24},{144,240},{168... | collective-permute-start | bytes 1966088 | tf_op jit(solution)/shard_map/ppermute | solution.py:114
  47.9 1.4 %shard_map.46 = (f32[192,1280]{1,0:T(8,128)S(1)}, f32[192,1280]{1,0:T(8,128)S(1)}, f32[192,1]{1,0:T(8,128)S(1)}) custom-call(bf16[192,4096]{1,0:T(8,128)(2,1)S(1)} %copy-done, bf16[192,4096]{1,0:T(8,128)(2,1)S(1)} %collective-permute-done.1.others, bf16[128,1280]{1,0:T(8,128)(2,1)S(1)} %pad_maximum_fusion.refs_0_, ...), custom_call_target="tpu_custom_call" | custom-call | flops 880803840 | bytes 6225920 | tf_op jit(solution)/shard_map/pallas_call | solution.py:93
  49.3 2.8 %collective-permute-done.3.block.refs_1_ = bf16[256,1280]{1,0:T(8,128)(2,1)S(1)} collective-permute-done((bf16[256,1280]{1,0:T(8,128)(2,1)S(1)}, bf16[256,1280]{1,0:T(8,128)(2,1)S(1)}, u32[]{:S(2)}, u32[]{:S(2)}) %collective-permute-start.3) | collective-permute-done | bytes 655392 | tf_op jit(solution)/shard_map/ppermute | solution.py:114
  52.2 2.8 %collective-permute-start.6 = (bf16[128,1280]{1,0:T(8,128)(2,1)S(1)}, bf16[128,1280]{1,0:T(8,128)(2,1)S(1)}, u32[]{:S(2)}, u32[]{:S(2)}) collective-permute-start(bf16[128,1280]{1,0:T(8,128)(2,1)S(1)} %shard_map.47), channel_id=1, source_target_pairs={{0,96},{24,696},{48,144},{72,744},{96,192},{120,24},{144,240},{168... | collective-permute-start | bytes 983048 | tf_op jit(solution)/shard_map/ppermute | solution.py:114
  55.2 1.9 %collective-permute-start.8 = (bf16[128,1280]{1,0:T(8,128)(2,1)S(1)}, bf16[128,1280]{1,0:T(8,128)(2,1)S(1)}, u32[]{:S(2)}, u32[]{:S(2)}) collective-permute-start(bf16[128,1280]{1,0:T(8,128)(2,1)S(1)} %shard_map.49), channel_id=1, source_target_pairs={{0,96},{24,696},{48,144},{72,744},{96,192},{120,24},{144,240},{168... | collective-permute-start | bytes 983048 | tf_op jit(solution)/shard_map/ppermute | solution.py:114
  57.2 2.0 %collective-permute-done.7.refs_2_.block = bf16[256,1280]{1,0:T(8,128)(2,1)S(1)} collective-permute-done((bf16[256,1280]{1,0:T(8,128)(2,1)S(1)}, bf16[256,1280]{1,0:T(8,128)(2,1)S(1)}, u32[]{:S(2)}, u32[]{:S(2)}) %collective-permute-start.7) | collective-permute-done | bytes 655392 | tf_op jit(solution)/shard_map/ppermute | solution.py:114
  59.3 2.8 %collective-permute-start.9 = (bf16[128,1280]{1,0:T(8,128)(2,1)S(1)}, bf16[128,1280]{1,0:T(8,128)(2,1)S(1)}, u32[]{:S(2)}, u32[]{:S(2)}) collective-permute-start(bf16[128,1280]{1,0:T(8,128)(2,1)S(1)} %shard_map.50), channel_id=1, source_target_pairs={{0,96},{24,696},{48,144},{72,744},{96,192},{120,24},{144,240},{168... | collective-permute-start | bytes 983048 | tf_op jit(solution)/shard_map/ppermute | solution.py:114
  63.0 2.4 %collective-permute-start.10 = (bf16[128,1280]{1,0:T(8,128)(2,1)S(1)}, bf16[128,1280]{1,0:T(8,128)(2,1)S(1)}, u32[]{:S(2)}, u32[]{:S(2)}) collective-permute-start(bf16[128,1280]{1,0:T(8,128)(2,1)S(1)} %collective-permute-done.6.refs_0_), channel_id=1, source_target_pairs={{0,96},{24,696},{48,144},{72,744},{96,192},{120,24},{144,240},{168... | collective-permute-start | bytes 983048 | tf_op jit(solution)/shard_map/ppermute | solution.py:114
  65.5 3.4 %all_gather.17.gate_arrived = f32[384,640]{1,0:T(8,128)S(1)} all-gather(f32[192,640]{1,0:T(8,128)S(1)} %get-tuple-element.29), channel_id=1, replica_groups={{0,24},{48,72},{96,120},{144,168},{192,216},{240,264},{288,312},{336,36..., dimensions={0}, use_global_device_ids=true | all-gather | bytes 1474560 | tf_op jit(solution)/shard_map/all_gather | solution.py:122
  68.9 2.5 %all_gather.18.up_arrived = f32[384,640]{1,0:T(8,128)S(1)} all-gather(f32[192,640]{1,0:T(8,128)S(1)} %get-tuple-element.30), channel_id=1, replica_groups={{0,24},{48,72},{96,120},{144,168},{192,216},{240,264},{288,312},{336,36..., dimensions={0}, use_global_device_ids=true | all-gather | bytes 1474560 | tf_op jit(solution)/shard_map/all_gather | solution.py:122
  71.4 1.8 %collective-permute-done.10.refs_3_ = bf16[128,1280]{1,0:T(8,128)(2,1)S(1)} collective-permute-done((bf16[128,1280]{1,0:T(8,128)(2,1)S(1)}, bf16[128,1280]{1,0:T(8,128)(2,1)S(1)}, u32[]{:S(2)}, u32[]{:S(2)}) %collective-permute-start.10) | collective-permute-done | bytes 327712 | tf_op jit(solution)/shard_map/ppermute | solution.py:114
  73.2 1.2 %shard_map.51 = (f32[192,1280]{1,0:T(8,128)S(1)}, bf16[192,1280]{1,0:T(8,128)(2,1)S(1)}) custom-call(bf16[192,4096]{1,0:T(8,128)(2,1)S(1)} %copy-done, bf16[192,4096]{1,0:T(8,128)(2,1)S(1)} %collective-permute-done.1.others, f32[192,1280]{1,0:T(8,128)S(1)} %get-tuple-element.26.total_before, bf16[128,1280]{1,0:T(8,128)(2,1)S(1)} %collective-permute-done.6.refs_0_, ...), custom_call_target="tpu_custom_call" | custom-call | flops 503316480 | bytes 5242880 | tf_op jit(solution)/shard_map/pallas_call | solution.py:93
  74.4 4.3 %all_gather.19.late = bf16[384,1280]{1,0:T(8,128)(2,1)S(1)} all-gather(bf16[192,1280]{1,0:T(8,128)(2,1)S(1)} %get-tuple-element.31), channel_id=1, replica_groups={{0,24},{48,72},{96,120},{144,168},{192,216},{240,264},{288,312},{336,36..., dimensions={0}, use_global_device_ids=true | all-gather | bytes 1474560 | tf_op jit(solution)/shard_map/all_gather | solution.py:122
  (14 shorter events, 2.3 us)
Async XLA Ops:
  0.0 24.2 %copy-start = (bf16[192,4096]{1,0:T(8,128)(2,1)S(1)}, bf16[192,4096]{1,0:T(8,128)(2,1)}, u32[]{:S(2)}) copy-start(bf16[192,4096]{1,0:T(8,128)(2,1)} %tokens.5) | copy-start | bytes 4718596
  1.3 16.3 %collective-permute-start = (bf16[128,1280]{1,0:T(8,128)(2,1)S(1)}, bf16[128,1280]{1,0:T(8,128)(2,1)S(1)}, u32[]{:S(2)}, u32[]{:S(2)}) collective-permute-start(bf16[128,1280]{1,0:T(8,128)(2,1)S(1)} %pad_maximum_fusion.refs_0_), channel_id=1, source_target_pairs={{0,48},{24,72},{48,0},{72,24},{96,144},{120,168},{144,96},{168,120... | collective-permute-start | bytes 983048 | tf_op jit(solution)/shard_map/ppermute | solution.py:114
  15.6 12.7 %collective-permute-start.4 = (bf16[256,1280]{1,0:T(8,128)(2,1)S(1)}, bf16[256,1280]{1,0:T(8,128)(2,1)S(1)}, u32[]{:S(2)}, u32[]{:S(2)}) collective-permute-start(bf16[256,1280]{1,0:T(8,128)(2,1)S(1)} %all_gather.16), channel_id=1, source_target_pairs={{0,96},{24,696},{48,144},{72,744},{96,192},{120,24},{144,240},{168... | collective-permute-start | bytes 1966088 | tf_op jit(solution)/shard_map/ppermute | solution.py:114
  24.2 23.8 %collective-permute-start.1 = (bf16[192,4096]{1,0:T(8,128)(2,1)S(1)}, bf16[192,4096]{1,0:T(8,128)(2,1)S(1)}, u32[]{:S(2)}, u32[]{:S(2)}) collective-permute-start(bf16[192,4096]{1,0:T(8,128)(2,1)S(1)} %copy-done), channel_id=1, source_target_pairs={{0,24},{24,0},{48,72},{72,48},{96,120},{120,96},{144,168},{168,144... | collective-permute-start | bytes 4718600 | tf_op jit(solution)/shard_map/ppermute | solution.py:114
  26.5 11.6 %collective-permute-start.2 = (bf16[256,1280]{1,0:T(8,128)(2,1)S(1)}, bf16[256,1280]{1,0:T(8,128)(2,1)S(1)}, u32[]{:S(2)}, u32[]{:S(2)}) collective-permute-start(bf16[256,1280]{1,0:T(8,128)(2,1)S(1)} %all_gather.15), channel_id=1, source_target_pairs={{0,96},{24,696},{48,144},{72,744},{96,192},{120,24},{144,240},{168... | collective-permute-start | bytes 1966088 | tf_op jit(solution)/shard_map/ppermute | solution.py:114
  28.4 16.7 %collective-permute-start.5 = (bf16[256,1280]{1,0:T(8,128)(2,1)S(1)}, bf16[256,1280]{1,0:T(8,128)(2,1)S(1)}, u32[]{:S(2)}, u32[]{:S(2)}) collective-permute-start(bf16[256,1280]{1,0:T(8,128)(2,1)S(1)} %collective-permute-done.4.refs_1_), channel_id=1, source_target_pairs={{0,96},{24,696},{48,144},{72,744},{96,192},{120,24},{144,240},{168... | collective-permute-start | bytes 1966088 | tf_op jit(solution)/shard_map/ppermute | solution.py:114
  38.1 14.0 %collective-permute-start.3 = (bf16[256,1280]{1,0:T(8,128)(2,1)S(1)}, bf16[256,1280]{1,0:T(8,128)(2,1)S(1)}, u32[]{:S(2)}, u32[]{:S(2)}) collective-permute-start(bf16[256,1280]{1,0:T(8,128)(2,1)S(1)} %collective-permute-done.2.refs_2_), channel_id=1, source_target_pairs={{0,96},{24,696},{48,144},{72,744},{96,192},{120,24},{144,240},{168... | collective-permute-start | bytes 1966088 | tf_op jit(solution)/shard_map/ppermute | solution.py:114
  45.1 14.0 %collective-permute-start.7 = (bf16[256,1280]{1,0:T(8,128)(2,1)S(1)}, bf16[256,1280]{1,0:T(8,128)(2,1)S(1)}, u32[]{:S(2)}, u32[]{:S(2)}) collective-permute-start(bf16[256,1280]{1,0:T(8,128)(2,1)S(1)} %collective-permute-done.5.refs_3_), channel_id=1, source_target_pairs={{0,96},{24,696},{48,144},{72,744},{96,192},{120,24},{144,240},{168... | collective-permute-start | bytes 1966088 | tf_op jit(solution)/shard_map/ppermute | solution.py:114
  52.2 10.8 %collective-permute-start.6 = (bf16[128,1280]{1,0:T(8,128)(2,1)S(1)}, bf16[128,1280]{1,0:T(8,128)(2,1)S(1)}, u32[]{:S(2)}, u32[]{:S(2)}) collective-permute-start(bf16[128,1280]{1,0:T(8,128)(2,1)S(1)} %shard_map.47), channel_id=1, source_target_pairs={{0,96},{24,696},{48,144},{72,744},{96,192},{120,24},{144,240},{168... | collective-permute-start | bytes 983048 | tf_op jit(solution)/shard_map/ppermute | solution.py:114
  55.2 16.2 %collective-permute-start.8 = (bf16[128,1280]{1,0:T(8,128)(2,1)S(1)}, bf16[128,1280]{1,0:T(8,128)(2,1)S(1)}, u32[]{:S(2)}, u32[]{:S(2)}) collective-permute-start(bf16[128,1280]{1,0:T(8,128)(2,1)S(1)} %shard_map.49), channel_id=1, source_target_pairs={{0,96},{24,696},{48,144},{72,744},{96,192},{120,24},{144,240},{168... | collective-permute-start | bytes 983048 | tf_op jit(solution)/shard_map/ppermute | solution.py:114
  59.3 12.2 %collective-permute-start.9 = (bf16[128,1280]{1,0:T(8,128)(2,1)S(1)}, bf16[128,1280]{1,0:T(8,128)(2,1)S(1)}, u32[]{:S(2)}, u32[]{:S(2)}) collective-permute-start(bf16[128,1280]{1,0:T(8,128)(2,1)S(1)} %shard_map.50), channel_id=1, source_target_pairs={{0,96},{24,696},{48,144},{72,744},{96,192},{120,24},{144,240},{168... | collective-permute-start | bytes 983048 | tf_op jit(solution)/shard_map/ppermute | solution.py:114
  63.0 10.1 %collective-permute-start.10 = (bf16[128,1280]{1,0:T(8,128)(2,1)S(1)}, bf16[128,1280]{1,0:T(8,128)(2,1)S(1)}, u32[]{:S(2)}, u32[]{:S(2)}) collective-permute-start(bf16[128,1280]{1,0:T(8,128)(2,1)S(1)} %collective-permute-done.6.refs_0_), channel_id=1, source_target_pairs={{0,96},{24,696},{48,144},{72,744},{96,192},{120,24},{144,240},{168... | collective-permute-start | bytes 983048 | tf_op jit(solution)/shard_map/ppermute | solution.py:114

commit v8 on v7

--- a/solution.py
+++ b/solution.py
@@ -20,13 +20,19 @@
     return (y * 2 + (1 - x if other else x)) * 2 + (0, core, 1 - core)[half]
 
 
+def theirs(ref):
+    rows = ref.shape[0]
+    return pl.ds(pl.multiple_of((1 - lax.rem(lax.axis_index("fsdp"), 2)) * rows, rows), rows)
+
+
 def add_blocks(specs, high, blocks, pairs):
     for spec, block in zip(specs, blocks):
         depth = block.shape[0]
         unit = depth if spec[2] else depth // 2
         start = pl.multiple_of(column(spec, high) * unit, unit)
         for tokens, total in pairs:
-            total[...] += jnp.dot(tokens[:, pl.ds(start, depth)], block[...], preferred_element_type=jnp.float32)
+            left = tokens[theirs(total) if tokens.shape[0] > total.shape[0] else slice(None), pl.ds(start, depth)]
+            total[...] += jnp.dot(left, block[...], preferred_element_type=jnp.float32)
 
 
 def first_kernel(add, n, tokens, others, *refs):
@@ -57,10 +63,10 @@
 
 
 def last_kernel(add, n, total, gate_arrived, up_arrived, late, scale, hidden):
-    rows, wide = hidden.shape
-    theirs = pl.ds(pl.multiple_of((1 - lax.rem(lax.axis_index("fsdp"), 2)) * rows, rows), rows)
-    gate = (total[:, :wide] + gate_arrived[theirs, :] + late[theirs, :wide].astype(jnp.float32)) * scale[...]
-    up = (total[:, wide:] + up_arrived[theirs, :] + late[theirs, wide:].astype(jnp.float32)) * scale[...]
+    wide = hidden.shape[1]
+    other = theirs(hidden)
+    gate = (total[:, :wide] + gate_arrived[other, :] + late[other, :wide].astype(jnp.float32)) * scale[...]
+    up = (total[:, wide:] + up_arrived[other, :] + late[other, wide:].astype(jnp.float32)) * scale[...]
     hidden[...] = (gate / (1.0 + jnp.exp(-gate)) * up).astype(hidden.dtype)
 
 
@@ -115,7 +121,6 @@
 
     along = move(lambda y, x, c: (y + 1 - 2 * c, x, c))
     across = move(lambda y, x, c: (y, x + 1, c))
-    swap = move(lambda y, x, c: (y, x, c + 1))
     core_pairs = [[f, f + 1] for f in range(0, count, 2)]
 
     def join(v):
@@ -132,9 +137,8 @@
         step = functools.partial(call, high=high, sum_width=wide)
 
         a1 = along(chip)
-        beside, late = lax.optimization_barrier((join(b0), tokens))
-        b1 = along(beside)
-        others = swap(late)
+        b1 = along(join(b0))
+        others = join(tokens)
         a2 = along(a1)
         b2 = along(b1)
         a3 = along(a2)

time: 80.1 us -> 95.4 us (1.19)
  between operations: 0.17 us -> 13.6 us
  local copies, waits for them, and re-layouts: 0.01 us -> 3.81 us
  waiting for transfers between devices: 18.5 us -> 15.6 us
  starting transfers between devices: 29.2 us -> 26.4 us
  blocking collectives: 25.7 us -> 28.3 us
  Pallas kernels: 4.81 us -> 6.11 us
    unnamed x2 -> x8, local copies, waits for them, and re-layouts: 0.01 us -> 3.81 us
    ppermute x11 -> x10, waiting for transfers between devices: 18.5 us -> 14.8 us  [move(): return lambda v: lax.ppermute(v, 'fsdp', pairs)]
    ppermute x11 -> x10, starting transfers between devices: 29.2 us -> 26.4 us  [move(): return lambda v: lax.ppermute(v, 'fsdp', pairs)]
    all_gather x5, blocking collectives: 25.7 us -> 28.3 us  [join(): lax.all_gather(v, 'fsdp', axis=0, tiled=True, axis_index_groups=core_pairs)]
    pallas_call x4, Pallas kernels: 4.46 us -> 5.74 us  [call(): pl.pallas_call(functools.partial(kernel, functools.partial(add_blocks, sp...]
  transfers between devices with their start and end apart: 11 -> 11, of which waited for: 5 -> 5; matrix products, arithmetic and copies ran while one was open for 0% -> 1% of each run, Pallas kernels for 3% -> 4%
where the time goes in v8:
time: 95.4 us; the launch traced here: 94.9 us
  blocking collectives  28.3 us (30%)
  starting transfers between devices  26.4 us (28%)
  waiting for transfers between devices  15.6 us (16%)
  between operations  13.6 us (14%)
  Pallas kernels  6.11 us (6%)
  local copies, waits for them, and re-layouts  3.81 us (4%)
  other arithmetic  1.16 us (1%)
    all_gather x5, blocking collectives, join(): lax.all_gather(v, 'fsdp', axis=0, tiled=True, axis_index_groups=core_pairs)  28.3 us
    ppermute x10, starting transfers between devices, move(): return lambda v: lax.ppermute(v, 'fsdp', pairs)  26.4 us
    ppermute x10, waiting for transfers between devices, move(): return lambda v: lax.ppermute(v, 'fsdp', pairs)  14.8 us
    pallas_call x4, Pallas kernels, call(): pl.pallas_call(functools.partial(kernel, functools.partial(add_blocks, sp...  5.74 us
    unnamed x8, local copies, waits for them, and re-layouts  3.81 us
  transfers between devices with their start and end apart: 11, of which 5 were waited for; matrix products, arithmetic and copies ran while one was open for 1% of the time, Pallas kernels for 4%

profile of v8, /device:TPU:1, one launch (start us, length us, event | category | flops | bytes accessed | tf_op | source)
XLA Modules:
  0.0 94.9 jit_solution(4809715042562269884)
XLA Ops:
  7.3 1.1 %multiply_convert_fusion.1 = (bf16[128,640]{1,0:T(8,128)(2,1)S(1)}, bf16[128,640]{1,0:T(8,128)(2,1)S(1)}) fusion(bf16[128,640]{1,0:T(8,128)(2,1)} %param.6, f32[128]{0:T(128)} %param.5, bf16[128,640]{1,0:T(8,128)(2,1)} %param.7), kind=kLoop, calls=%fused_computation.2 | loop fusion | flops 491520 | bytes 655872 | tf_op jit(solution)/shard_map/convert
  8.4 5.5 %collective-permute-start = (bf16[128,1280]{1,0:T(8,128)(2,1)S(1)}, bf16[128,1280]{1,0:T(8,128)(2,1)S(1)}, u32[]{:S(2)}, u32[]{:S(2)}) collective-permute-start(bf16[128,1280]{1,0:T(8,128)(2,1)S(1)} %pad_maximum_fusion.refs_0_), channel_id=1, source_target_pairs={{0,48},{24,72},{48,0},{72,24},{96,144},{120,168},{144,96},{168,120... | collective-permute-start | bytes 983048 | tf_op jit(solution)/shard_map/ppermute | solution.py:120
  13.9 8.9 %all_gather.20 = bf16[256,1280]{1,0:T(8,128)(2,1)S(1)} all-gather(bf16[128,1280]{1,0:T(8,128)(2,1)S(1)} %pad_maximum_fusion.refs_0_), channel_id=1, replica_groups={{0,24},{48,72},{96,120},{144,168},{192,216},{240,264},{288,312},{336,36..., dimensions={0}, use_global_device_ids=true | all-gather | bytes 983040 | tf_op jit(solution)/shard_map/all_gather | solution.py:127
  22.8 1.9 %collective-permute-start.3 = (bf16[256,1280]{1,0:T(8,128)(2,1)S(1)}, bf16[256,1280]{1,0:T(8,128)(2,1)S(1)}, u32[]{:S(2)}, u32[]{:S(2)}) collective-permute-start(bf16[256,1280]{1,0:T(8,128)(2,1)S(1)} %all_gather.20), channel_id=1, source_target_pairs={{0,96},{24,696},{48,144},{72,744},{96,192},{120,24},{144,240},{168... | collective-permute-start | bytes 1966088 | tf_op jit(solution)/shard_map/ppermute | solution.py:120
  24.7 6.6 %all_gather.19 = bf16[256,1280]{1,0:T(8,128)(2,1)S(1)} all-gather(bf16[128,1280]{1,0:T(8,128)(2,1)S(1)} %collective-permute-done.refs_0_), channel_id=1, replica_groups={{0,24},{48,72},{96,120},{144,168},{192,216},{240,264},{288,312},{336,36..., dimensions={0}, use_global_device_ids=true | all-gather | bytes 983040 | tf_op jit(solution)/shard_map/all_gather | solution.py:127
  31.3 1.9 %collective-permute-start.1 = (bf16[256,1280]{1,0:T(8,128)(2,1)S(1)}, bf16[256,1280]{1,0:T(8,128)(2,1)}, u32[]{:S(2)}, u32[]{:S(2)}) collective-permute-start(bf16[256,1280]{1,0:T(8,128)(2,1)S(1)} %all_gather.19), channel_id=1, source_target_pairs={{0,96},{24,696},{48,144},{72,744},{96,192},{120,24},{144,240},{168... | collective-permute-start | bytes 1966088 | tf_op jit(solution)/shard_map/ppermute | solution.py:120
  33.2 1.2 %collective-permute-done.3.refs_1_ = bf16[256,1280]{1,0:T(8,128)(2,1)S(1)} collective-permute-done((bf16[256,1280]{1,0:T(8,128)(2,1)S(1)}, bf16[256,1280]{1,0:T(8,128)(2,1)S(1)}, u32[]{:S(2)}, u32[]{:S(2)}) %collective-permute-start.3) | collective-permute-done | bytes 655392 | tf_op jit(solution)/shard_map/ppermute | solution.py:120
  34.4 2.8 %collective-permute-start.4 = (bf16[256,1280]{1,0:T(8,128)(2,1)S(1)}, bf16[256,1280]{1,0:T(8,128)(2,1)}, u32[]{:S(2)}, u32[]{:S(2)}) collective-permute-start(bf16[256,1280]{1,0:T(8,128)(2,1)S(1)} %collective-permute-done.3.refs_1_), channel_id=1, source_target_pairs={{0,96},{24,696},{48,144},{72,744},{96,192},{120,24},{144,240},{168... | collective-permute-start | bytes 1966088 | tf_op jit(solution)/shard_map/ppermute | solution.py:120
  38.1 5.0 %collective-permute-done.1.refs_2_ = bf16[256,1280]{1,0:T(8,128)(2,1)} collective-permute-done((bf16[256,1280]{1,0:T(8,128)(2,1)S(1)}, bf16[256,1280]{1,0:T(8,128)(2,1)}, u32[]{:S(2)}, u32[]{:S(2)}) %collective-permute-start.1) | collective-permute-done | bytes 655392 | tf_op jit(solution)/shard_map/ppermute | solution.py:120
  43.0 2.8 %collective-permute-start.2 = (bf16[256,1280]{1,0:T(8,128)(2,1)}, bf16[256,1280]{1,0:T(8,128)(2,1)S(1)}, u32[]{:S(2)}, u32[]{:S(2)}) collective-permute-start(bf16[256,1280]{1,0:T(8,128)(2,1)} %collective-permute-done.1.refs_2_), channel_id=1, source_target_pairs={{0,96},{24,696},{48,144},{72,744},{96,192},{120,24},{144,240},{168... | collective-permute-start | bytes 1966088 | tf_op jit(solution)/shard_map/ppermute | solution.py:120
  45.9 4.2 %collective-permute-done.4.refs_3_ = bf16[256,1280]{1,0:T(8,128)(2,1)} collective-permute-done((bf16[256,1280]{1,0:T(8,128)(2,1)S(1)}, bf16[256,1280]{1,0:T(8,128)(2,1)}, u32[]{:S(2)}, u32[]{:S(2)}) %collective-permute-start.4) | collective-permute-done | bytes 655392 | tf_op jit(solution)/shard_map/ppermute | solution.py:120
  50.1 2.8 %collective-permute-start.6 = (bf16[256,1280]{1,0:T(8,128)(2,1)}, bf16[256,1280]{1,0:T(8,128)(2,1)S(1)}, u32[]{:S(2)}, u32[]{:S(2)}) collective-permute-start(bf16[256,1280]{1,0:T(8,128)(2,1)} %collective-permute-done.4.refs_3_), channel_id=1, source_target_pairs={{0,96},{24,696},{48,144},{72,744},{96,192},{120,24},{144,240},{168... | collective-permute-start | bytes 1966088 | tf_op jit(solution)/shard_map/ppermute | solution.py:120
  52.9 1.9 %copy-done = bf16[384,4096]{1,0:T(8,128)(2,1)S(1)} copy-done((bf16[384,4096]{1,0:T(8,128)(2,1)S(1)}, bf16[384,4096]{1,0:T(8,128)(2,1)}, u32[]{:S(2)}) %copy-start) | copy-done | bytes 3145752
  55.9 2.7 %shard_map.46 = (f32[192,1280]{1,0:T(8,128)S(1)}, f32[192,1280]{1,0:T(8,128)S(1)}, f32[192,1]{1,0:T(8,128)S(1)}) custom-call(bf16[192,4096]{1,0:T(8,128)(2,1)S(1)} %copy-done.1, bf16[384,4096]{1,0:T(8,128)(2,1)S(1)} %copy-done, bf16[128,1280]{1,0:T(8,128)(2,1)S(1)} %pad_maximum_fusion.refs_0_, bf16[256,1280]{1,0:T(8,128)(2,1)S(1)} %copy-done.3, ...), custom_call_target="tpu_custom_call" | custom-call | flops 880803840 | bytes 6225920 | tf_op jit(solution)/shard_map/pallas_call | solution.py:99
  58.7 1.9 %collective-permute-start.5 = (bf16[128,1280]{1,0:T(8,128)(2,1)S(1)}, bf16[128,1280]{1,0:T(8,128)(2,1)S(1)}, u32[]{:S(2)}, u32[]{:S(2)}) collective-permute-start(bf16[128,1280]{1,0:T(8,128)(2,1)S(1)} %shard_map.47), channel_id=1, source_target_pairs={{0,96},{24,696},{48,144},{72,744},{96,192},{120,24},{144,240},{168... | collective-permute-start | bytes 983048 | tf_op jit(solution)/shard_map/ppermute | solution.py:120
  60.7 3.3 %collective-permute-done.6.refs_2_.block = bf16[256,1280]{1,0:T(8,128)(2,1)S(1)} collective-permute-done((bf16[256,1280]{1,0:T(8,128)(2,1)}, bf16[256,1280]{1,0:T(8,128)(2,1)S(1)}, u32[]{:S(2)}, u32[]{:S(2)}) %collective-permute-start.6) | collective-permute-done | bytes 655392 | tf_op jit(solution)/shard_map/ppermute | solution.py:120
  64.1 2.8 %collective-permute-start.8 = (bf16[128,1280]{1,0:T(8,128)(2,1)S(1)}, bf16[128,1280]{1,0:T(8,128)(2,1)S(1)}, u32[]{:S(2)}, u32[]{:S(2)}) collective-permute-start(bf16[128,1280]{1,0:T(8,128)(2,1)S(1)} %shard_map.50), channel_id=1, source_target_pairs={{0,96},{24,696},{48,144},{72,744},{96,192},{120,24},{144,240},{168... | collective-permute-start | bytes 983048 | tf_op jit(solution)/shard_map/ppermute | solution.py:120
  67.1 1.9 %collective-permute-start.7 = (bf16[128,1280]{1,0:T(8,128)(2,1)S(1)}, bf16[128,1280]{1,0:T(8,128)(2,1)S(1)}, u32[]{:S(2)}, u32[]{:S(2)}) collective-permute-start(bf16[128,1280]{1,0:T(8,128)(2,1)S(1)} %shard_map.49), channel_id=1, source_target_pairs={{0,96},{24,696},{48,144},{72,744},{96,192},{120,24},{144,240},{168... | collective-permute-start | bytes 983048 | tf_op jit(solution)/shard_map/ppermute | solution.py:120
  70.0 1.9 %collective-permute-start.9 = (bf16[128,1280]{1,0:T(8,128)(2,1)S(1)}, bf16[128,1280]{1,0:T(8,128)(2,1)S(1)}, u32[]{:S(2)}, u32[]{:S(2)}) collective-permute-start(bf16[128,1280]{1,0:T(8,128)(2,1)S(1)} %collective-permute-done.5.refs_0_), channel_id=1, source_target_pairs={{0,96},{24,696},{48,144},{72,744},{96,192},{120,24},{144,240},{168... | collective-permute-start | bytes 983048 | tf_op jit(solution)/shard_map/ppermute | solution.py:120
  71.9 3.7 %all_gather.21.gate_arrived = f32[384,640]{1,0:T(8,128)S(1)} all-gather(f32[192,640]{1,0:T(8,128)S(1)} %get-tuple-element.25), channel_id=1, replica_groups={{0,24},{48,72},{96,120},{144,168},{192,216},{240,264},{288,312},{336,36..., dimensions={0}, use_global_device_ids=true | all-gather | bytes 1474560 | tf_op jit(solution)/shard_map/all_gather | solution.py:127
  75.5 2.5 %all_gather.22.up_arrived = f32[384,640]{1,0:T(8,128)S(1)} all-gather(f32[192,640]{1,0:T(8,128)S(1)} %get-tuple-element.26), channel_id=1, replica_groups={{0,24},{48,72},{96,120},{144,168},{192,216},{240,264},{288,312},{336,36..., dimensions={0}, use_global_device_ids=true | all-gather | bytes 1474560 | tf_op jit(solution)/shard_map/all_gather | solution.py:127
  78.0 1.2 %collective-permute-done.9.refs_3_ = bf16[128,1280]{1,0:T(8,128)(2,1)S(1)} collective-permute-done((bf16[128,1280]{1,0:T(8,128)(2,1)S(1)}, bf16[128,1280]{1,0:T(8,128)(2,1)S(1)}, u32[]{:S(2)}, u32[]{:S(2)}) %collective-permute-start.9) | collective-permute-done | bytes 327712 | tf_op jit(solution)/shard_map/ppermute | solution.py:120
  79.2 1.2 %shard_map.51 = (f32[192,1280]{1,0:T(8,128)S(1)}, bf16[192,1280]{1,0:T(8,128)(2,1)S(1)}) custom-call(bf16[192,4096]{1,0:T(8,128)(2,1)S(1)} %copy-done.1, bf16[384,4096]{1,0:T(8,128)(2,1)S(1)} %copy-done, f32[192,1280]{1,0:T(8,128)S(1)} %get-tuple-element.22.total_before, bf16[128,1280]{1,0:T(8,128)(2,1)S(1)} %collective-permute-done.5.refs_0_, ...), custom_call_target="tpu_custom_call" | custom-call | flops 503316480 | bytes 5242880 | tf_op jit(solution)/shard_map/pallas_call | solution.py:99
  80.4 6.6 %all_gather.23.late = bf16[384,1280]{1,0:T(8,128)(2,1)S(1)} all-gather(bf16[192,1280]{1,0:T(8,128)(2,1)S(1)} %get-tuple-element.27), channel_id=1, replica_groups={{0,24},{48,72},{96,120},{144,168},{192,216},{240,264},{288,312},{336,36..., dimensions={0}, use_global_device_ids=true | all-gather | bytes 1474560 | tf_op jit(solution)/shard_map/all_gather | solution.py:127
  (21 shorter events, 5.0 us)
Async XLA Ops:
  6.5 46.4 %copy-start.1 = (bf16[192,4096]{1,0:T(8,128)(2,1)S(1)}, bf16[192,4096]{1,0:T(8,128)(2,1)}, u32[]{:S(2)}) copy-start(bf16[192,4096]{1,0:T(8,128)(2,1)} %tokens.5) | copy-start | bytes 4718596
  6.5 46.4 %all-gather.2.cloned.1.call-start = ((), (), s32[]{:S(2)}) async-start(), calls=%async_computation | async-start | bytes 4718592 | tf_op jit(solution)/shard_map/all_gather | solution.py:127
  8.4 16.3 %collective-permute-start = (bf16[128,1280]{1,0:T(8,128)(2,1)S(1)}, bf16[128,1280]{1,0:T(8,128)(2,1)S(1)}, u32[]{:S(2)}, u32[]{:S(2)}) collective-permute-start(bf16[128,1280]{1,0:T(8,128)(2,1)S(1)} %pad_maximum_fusion.refs_0_), channel_id=1, source_target_pairs={{0,48},{24,72},{48,0},{72,24},{96,144},{120,168},{144,96},{168,120... | collective-permute-start | bytes 983048 | tf_op jit(solution)/shard_map/ppermute | solution.py:120
  22.8 11.6 %collective-permute-start.3 = (bf16[256,1280]{1,0:T(8,128)(2,1)S(1)}, bf16[256,1280]{1,0:T(8,128)(2,1)S(1)}, u32[]{:S(2)}, u32[]{:S(2)}) collective-permute-start(bf16[256,1280]{1,0:T(8,128)(2,1)S(1)} %all_gather.20), channel_id=1, source_target_pairs={{0,96},{24,696},{48,144},{72,744},{96,192},{120,24},{144,240},{168... | collective-permute-start | bytes 1966088 | tf_op jit(solution)/shard_map/ppermute | solution.py:120
  31.3 11.7 %collective-permute-start.1 = (bf16[256,1280]{1,0:T(8,128)(2,1)S(1)}, bf16[256,1280]{1,0:T(8,128)(2,1)}, u32[]{:S(2)}, u32[]{:S(2)}) collective-permute-start(bf16[256,1280]{1,0:T(8,128)(2,1)S(1)} %all_gather.19), channel_id=1, source_target_pairs={{0,96},{24,696},{48,144},{72,744},{96,192},{120,24},{144,240},{168... | collective-permute-start | bytes 1966088 | tf_op jit(solution)/shard_map/ppermute | solution.py:120
  34.4 15.7 %collective-permute-start.4 = (bf16[256,1280]{1,0:T(8,128)(2,1)S(1)}, bf16[256,1280]{1,0:T(8,128)(2,1)}, u32[]{:S(2)}, u32[]{:S(2)}) collective-permute-start(bf16[256,1280]{1,0:T(8,128)(2,1)S(1)} %collective-permute-done.3.refs_1_), channel_id=1, source_target_pairs={{0,96},{24,696},{48,144},{72,744},{96,192},{120,24},{144,240},{168... | collective-permute-start | bytes 1966088 | tf_op jit(solution)/shard_map/ppermute | solution.py:120
  37.2 0.8 copy-start.2
  43.0 15.6 %collective-permute-start.2 = (bf16[256,1280]{1,0:T(8,128)(2,1)}, bf16[256,1280]{1,0:T(8,128)(2,1)S(1)}, u32[]{:S(2)}, u32[]{:S(2)}) collective-permute-start(bf16[256,1280]{1,0:T(8,128)(2,1)} %collective-permute-done.1.refs_2_), channel_id=1, source_target_pairs={{0,96},{24,696},{48,144},{72,744},{96,192},{120,24},{144,240},{168... | collective-permute-start | bytes 1966088 | tf_op jit(solution)/shard_map/ppermute | solution.py:120
  50.1 13.9 %collective-permute-start.6 = (bf16[256,1280]{1,0:T(8,128)(2,1)}, bf16[256,1280]{1,0:T(8,128)(2,1)S(1)}, u32[]{:S(2)}, u32[]{:S(2)}) collective-permute-start(bf16[256,1280]{1,0:T(8,128)(2,1)} %collective-permute-done.4.refs_3_), channel_id=1, source_target_pairs={{0,96},{24,696},{48,144},{72,744},{96,192},{120,24},{144,240},{168... | collective-permute-start | bytes 1966088 | tf_op jit(solution)/shard_map/ppermute | solution.py:120
  52.9 1.9 %copy-start = (bf16[384,4096]{1,0:T(8,128)(2,1)S(1)}, bf16[384,4096]{1,0:T(8,128)(2,1)}, u32[]{:S(2)}) copy-start(bf16[384,4096]{1,0:T(8,128)(2,1)} %all-gather.2.cloned.1.call-done.others) | copy-start | bytes 9437188
  54.8 1.1 %copy-start.3 = (bf16[256,1280]{1,0:T(8,128)(2,1)S(1)}, bf16[256,1280]{1,0:T(8,128)(2,1)}, u32[]{:S(2)}) copy-start(bf16[256,1280]{1,0:T(8,128)(2,1)} %copy-done.2) | copy-start | bytes 1966084
  58.7 11.2 %collective-permute-start.5 = (bf16[128,1280]{1,0:T(8,128)(2,1)S(1)}, bf16[128,1280]{1,0:T(8,128)(2,1)S(1)}, u32[]{:S(2)}, u32[]{:S(2)}) collective-permute-start(bf16[128,1280]{1,0:T(8,128)(2,1)S(1)} %shard_map.47), channel_id=1, source_target_pairs={{0,96},{24,696},{48,144},{72,744},{96,192},{120,24},{144,240},{168... | collective-permute-start | bytes 983048 | tf_op jit(solution)/shard_map/ppermute | solution.py:120
  64.1 13.9 %collective-permute-start.8 = (bf16[128,1280]{1,0:T(8,128)(2,1)S(1)}, bf16[128,1280]{1,0:T(8,128)(2,1)S(1)}, u32[]{:S(2)}, u32[]{:S(2)}) collective-permute-start(bf16[128,1280]{1,0:T(8,128)(2,1)S(1)} %shard_map.50), channel_id=1, source_target_pairs={{0,96},{24,696},{48,144},{72,744},{96,192},{120,24},{144,240},{168... | collective-permute-start | bytes 983048 | tf_op jit(solution)/shard_map/ppermute | solution.py:120
  67.1 11.0 %collective-permute-start.7 = (bf16[128,1280]{1,0:T(8,128)(2,1)S(1)}, bf16[128,1280]{1,0:T(8,128)(2,1)S(1)}, u32[]{:S(2)}, u32[]{:S(2)}) collective-permute-start(bf16[128,1280]{1,0:T(8,128)(2,1)S(1)} %shard_map.49), channel_id=1, source_target_pairs={{0,96},{24,696},{48,144},{72,744},{96,192},{120,24},{144,240},{168... | collective-permute-start | bytes 983048 | tf_op jit(solution)/shard_map/ppermute | solution.py:120
  70.0 9.3 %collective-permute-start.9 = (bf16[128,1280]{1,0:T(8,128)(2,1)S(1)}, bf16[128,1280]{1,0:T(8,128)(2,1)S(1)}, u32[]{:S(2)}, u32[]{:S(2)}) collective-permute-start(bf16[128,1280]{1,0:T(8,128)(2,1)S(1)} %collective-permute-done.5.refs_0_), channel_id=1, source_target_pairs={{0,96},{24,696},{48,144},{72,744},{96,192},{120,24},{144,240},{168... | collective-permute-start | bytes 983048 | tf_op jit(solution)/shard_map/ppermute | solution.py:120
Sparse Core Ops, SparseCore 0:
  9.7 32.7 all-gather.1

commit v9 on v7

--- a/solution.py
+++ b/solution.py
@@ -48,19 +48,33 @@
     up[...] = partial[:, wide:]
 
 
-def third_kernel(add, n, tokens, others, total_before, *refs):
+def their_rows(rows):
+    return pl.ds(pl.multiple_of((1 - lax.rem(lax.axis_index("fsdp"), 2)) * rows, rows), rows)
+
+
+def third_kernel(add, n, tokens, others, total_before, gate_arrived, up_arrived, *refs):
+    blocks, (total, partial) = refs[:n], refs[n:]
+    wide = gate_arrived.shape[1]
+    theirs = their_rows(total.shape[0])
+    total[:, :wide] = total_before[:, :wide] + gate_arrived[theirs, :]
+    total[:, wide:] = total_before[:, wide:] + up_arrived[theirs, :]
+    partial[...] = jnp.zeros_like(partial)
+    add(blocks, [(tokens, total), (others, partial)])
+
+
+def fourth_kernel(add, n, tokens, others, total_before, partial_before, *refs):
     blocks, (total, leaving, partial) = refs[:n], refs[n:]
     total[...] = total_before[...]
-    partial[...] = jnp.zeros_like(partial)
+    partial[...] = partial_before[...]
     add(blocks, [(tokens, total), (others, partial)])
     leaving[...] = partial[...].astype(leaving.dtype)
 
 
-def last_kernel(add, n, total, gate_arrived, up_arrived, late, scale, hidden):
+def last_kernel(add, n, total, late, scale, hidden):
     rows, wide = hidden.shape
-    theirs = pl.ds(pl.multiple_of((1 - lax.rem(lax.axis_index("fsdp"), 2)) * rows, rows), rows)
-    gate = (total[:, :wide] + gate_arrived[theirs, :] + late[theirs, :wide].astype(jnp.float32)) * scale[...]
-    up = (total[:, wide:] + up_arrived[theirs, :] + late[theirs, wide:].astype(jnp.float32)) * scale[...]
+    theirs = their_rows(rows)
+    gate = (total[:, :wide] + late[theirs, :wide].astype(jnp.float32)) * scale[...]
+    up = (total[:, wide:] + late[theirs, wide:].astype(jnp.float32)) * scale[...]
     hidden[...] = (gate / (1.0 + jnp.exp(-gate)) * up).astype(hidden.dtype)
 
 
@@ -126,14 +140,13 @@
         own = jnp.concatenate([gate_weight * gain, up_weight * gain], axis=1).astype(jnp.bfloat16)
         wide = own.shape[1]
         b0 = across(own)
-        chip = join(own)
+        chip, late = lax.optimization_barrier((join(own), tokens))
         rows = tokens.shape[0]
         sums = jax.ShapeDtypeStruct((rows, wide), jnp.float32)
         step = functools.partial(call, high=high, sum_width=wide)
 
         a1 = along(chip)
-        beside, late = lax.optimization_barrier((join(b0), tokens))
-        b1 = along(beside)
+        b1 = along(join(b0))
         others = swap(late)
         a2 = along(a1)
         b2 = along(b1)
@@ -160,18 +173,26 @@
         )
         b3, total = lax.optimization_barrier((b3, total))
         b4 = along(b3)
+        total, partial = step(
+            third_kernel,
+            specs=[(3, 1, 1), (3, 1, 2), (4, 0, 1)],
+            arrays=[tokens, others, total, join(gate), join(up)],
+            blocks=[b3, b3_rest, a4],
+            out_shape=(sums, sums),
+        )
+        b4, total = lax.optimization_barrier((b4, total))
         total, late = step(
-            third_kernel,
-            specs=[(3, 1, 1), (3, 1, 2), (4, 0, 1), (4, 1, 1)],
-            arrays=[tokens, others, total],
-            blocks=[b3, b3_rest, a4, b4],
+            fourth_kernel,
+            specs=[(4, 1, 1)],
+            arrays=[tokens, others, total, partial],
+            blocks=[b4],
             out_shape=(sums, jax.ShapeDtypeStruct((rows, wide), jnp.bfloat16)),
             scratch=[pltpu.VMEM((rows, wide), jnp.float32)],
         )
         return step(
             last_kernel,
             specs=[],
-            arrays=[total, join(gate), join(up), join(late), scale],
+            arrays=[total, join(late), scale],
             blocks=[],
             out_shape=jax.ShapeDtypeStruct((rows, wide // 2), jnp.bfloat16),
         )

time: 80.1 us -> 80.6 us (level)
  starting transfers between devices: 29.2 us -> 39.2 us
  waiting for transfers between devices: 18.5 us -> 11.2 us
  blocking collectives: 25.7 us -> 23.4 us
    ppermute x11, starting transfers between devices: 29.2 us -> 39.2 us  [move(): return lambda v: lax.ppermute(v, 'fsdp', pairs)]
    ppermute x11, waiting for transfers between devices: 18.5 us -> 11.2 us  [move(): return lambda v: lax.ppermute(v, 'fsdp', pairs)]
    all_gather x5, blocking collectives: 25.7 us -> 23.4 us  [join(): lax.all_gather(v, 'fsdp', axis=0, tiled=True, axis_index_groups=core_pairs)]
    pallas_call x4 -> x5, Pallas kernels: 4.46 us -> 4.6 us  [call(): pl.pallas_call(functools.partial(kernel, functools.partial(add_blocks, sp...]
  transfers between devices with their start and end apart: 11 -> 11, of which waited for: 5 -> 5; matrix products, arithmetic and copies ran while one was open for 0% -> 0% of each run, Pallas kernels for 3% -> 4%
where the time goes in v9:
time: 80.6 us; the launch traced here: 80.1 us
  starting transfers between devices  39.2 us (49%)
  blocking collectives  23.4 us (29%)
  waiting for transfers between devices  11.2 us (14%)
  Pallas kernels  4.95 us (6%)
  other arithmetic  1.28 us (2%)
    ppermute x11, starting transfers between devices, move(): return lambda v: lax.ppermute(v, 'fsdp', pairs)  39.2 us
    all_gather x5, blocking collectives, join(): lax.all_gather(v, 'fsdp', axis=0, tiled=True, axis_index_groups=core_pairs)  23.4 us
    ppermute x11, waiting for transfers between devices, move(): return lambda v: lax.ppermute(v, 'fsdp', pairs)  11.2 us
    pallas_call x5, Pallas kernels, call(): pl.pallas_call(functools.partial(kernel, functools.partial(add_blocks, sp...  4.6 us
  transfers between devices with their start and end apart: 11, of which 5 were waited for; matrix products, arithmetic and copies ran while one was open for 0% of the time, Pallas kernels for 4%

profile of v9, /device:TPU:1, one launch (start us, length us, event | category | flops | bytes accessed | tf_op | source)
XLA Modules:
  0.0 80.1 jit_solution(12836546895125954737)
XLA Ops:
  0.0 1.3 %multiply_convert_fusion.1 = (bf16[128,640]{1,0:T(8,128)(2,1)S(1)}, bf16[128,640]{1,0:T(8,128)(2,1)S(1)}) fusion(bf16[128,640]{1,0:T(8,128)(2,1)} %param.6, f32[128]{0:T(128)} %param.5, bf16[128,640]{1,0:T(8,128)(2,1)} %param.7), kind=kLoop, calls=%fused_computation.2 | loop fusion | flops 491520 | bytes 655872 | tf_op jit(solution)/shard_map/convert
  1.3 5.5 %collective-permute-start.1 = (bf16[128,1280]{1,0:T(8,128)(2,1)S(1)}, bf16[128,1280]{1,0:T(8,128)(2,1)S(1)}, u32[]{:S(2)}, u32[]{:S(2)}) collective-permute-start(bf16[128,1280]{1,0:T(8,128)(2,1)S(1)} %pad_maximum_fusion.refs_0_), channel_id=1, source_target_pairs={{0,48},{24,72},{48,0},{72,24},{96,144},{120,168},{144,96},{168,120... | collective-permute-start | bytes 983048 | tf_op jit(solution)/shard_map/ppermute | solution.py:128
  6.8 8.9 %all_gather.15 = bf16[256,1280]{1,0:T(8,128)(2,1)S(1)} all-gather(bf16[128,1280]{1,0:T(8,128)(2,1)S(1)} %pad_maximum_fusion.refs_0_), channel_id=1, replica_groups={{0,24},{48,72},{96,120},{144,168},{192,216},{240,264},{288,312},{336,36..., dimensions={0}, use_global_device_ids=true | all-gather | bytes 983040 | tf_op jit(solution)/shard_map/all_gather | solution.py:136
  15.6 1.9 %collective-permute-start.4 = (bf16[256,1280]{1,0:T(8,128)(2,1)S(1)}, bf16[256,1280]{1,0:T(8,128)(2,1)S(1)}, u32[]{:S(2)}, u32[]{:S(2)}) collective-permute-start(bf16[256,1280]{1,0:T(8,128)(2,1)S(1)} %all_gather.15), channel_id=1, source_target_pairs={{0,96},{24,696},{48,144},{72,744},{96,192},{120,24},{144,240},{168... | collective-permute-start | bytes 1966088 | tf_op jit(solution)/shard_map/ppermute | solution.py:128
  17.6 2.3 %collective-permute-start = (bf16[192,4096]{1,0:T(8,128)(2,1)S(1)}, bf16[192,4096]{1,0:T(8,128)(2,1)S(1)}, u32[]{:S(2)}, u32[]{:S(2)}) collective-permute-start(bf16[192,4096]{1,0:T(8,128)(2,1)S(1)} %copy-done), channel_id=1, source_target_pairs={{0,24},{24,0},{48,72},{72,48},{96,120},{120,96},{144,168},{168,144... | collective-permute-start | bytes 4718600 | tf_op jit(solution)/shard_map/ppermute | solution.py:128
  19.9 4.3 %all_gather.16 = bf16[256,1280]{1,0:T(8,128)(2,1)S(1)} all-gather(bf16[128,1280]{1,0:T(8,128)(2,1)S(1)} %collective-permute-done.1.refs_0_), channel_id=1, replica_groups={{0,24},{48,72},{96,120},{144,168},{192,216},{240,264},{288,312},{336,36..., dimensions={0}, use_global_device_ids=true | all-gather | bytes 983040 | tf_op jit(solution)/shard_map/all_gather | solution.py:136
  24.2 4.0 %collective-permute-start.2 = (bf16[256,1280]{1,0:T(8,128)(2,1)S(1)}, bf16[256,1280]{1,0:T(8,128)(2,1)S(1)}, u32[]{:S(2)}, u32[]{:S(2)}) collective-permute-start(bf16[256,1280]{1,0:T(8,128)(2,1)S(1)} %all_gather.16), channel_id=1, source_target_pairs={{0,96},{24,696},{48,144},{72,744},{96,192},{120,24},{144,240},{168... | collective-permute-start | bytes 1966088 | tf_op jit(solution)/shard_map/ppermute | solution.py:128
  28.2 1.9 %collective-permute-start.5 = (bf16[256,1280]{1,0:T(8,128)(2,1)S(1)}, bf16[256,1280]{1,0:T(8,128)(2,1)S(1)}, u32[]{:S(2)}, u32[]{:S(2)}) collective-permute-start(bf16[256,1280]{1,0:T(8,128)(2,1)S(1)} %collective-permute-done.4.refs_1_), channel_id=1, source_target_pairs={{0,96},{24,696},{48,144},{72,744},{96,192},{120,24},{144,240},{168... | collective-permute-start | bytes 1966088 | tf_op jit(solution)/shard_map/ppermute | solution.py:128
  30.1 5.7 %collective-permute-done.2.refs_2_ = bf16[256,1280]{1,0:T(8,128)(2,1)S(1)} collective-permute-done((bf16[256,1280]{1,0:T(8,128)(2,1)S(1)}, bf16[256,1280]{1,0:T(8,128)(2,1)S(1)}, u32[]{:S(2)}, u32[]{:S(2)}) %collective-permute-start.2) | collective-permute-done | bytes 655392 | tf_op jit(solution)/shard_map/ppermute | solution.py:128
  35.8 4.9 %collective-permute-start.3 = (bf16[256,1280]{1,0:T(8,128)(2,1)S(1)}, bf16[256,1280]{1,0:T(8,128)(2,1)S(1)}, u32[]{:S(2)}, u32[]{:S(2)}) collective-permute-start(bf16[256,1280]{1,0:T(8,128)(2,1)S(1)} %collective-permute-done.2.refs_2_), channel_id=1, source_target_pairs={{0,96},{24,696},{48,144},{72,744},{96,192},{120,24},{144,240},{168... | collective-permute-start | bytes 1966088 | tf_op jit(solution)/shard_map/ppermute | solution.py:128
  40.7 2.1 %collective-permute-done.5.refs_3_ = bf16[256,1280]{1,0:T(8,128)(2,1)S(1)} collective-permute-done((bf16[256,1280]{1,0:T(8,128)(2,1)S(1)}, bf16[256,1280]{1,0:T(8,128)(2,1)S(1)}, u32[]{:S(2)}, u32[]{:S(2)}) %collective-permute-start.5) | collective-permute-done | bytes 655392 | tf_op jit(solution)/shard_map/ppermute | solution.py:128
  42.8 4.9 %collective-permute-start.7 = (bf16[256,1280]{1,0:T(8,128)(2,1)S(1)}, bf16[256,1280]{1,0:T(8,128)(2,1)S(1)}, u32[]{:S(2)}, u32[]{:S(2)}) collective-permute-start(bf16[256,1280]{1,0:T(8,128)(2,1)S(1)} %collective-permute-done.5.refs_3_), channel_id=1, source_target_pairs={{0,96},{24,696},{48,144},{72,744},{96,192},{120,24},{144,240},{168... | collective-permute-start | bytes 1966088 | tf_op jit(solution)/shard_map/ppermute | solution.py:128
  47.8 1.4 %shard_map.46 = (f32[192,1280]{1,0:T(8,128)S(1)}, f32[192,1280]{1,0:T(8,128)S(1)}, f32[192,1]{1,0:T(8,128)S(1)}) custom-call(bf16[192,4096]{1,0:T(8,128)(2,1)S(1)} %copy-done, bf16[192,4096]{1,0:T(8,128)(2,1)S(1)} %collective-permute-done.others, bf16[128,1280]{1,0:T(8,128)(2,1)S(1)} %pad_maximum_fusion.refs_0_, ...), custom_call_target="tpu_custom_call" | custom-call | flops 880803840 | bytes 6225920 | tf_op jit(solution)/shard_map/pallas_call | solution.py:107
  49.9 4.9 %collective-permute-start.6 = (bf16[128,1280]{1,0:T(8,128)(2,1)S(1)}, bf16[128,1280]{1,0:T(8,128)(2,1)S(1)}, u32[]{:S(2)}, u32[]{:S(2)}) collective-permute-start(bf16[128,1280]{1,0:T(8,128)(2,1)S(1)} %shard_map.47), channel_id=1, source_target_pairs={{0,96},{24,696},{48,144},{72,744},{96,192},{120,24},{144,240},{168... | collective-permute-start | bytes 983048 | tf_op jit(solution)/shard_map/ppermute | solution.py:128
  55.0 1.9 %collective-permute-start.9 = (bf16[128,1280]{1,0:T(8,128)(2,1)S(1)}, bf16[128,1280]{1,0:T(8,128)(2,1)S(1)}, u32[]{:S(2)}, u32[]{:S(2)}) collective-permute-start(bf16[128,1280]{1,0:T(8,128)(2,1)S(1)} %shard_map.49), channel_id=1, source_target_pairs={{0,96},{24,696},{48,144},{72,744},{96,192},{120,24},{144,240},{168... | collective-permute-start | bytes 983048 | tf_op jit(solution)/shard_map/ppermute | solution.py:128
  57.0 0.9 %shard_map.48 = (f32[192,1280]{1,0:T(8,128)S(1)}, f32[192,640]{1,0:T(8,128)S(1)}, f32[192,640]{1,0:T(8,128)S(1)}) custom-call(bf16[192,4096]{1,0:T(8,128)(2,1)S(1)} %copy-done, bf16[192,4096]{1,0:T(8,128)(2,1)S(1)} %collective-permute-done.others, f32[192,1280]{1,0:T(8,128)S(1)} %get-tuple-element.27.total_before, ...), custom_call_target="tpu_custom_call" | custom-call | flops 629145600 | bytes 5570560 | tf_op jit(solution)/shard_map/pallas_call | solution.py:107
  57.9 2.5 %collective-permute-done.6.refs_0_ = bf16[128,1280]{1,0:T(8,128)(2,1)S(1)} collective-permute-done((bf16[128,1280]{1,0:T(8,128)(2,1)S(1)}, bf16[128,1280]{1,0:T(8,128)(2,1)S(1)}, u32[]{:S(2)}, u32[]{:S(2)}) %collective-permute-start.6) | collective-permute-done | bytes 327712 | tf_op jit(solution)/shard_map/ppermute | solution.py:128
  60.5 4.9 %collective-permute-start.10 = (bf16[128,1280]{1,0:T(8,128)(2,1)S(1)}, bf16[128,1280]{1,0:T(8,128)(2,1)S(1)}, u32[]{:S(2)}, u32[]{:S(2)}) collective-permute-start(bf16[128,1280]{1,0:T(8,128)(2,1)S(1)} %shard_map.50), channel_id=1, source_target_pairs={{0,96},{24,696},{48,144},{72,744},{96,192},{120,24},{144,240},{168... | collective-permute-start | bytes 983048 | tf_op jit(solution)/shard_map/ppermute | solution.py:128
  65.4 1.9 %collective-permute-start.8 = (bf16[128,1280]{1,0:T(8,128)(2,1)S(1)}, bf16[128,1280]{1,0:T(8,128)(2,1)S(1)}, u32[]{:S(2)}, u32[]{:S(2)}) collective-permute-start(bf16[128,1280]{1,0:T(8,128)(2,1)S(1)} %collective-permute-done.6.refs_0_), channel_id=1, source_target_pairs={{0,96},{24,696},{48,144},{72,744},{96,192},{120,24},{144,240},{168... | collective-permute-start | bytes 983048 | tf_op jit(solution)/shard_map/ppermute | solution.py:128
  67.4 2.5 %all_gather.17.gate_arrived = f32[384,640]{1,0:T(8,128)S(1)} all-gather(f32[192,640]{1,0:T(8,128)S(1)} %get-tuple-element.32), channel_id=1, replica_groups={{0,24},{48,72},{96,120},{144,168},{192,216},{240,264},{288,312},{336,36..., dimensions={0}, use_global_device_ids=true | all-gather | bytes 1474560 | tf_op jit(solution)/shard_map/all_gather | solution.py:136
  69.9 2.5 %all_gather.18.up_arrived = f32[384,640]{1,0:T(8,128)S(1)} all-gather(f32[192,640]{1,0:T(8,128)S(1)} %get-tuple-element.33), channel_id=1, replica_groups={{0,24},{48,72},{96,120},{144,168},{192,216},{240,264},{288,312},{336,36..., dimensions={0}, use_global_device_ids=true | all-gather | bytes 1474560 | tf_op jit(solution)/shard_map/all_gather | solution.py:136
  72.4 0.9 %shard_map.51 = (f32[192,1280]{1,0:T(8,128)S(1)}, f32[192,1280]{1,0:T(8,128)S(1)}) custom-call(bf16[192,4096]{1,0:T(8,128)(2,1)S(1)} %copy-done, bf16[192,4096]{1,0:T(8,128)(2,1)S(1)} %collective-permute-done.others, f32[192,1280]{1,0:T(8,128)S(1)} %get-tuple-element.31.total_before, f32[384,640]{1,0:T(8,128)S(1)} %all_gather.17.gate_arrived, ...), custom_call_target="tpu_custom_call" | custom-call | flops 377487360 | bytes 4915200 | tf_op jit(solution)/shard_map/pallas_call | solution.py:107
  73.9 5.2 %all_gather.19.late = bf16[384,1280]{1,0:T(8,128)(2,1)S(1)} all-gather(bf16[192,1280]{1,0:T(8,128)(2,1)S(1)} %get-tuple-element.39), channel_id=1, replica_groups={{0,24},{48,72},{96,120},{144,168},{192,216},{240,264},{288,312},{336,36..., dimensions={0}, use_global_device_ids=true | all-gather | bytes 1474560 | tf_op jit(solution)/shard_map/all_gather | solution.py:136
  79.2 1.0 %shard_map.53 = bf16[192,640]{1,0:T(8,128)(2,1)} custom-call(f32[192,1280]{1,0:T(8,128)S(1)} %get-tuple-element.38.total, bf16[384,1280]{1,0:T(8,128)(2,1)S(1)} %all_gather.19.late, f32[192,1]{1,0:T(8,128)S(1)} %get-tuple-element.40.scale), custom_call_target="tpu_custom_call" | custom-call | bytes 3932160 | tf_op jit(solution)/shard_map/pallas_call | solution.py:107
  (15 shorter events, 1.7 us)
Async XLA Ops:
  0.0 17.6 %copy-start = (bf16[192,4096]{1,0:T(8,128)(2,1)S(1)}, bf16[192,4096]{1,0:T(8,128)(2,1)}, u32[]{:S(2)}) copy-start(bf16[192,4096]{1,0:T(8,128)(2,1)} %tokens.7) | copy-start | bytes 4718596
  1.3 18.6 %collective-permute-start.1 = (bf16[128,1280]{1,0:T(8,128)(2,1)S(1)}, bf16[128,1280]{1,0:T(8,128)(2,1)S(1)}, u32[]{:S(2)}, u32[]{:S(2)}) collective-permute-start(bf16[128,1280]{1,0:T(8,128)(2,1)S(1)} %pad_maximum_fusion.refs_0_), channel_id=1, source_target_pairs={{0,48},{24,72},{48,0},{72,24},{96,144},{120,168},{144,96},{168,120... | collective-permute-start | bytes 983048 | tf_op jit(solution)/shard_map/ppermute | solution.py:128
  15.6 12.6 %collective-permute-start.4 = (bf16[256,1280]{1,0:T(8,128)(2,1)S(1)}, bf16[256,1280]{1,0:T(8,128)(2,1)S(1)}, u32[]{:S(2)}, u32[]{:S(2)}) collective-permute-start(bf16[256,1280]{1,0:T(8,128)(2,1)S(1)} %all_gather.15), channel_id=1, source_target_pairs={{0,96},{24,696},{48,144},{72,744},{96,192},{120,24},{144,240},{168... | collective-permute-start | bytes 1966088 | tf_op jit(solution)/shard_map/ppermute | solution.py:128
  17.6 30.2 %collective-permute-start = (bf16[192,4096]{1,0:T(8,128)(2,1)S(1)}, bf16[192,4096]{1,0:T(8,128)(2,1)S(1)}, u32[]{:S(2)}, u32[]{:S(2)}) collective-permute-start(bf16[192,4096]{1,0:T(8,128)(2,1)S(1)} %copy-done), channel_id=1, source_target_pairs={{0,24},{24,0},{48,72},{72,48},{96,120},{120,96},{144,168},{168,144... | collective-permute-start | bytes 4718600 | tf_op jit(solution)/shard_map/ppermute | solution.py:128
  24.2 11.6 %collective-permute-start.2 = (bf16[256,1280]{1,0:T(8,128)(2,1)S(1)}, bf16[256,1280]{1,0:T(8,128)(2,1)S(1)}, u32[]{:S(2)}, u32[]{:S(2)}) collective-permute-start(bf16[256,1280]{1,0:T(8,128)(2,1)S(1)} %all_gather.16), channel_id=1, source_target_pairs={{0,96},{24,696},{48,144},{72,744},{96,192},{120,24},{144,240},{168... | collective-permute-start | bytes 1966088 | tf_op jit(solution)/shard_map/ppermute | solution.py:128
  28.2 14.6 %collective-permute-start.5 = (bf16[256,1280]{1,0:T(8,128)(2,1)S(1)}, bf16[256,1280]{1,0:T(8,128)(2,1)S(1)}, u32[]{:S(2)}, u32[]{:S(2)}) collective-permute-start(bf16[256,1280]{1,0:T(8,128)(2,1)S(1)} %collective-permute-done.4.refs_1_), channel_id=1, source_target_pairs={{0,96},{24,696},{48,144},{72,744},{96,192},{120,24},{144,240},{168... | collective-permute-start | bytes 1966088 | tf_op jit(solution)/shard_map/ppermute | solution.py:128
  35.8 14.0 %collective-permute-start.3 = (bf16[256,1280]{1,0:T(8,128)(2,1)S(1)}, bf16[256,1280]{1,0:T(8,128)(2,1)S(1)}, u32[]{:S(2)}, u32[]{:S(2)}) collective-permute-start(bf16[256,1280]{1,0:T(8,128)(2,1)S(1)} %collective-permute-done.2.refs_2_), channel_id=1, source_target_pairs={{0,96},{24,696},{48,144},{72,744},{96,192},{120,24},{144,240},{168... | collective-permute-start | bytes 1966088 | tf_op jit(solution)/shard_map/ppermute | solution.py:128
  42.8 14.2 %collective-permute-start.7 = (bf16[256,1280]{1,0:T(8,128)(2,1)S(1)}, bf16[256,1280]{1,0:T(8,128)(2,1)S(1)}, u32[]{:S(2)}, u32[]{:S(2)}) collective-permute-start(bf16[256,1280]{1,0:T(8,128)(2,1)S(1)} %collective-permute-done.5.refs_3_), channel_id=1, source_target_pairs={{0,96},{24,696},{48,144},{72,744},{96,192},{120,24},{144,240},{168... | collective-permute-start | bytes 1966088 | tf_op jit(solution)/shard_map/ppermute | solution.py:128
  49.9 10.4 %collective-permute-start.6 = (bf16[128,1280]{1,0:T(8,128)(2,1)S(1)}, bf16[128,1280]{1,0:T(8,128)(2,1)S(1)}, u32[]{:S(2)}, u32[]{:S(2)}) collective-permute-start(bf16[128,1280]{1,0:T(8,128)(2,1)S(1)} %shard_map.47), channel_id=1, source_target_pairs={{0,96},{24,696},{48,144},{72,744},{96,192},{120,24},{144,240},{168... | collective-permute-start | bytes 983048 | tf_op jit(solution)/shard_map/ppermute | solution.py:128
  55.0 17.3 %collective-permute-start.9 = (bf16[128,1280]{1,0:T(8,128)(2,1)S(1)}, bf16[128,1280]{1,0:T(8,128)(2,1)S(1)}, u32[]{:S(2)}, u32[]{:S(2)}) collective-permute-start(bf16[128,1280]{1,0:T(8,128)(2,1)S(1)} %shard_map.49), channel_id=1, source_target_pairs={{0,96},{24,696},{48,144},{72,744},{96,192},{120,24},{144,240},{168... | collective-permute-start | bytes 983048 | tf_op jit(solution)/shard_map/ppermute | solution.py:128
  60.5 11.9 %collective-permute-start.10 = (bf16[128,1280]{1,0:T(8,128)(2,1)S(1)}, bf16[128,1280]{1,0:T(8,128)(2,1)S(1)}, u32[]{:S(2)}, u32[]{:S(2)}) collective-permute-start(bf16[128,1280]{1,0:T(8,128)(2,1)S(1)} %shard_map.50), channel_id=1, source_target_pairs={{0,96},{24,696},{48,144},{72,744},{96,192},{120,24},{144,240},{168... | collective-permute-start | bytes 983048 | tf_op jit(solution)/shard_map/ppermute | solution.py:128
  65.4 8.1 %collective-permute-start.8 = (bf16[128,1280]{1,0:T(8,128)(2,1)S(1)}, bf16[128,1280]{1,0:T(8,128)(2,1)S(1)}, u32[]{:S(2)}, u32[]{:S(2)}) collective-permute-start(bf16[128,1280]{1,0:T(8,128)(2,1)S(1)} %collective-permute-done.6.refs_0_), channel_id=1, source_target_pairs={{0,96},{24,696},{48,144},{72,744},{96,192},{120,24},{144,240},{168... | collective-permute-start | bytes 983048 | tf_op jit(solution)/shard_map/ppermute | solution.py:128

commit v10 on v9

--- a/solution.py
+++ b/solution.py
@@ -150,7 +150,8 @@
         others = swap(late)
         a2 = along(a1)
         b2 = along(b1)
-        a3 = along(a2)
+        a3 = along(cut(a2))
+        a3_rest = along(cut(a2, 1))
         total, partial, scale = step(
             first_kernel,
             specs=[(0, 0, 1), (1, 0, 0), (1, 1, 0), (2, 0, 0)],
@@ -161,13 +162,13 @@
         b2, total = lax.optimization_barrier((b2, total))
         b3 = along(cut(b2))
         b3_rest = along(cut(b2, 1))
-        a4 = along(cut(a3))
+        a4 = along(a3)
         narrow = jax.ShapeDtypeStruct((rows, wide // 2), jnp.float32)
         total, gate, up = step(
             second_kernel,
-            specs=[(0, 1, 1), (2, 1, 0), (3, 0, 0)],
+            specs=[(0, 1, 1), (2, 1, 0), (3, 0, 1), (3, 0, 2)],
             arrays=[tokens, others, total, partial],
-            blocks=[b0, b2, a3],
+            blocks=[b0, b2, a3, a3_rest],
             out_shape=(sums, narrow, narrow),
             scratch=[pltpu.VMEM((rows, wide), jnp.float32)],
         )

time: 80.6 us -> 77.9 us (0.967)
  starting transfers between devices: 39.2 us -> 32.1 us
  waiting for transfers between devices: 11.2 us -> 15 us
    ppermute x11 -> x12, starting transfers between devices: 39.2 us -> 32.1 us  [move(): return lambda v: lax.ppermute(v, 'fsdp', pairs)]
    ppermute x11 -> x12, waiting for transfers between devices: 11.2 us -> 15 us  [move(): return lambda v: lax.ppermute(v, 'fsdp', pairs)]
  transfers between devices with their start and end apart: 11 -> 12, of which waited for: 5 -> 7; matrix products, arithmetic and copies ran while one was open for 0% -> 0% of each run, Pallas kernels for 4% -> 5%
where the time goes in v10:
time: 77.9 us; the launch traced here: 77.4 us
  starting transfers between devices  32.1 us (41%)
  blocking collectives  23.4 us (30%)
  waiting for transfers between devices  15 us (19%)
  Pallas kernels  5.32 us (7%)
  other arithmetic  1.28 us (2%)
    ppermute x12, starting transfers between devices, move(): return lambda v: lax.ppermute(v, 'fsdp', pairs)  32.1 us
    all_gather x5, blocking collectives, join(): lax.all_gather(v, 'fsdp', axis=0, tiled=True, axis_index_groups=core_pairs)  23.4 us
    ppermute x12, waiting for transfers between devices, move(): return lambda v: lax.ppermute(v, 'fsdp', pairs)  15 us
    pallas_call x5, Pallas kernels, call(): pl.pallas_call(functools.partial(kernel, functools.partial(add_blocks, sp...  4.85 us
  transfers between devices with their start and end apart: 12, of which 7 were waited for; matrix products, arithmetic and copies ran while one was open for 0% of the time, Pallas kernels for 5%

profile of v10, /device:TPU:1, one launch (start us, length us, event | category | flops | bytes accessed | tf_op | source)
XLA Modules:
  0.0 77.4 jit_solution(17254974971934474022)
XLA Ops:
  0.0 1.3 %multiply_convert_fusion.1 = (bf16[128,640]{1,0:T(8,128)(2,1)S(1)}, bf16[128,640]{1,0:T(8,128)(2,1)S(1)}) fusion(bf16[128,640]{1,0:T(8,128)(2,1)} %param.6, f32[128]{0:T(128)} %param.5, bf16[128,640]{1,0:T(8,128)(2,1)} %param.7), kind=kLoop, calls=%fused_computation.2 | loop fusion | flops 491520 | bytes 655872 | tf_op jit(solution)/shard_map/convert
  1.3 5.5 %collective-permute-start.1 = (bf16[128,1280]{1,0:T(8,128)(2,1)S(1)}, bf16[128,1280]{1,0:T(8,128)(2,1)S(1)}, u32[]{:S(2)}, u32[]{:S(2)}) collective-permute-start(bf16[128,1280]{1,0:T(8,128)(2,1)S(1)} %pad_maximum_fusion.refs_0_), channel_id=1, source_target_pairs={{0,48},{24,72},{48,0},{72,24},{96,144},{120,168},{144,96},{168,120... | collective-permute-start | bytes 983048 | tf_op jit(solution)/shard_map/ppermute | solution.py:128
  6.8 8.9 %all_gather.15 = bf16[256,1280]{1,0:T(8,128)(2,1)S(1)} all-gather(bf16[128,1280]{1,0:T(8,128)(2,1)S(1)} %pad_maximum_fusion.refs_0_), channel_id=1, replica_groups={{0,24},{48,72},{96,120},{144,168},{192,216},{240,264},{288,312},{336,36..., dimensions={0}, use_global_device_ids=true | all-gather | bytes 983040 | tf_op jit(solution)/shard_map/all_gather | solution.py:136
  15.6 2.3 %collective-permute-start = (bf16[192,4096]{1,0:T(8,128)(2,1)S(1)}, bf16[192,4096]{1,0:T(8,128)(2,1)S(1)}, u32[]{:S(2)}, u32[]{:S(2)}) collective-permute-start(bf16[192,4096]{1,0:T(8,128)(2,1)S(1)} %copy-done), channel_id=1, source_target_pairs={{0,24},{24,0},{48,72},{72,48},{96,120},{120,96},{144,168},{168,144... | collective-permute-start | bytes 4718600 | tf_op jit(solution)/shard_map/ppermute | solution.py:128
  17.9 1.9 %collective-permute-start.4 = (bf16[256,1280]{1,0:T(8,128)(2,1)S(1)}, bf16[256,1280]{1,0:T(8,128)(2,1)S(1)}, u32[]{:S(2)}, u32[]{:S(2)}) collective-permute-start(bf16[256,1280]{1,0:T(8,128)(2,1)S(1)} %all_gather.15), channel_id=1, source_target_pairs={{0,96},{24,696},{48,144},{72,744},{96,192},{120,24},{144,240},{168... | collective-permute-start | bytes 1966088 | tf_op jit(solution)/shard_map/ppermute | solution.py:128
  19.9 4.3 %all_gather.16 = bf16[256,1280]{1,0:T(8,128)(2,1)S(1)} all-gather(bf16[128,1280]{1,0:T(8,128)(2,1)S(1)} %collective-permute-done.1.refs_0_), channel_id=1, replica_groups={{0,24},{48,72},{96,120},{144,168},{192,216},{240,264},{288,312},{336,36..., dimensions={0}, use_global_device_ids=true | all-gather | bytes 983040 | tf_op jit(solution)/shard_map/all_gather | solution.py:136
  24.2 2.6 %collective-permute-start.2 = (bf16[256,1280]{1,0:T(8,128)(2,1)S(1)}, bf16[256,1280]{1,0:T(8,128)(2,1)S(1)}, u32[]{:S(2)}, u32[]{:S(2)}) collective-permute-start(bf16[256,1280]{1,0:T(8,128)(2,1)S(1)} %all_gather.16), channel_id=1, source_target_pairs={{0,96},{24,696},{48,144},{72,744},{96,192},{120,24},{144,240},{168... | collective-permute-start | bytes 1966088 | tf_op jit(solution)/shard_map/ppermute | solution.py:128
  26.8 2.8 %collective-permute-done.4.refs_1_ = bf16[256,1280]{1,0:T(8,128)(2,1)S(1)} collective-permute-done((bf16[256,1280]{1,0:T(8,128)(2,1)S(1)}, bf16[256,1280]{1,0:T(8,128)(2,1)S(1)}, u32[]{:S(2)}, u32[]{:S(2)}) %collective-permute-start.4) | collective-permute-done | bytes 655392 | tf_op jit(solution)/shard_map/ppermute | solution.py:128
  29.5 2.8 %collective-permute-start.5 = (bf16[256,1280]{1,0:T(8,128)(2,1)S(1)}, bf16[256,1280]{1,0:T(8,128)(2,1)S(1)}, u32[]{:S(2)}, u32[]{:S(2)}) collective-permute-start(bf16[256,1280]{1,0:T(8,128)(2,1)S(1)} %collective-permute-done.4.refs_1_), channel_id=1, source_target_pairs={{0,96},{24,696},{48,144},{72,744},{96,192},{120,24},{144,240},{168... | collective-permute-start | bytes 1966088 | tf_op jit(solution)/shard_map/ppermute | solution.py:128
  32.4 4.2 %collective-permute-done.2.refs_2_ = bf16[256,1280]{1,0:T(8,128)(2,1)S(1)} collective-permute-done((bf16[256,1280]{1,0:T(8,128)(2,1)S(1)}, bf16[256,1280]{1,0:T(8,128)(2,1)S(1)}, u32[]{:S(2)}, u32[]{:S(2)}) %collective-permute-start.2) | collective-permute-done | bytes 655392 | tf_op jit(solution)/shard_map/ppermute | solution.py:128
  36.6 2.8 %collective-permute-start.3 = (bf16[256,1280]{1,0:T(8,128)(2,1)S(1)}, bf16[256,1280]{1,0:T(8,128)(2,1)S(1)}, u32[]{:S(2)}, u32[]{:S(2)}) collective-permute-start(bf16[256,1280]{1,0:T(8,128)(2,1)S(1)} %collective-permute-done.2.refs_2_), channel_id=1, source_target_pairs={{0,96},{24,696},{48,144},{72,744},{96,192},{120,24},{144,240},{168... | collective-permute-start | bytes 1966088 | tf_op jit(solution)/shard_map/ppermute | solution.py:128
  39.4 4.2 %collective-permute-done.5.refs_3_.block = bf16[256,1280]{1,0:T(8,128)(2,1)S(1)} collective-permute-done((bf16[256,1280]{1,0:T(8,128)(2,1)S(1)}, bf16[256,1280]{1,0:T(8,128)(2,1)S(1)}, u32[]{:S(2)}, u32[]{:S(2)}) %collective-permute-start.5) | collective-permute-done | bytes 655392 | tf_op jit(solution)/shard_map/ppermute | solution.py:128
  43.7 2.8 %collective-permute-start.7 = (bf16[128,1280]{1,0:T(8,128)(2,1)S(1)}, bf16[128,1280]{1,0:T(8,128)(2,1)S(1)}, u32[]{:S(2)}, u32[]{:S(2)}) collective-permute-start(bf16[128,1280]{1,0:T(8,128)(2,1)S(1)} %shard_map.48), channel_id=1, source_target_pairs={{0,96},{24,696},{48,144},{72,744},{96,192},{120,24},{144,240},{168... | collective-permute-start | bytes 983048 | tf_op jit(solution)/shard_map/ppermute | solution.py:128
  46.7 1.9 %collective-permute-start.8 = (bf16[128,1280]{1,0:T(8,128)(2,1)S(1)}, bf16[128,1280]{1,0:T(8,128)(2,1)S(1)}, u32[]{:S(2)}, u32[]{:S(2)}) collective-permute-start(bf16[128,1280]{1,0:T(8,128)(2,1)S(1)} %shard_map.49), channel_id=1, source_target_pairs={{0,96},{24,696},{48,144},{72,744},{96,192},{120,24},{144,240},{168... | collective-permute-start | bytes 983048 | tf_op jit(solution)/shard_map/ppermute | solution.py:128
  48.6 1.4 %shard_map.46 = (f32[192,1280]{1,0:T(8,128)S(1)}, f32[192,1280]{1,0:T(8,128)S(1)}, f32[192,1]{1,0:T(8,128)S(1)}) custom-call(bf16[192,4096]{1,0:T(8,128)(2,1)S(1)} %copy-done, bf16[192,4096]{1,0:T(8,128)(2,1)S(1)} %collective-permute-done.others, bf16[128,1280]{1,0:T(8,128)(2,1)S(1)} %pad_maximum_fusion.refs_0_, ...), custom_call_target="tpu_custom_call" | custom-call | flops 880803840 | bytes 6225920 | tf_op jit(solution)/shard_map/pallas_call | solution.py:107
  50.7 2.8 %collective-permute-start.6 = (bf16[128,1280]{1,0:T(8,128)(2,1)S(1)}, bf16[128,1280]{1,0:T(8,128)(2,1)S(1)}, u32[]{:S(2)}, u32[]{:S(2)}) collective-permute-start(bf16[128,1280]{1,0:T(8,128)(2,1)S(1)} %shard_map.47), channel_id=1, source_target_pairs={{0,96},{24,696},{48,144},{72,744},{96,192},{120,24},{144,240},{168... | collective-permute-start | bytes 983048 | tf_op jit(solution)/shard_map/ppermute | solution.py:128
  53.7 1.9 %collective-permute-start.10 = (bf16[128,1280]{1,0:T(8,128)(2,1)S(1)}, bf16[128,1280]{1,0:T(8,128)(2,1)S(1)}, u32[]{:S(2)}, u32[]{:S(2)}) collective-permute-start(bf16[128,1280]{1,0:T(8,128)(2,1)S(1)} %shard_map.51), channel_id=1, source_target_pairs={{0,96},{24,696},{48,144},{72,744},{96,192},{120,24},{144,240},{168... | collective-permute-start | bytes 983048 | tf_op jit(solution)/shard_map/ppermute | solution.py:128
  55.7 1.9 %collective-permute-start.11 = (bf16[128,1280]{1,0:T(8,128)(2,1)S(1)}, bf16[128,1280]{1,0:T(8,128)(2,1)S(1)}, u32[]{:S(2)}, u32[]{:S(2)}) collective-permute-start(bf16[128,1280]{1,0:T(8,128)(2,1)S(1)} %collective-permute-done.7.refs_2_), channel_id=1, source_target_pairs={{0,96},{24,696},{48,144},{72,744},{96,192},{120,24},{144,240},{168... | collective-permute-start | bytes 983048 | tf_op jit(solution)/shard_map/ppermute | solution.py:128
  57.6 1.2 %shard_map.50 = (f32[192,1280]{1,0:T(8,128)S(1)}, f32[192,640]{1,0:T(8,128)S(1)}, f32[192,640]{1,0:T(8,128)S(1)}) custom-call(bf16[192,4096]{1,0:T(8,128)(2,1)S(1)} %copy-done, bf16[192,4096]{1,0:T(8,128)(2,1)S(1)} %collective-permute-done.others, f32[192,1280]{1,0:T(8,128)S(1)} %get-tuple-element.27.total_before, ...), custom_call_target="tpu_custom_call" | custom-call | flops 629145600 | bytes 5570560 | tf_op jit(solution)/shard_map/pallas_call | solution.py:107
  58.8 2.3 %collective-permute-done.6.refs_0_ = bf16[128,1280]{1,0:T(8,128)(2,1)S(1)} collective-permute-done((bf16[128,1280]{1,0:T(8,128)(2,1)S(1)}, bf16[128,1280]{1,0:T(8,128)(2,1)S(1)}, u32[]{:S(2)}, u32[]{:S(2)}) %collective-permute-start.6) | collective-permute-done | bytes 327712 | tf_op jit(solution)/shard_map/ppermute | solution.py:128
  61.1 2.8 %collective-permute-start.9 = (bf16[128,1280]{1,0:T(8,128)(2,1)S(1)}, bf16[128,1280]{1,0:T(8,128)(2,1)S(1)}, u32[]{:S(2)}, u32[]{:S(2)}) collective-permute-start(bf16[128,1280]{1,0:T(8,128)(2,1)S(1)} %collective-permute-done.6.refs_0_), channel_id=1, source_target_pairs={{0,96},{24,696},{48,144},{72,744},{96,192},{120,24},{144,240},{168... | collective-permute-start | bytes 983048 | tf_op jit(solution)/shard_map/ppermute | solution.py:128
  64.0 3.4 %all_gather.17.gate_arrived = f32[384,640]{1,0:T(8,128)S(1)} all-gather(f32[192,640]{1,0:T(8,128)S(1)} %get-tuple-element.32), channel_id=1, replica_groups={{0,24},{48,72},{96,120},{144,168},{192,216},{240,264},{288,312},{336,36..., dimensions={0}, use_global_device_ids=true | all-gather | bytes 1474560 | tf_op jit(solution)/shard_map/all_gather | solution.py:136
  67.4 2.5 %all_gather.18.up_arrived = f32[384,640]{1,0:T(8,128)S(1)} all-gather(f32[192,640]{1,0:T(8,128)S(1)} %get-tuple-element.33), channel_id=1, replica_groups={{0,24},{48,72},{96,120},{144,168},{192,216},{240,264},{288,312},{336,36..., dimensions={0}, use_global_device_ids=true | all-gather | bytes 1474560 | tf_op jit(solution)/shard_map/all_gather | solution.py:136
  72.1 4.3 %all_gather.19.late = bf16[384,1280]{1,0:T(8,128)(2,1)S(1)} all-gather(bf16[192,1280]{1,0:T(8,128)(2,1)S(1)} %get-tuple-element.39), channel_id=1, replica_groups={{0,24},{48,72},{96,120},{144,168},{192,216},{240,264},{288,312},{336,36..., dimensions={0}, use_global_device_ids=true | all-gather | bytes 1474560 | tf_op jit(solution)/shard_map/all_gather | solution.py:136
  (18 shorter events, 4.3 us)
Async XLA Ops:
  0.0 15.6 %copy-start = (bf16[192,4096]{1,0:T(8,128)(2,1)S(1)}, bf16[192,4096]{1,0:T(8,128)(2,1)}, u32[]{:S(2)}) copy-start(bf16[192,4096]{1,0:T(8,128)(2,1)} %tokens.7) | copy-start | bytes 4718596
  1.3 18.6 %collective-permute-start.1 = (bf16[128,1280]{1,0:T(8,128)(2,1)S(1)}, bf16[128,1280]{1,0:T(8,128)(2,1)S(1)}, u32[]{:S(2)}, u32[]{:S(2)}) collective-permute-start(bf16[128,1280]{1,0:T(8,128)(2,1)S(1)} %pad_maximum_fusion.refs_0_), channel_id=1, source_target_pairs={{0,48},{24,72},{48,0},{72,24},{96,144},{120,168},{144,96},{168,120... | collective-permute-start | bytes 983048 | tf_op jit(solution)/shard_map/ppermute | solution.py:128
  15.6 33.0 %collective-permute-start = (bf16[192,4096]{1,0:T(8,128)(2,1)S(1)}, bf16[192,4096]{1,0:T(8,128)(2,1)S(1)}, u32[]{:S(2)}, u32[]{:S(2)}) collective-permute-start(bf16[192,4096]{1,0:T(8,128)(2,1)S(1)} %copy-done), channel_id=1, source_target_pairs={{0,24},{24,0},{48,72},{72,48},{96,120},{120,96},{144,168},{168,144... | collective-permute-start | bytes 4718600 | tf_op jit(solution)/shard_map/ppermute | solution.py:128
  17.9 11.6 %collective-permute-start.4 = (bf16[256,1280]{1,0:T(8,128)(2,1)S(1)}, bf16[256,1280]{1,0:T(8,128)(2,1)S(1)}, u32[]{:S(2)}, u32[]{:S(2)}) collective-permute-start(bf16[256,1280]{1,0:T(8,128)(2,1)S(1)} %all_gather.15), channel_id=1, source_target_pairs={{0,96},{24,696},{48,144},{72,744},{96,192},{120,24},{144,240},{168... | collective-permute-start | bytes 1966088 | tf_op jit(solution)/shard_map/ppermute | solution.py:128
  24.2 12.4 %collective-permute-start.2 = (bf16[256,1280]{1,0:T(8,128)(2,1)S(1)}, bf16[256,1280]{1,0:T(8,128)(2,1)S(1)}, u32[]{:S(2)}, u32[]{:S(2)}) collective-permute-start(bf16[256,1280]{1,0:T(8,128)(2,1)S(1)} %all_gather.16), channel_id=1, source_target_pairs={{0,96},{24,696},{48,144},{72,744},{96,192},{120,24},{144,240},{168... | collective-permute-start | bytes 1966088 | tf_op jit(solution)/shard_map/ppermute | solution.py:128
  29.5 14.0 %collective-permute-start.5 = (bf16[256,1280]{1,0:T(8,128)(2,1)S(1)}, bf16[256,1280]{1,0:T(8,128)(2,1)S(1)}, u32[]{:S(2)}, u32[]{:S(2)}) collective-permute-start(bf16[256,1280]{1,0:T(8,128)(2,1)S(1)} %collective-permute-done.4.refs_1_), channel_id=1, source_target_pairs={{0,96},{24,696},{48,144},{72,744},{96,192},{120,24},{144,240},{168... | collective-permute-start | bytes 1966088 | tf_op jit(solution)/shard_map/ppermute | solution.py:128
  36.6 14.0 %collective-permute-start.3 = (bf16[256,1280]{1,0:T(8,128)(2,1)S(1)}, bf16[256,1280]{1,0:T(8,128)(2,1)S(1)}, u32[]{:S(2)}, u32[]{:S(2)}) collective-permute-start(bf16[256,1280]{1,0:T(8,128)(2,1)S(1)} %collective-permute-done.2.refs_2_), channel_id=1, source_target_pairs={{0,96},{24,696},{48,144},{72,744},{96,192},{120,24},{144,240},{168... | collective-permute-start | bytes 1966088 | tf_op jit(solution)/shard_map/ppermute | solution.py:128
  43.7 11.9 %collective-permute-start.7 = (bf16[128,1280]{1,0:T(8,128)(2,1)S(1)}, bf16[128,1280]{1,0:T(8,128)(2,1)S(1)}, u32[]{:S(2)}, u32[]{:S(2)}) collective-permute-start(bf16[128,1280]{1,0:T(8,128)(2,1)S(1)} %shard_map.48), channel_id=1, source_target_pairs={{0,96},{24,696},{48,144},{72,744},{96,192},{120,24},{144,240},{168... | collective-permute-start | bytes 983048 | tf_op jit(solution)/shard_map/ppermute | solution.py:128
  46.7 10.9 %collective-permute-start.8 = (bf16[128,1280]{1,0:T(8,128)(2,1)S(1)}, bf16[128,1280]{1,0:T(8,128)(2,1)S(1)}, u32[]{:S(2)}, u32[]{:S(2)}) collective-permute-start(bf16[128,1280]{1,0:T(8,128)(2,1)S(1)} %shard_map.49), channel_id=1, source_target_pairs={{0,96},{24,696},{48,144},{72,744},{96,192},{120,24},{144,240},{168... | collective-permute-start | bytes 983048 | tf_op jit(solution)/shard_map/ppermute | solution.py:128
  50.7 10.4 %collective-permute-start.6 = (bf16[128,1280]{1,0:T(8,128)(2,1)S(1)}, bf16[128,1280]{1,0:T(8,128)(2,1)S(1)}, u32[]{:S(2)}, u32[]{:S(2)}) collective-permute-start(bf16[128,1280]{1,0:T(8,128)(2,1)S(1)} %shard_map.47), channel_id=1, source_target_pairs={{0,96},{24,696},{48,144},{72,744},{96,192},{120,24},{144,240},{168... | collective-permute-start | bytes 983048 | tf_op jit(solution)/shard_map/ppermute | solution.py:128
  53.7 16.2 %collective-permute-start.10 = (bf16[128,1280]{1,0:T(8,128)(2,1)S(1)}, bf16[128,1280]{1,0:T(8,128)(2,1)S(1)}, u32[]{:S(2)}, u32[]{:S(2)}) collective-permute-start(bf16[128,1280]{1,0:T(8,128)(2,1)S(1)} %shard_map.51), channel_id=1, source_target_pairs={{0,96},{24,696},{48,144},{72,744},{96,192},{120,24},{144,240},{168... | collective-permute-start | bytes 983048 | tf_op jit(solution)/shard_map/ppermute | solution.py:128
  55.7 14.3 %collective-permute-start.11 = (bf16[128,1280]{1,0:T(8,128)(2,1)S(1)}, bf16[128,1280]{1,0:T(8,128)(2,1)S(1)}, u32[]{:S(2)}, u32[]{:S(2)}) collective-permute-start(bf16[128,1280]{1,0:T(8,128)(2,1)S(1)} %collective-permute-done.7.refs_2_), channel_id=1, source_target_pairs={{0,96},{24,696},{48,144},{72,744},{96,192},{120,24},{144,240},{168... | collective-permute-start | bytes 983048 | tf_op jit(solution)/shard_map/ppermute | solution.py:128
  61.1 10.5 %collective-permute-start.9 = (bf16[128,1280]{1,0:T(8,128)(2,1)S(1)}, bf16[128,1280]{1,0:T(8,128)(2,1)S(1)}, u32[]{:S(2)}, u32[]{:S(2)}) collective-permute-start(bf16[128,1280]{1,0:T(8,128)(2,1)S(1)} %collective-permute-done.6.refs_0_), channel_id=1, source_target_pairs={{0,96},{24,696},{48,144},{72,744},{96,192},{120,24},{144,240},{168... | collective-permute-start | bytes 983048 | tf_op jit(solution)/shard_map/ppermute | solution.py:128

commit v11 on v10

--- a/solution.py
+++ b/solution.py
@@ -53,28 +53,23 @@
 
 
 def third_kernel(add, n, tokens, others, total_before, gate_arrived, up_arrived, *refs):
-    blocks, (total, partial) = refs[:n], refs[n:]
+    blocks, (total, leaving, partial) = refs[:n], refs[n:]
     wide = gate_arrived.shape[1]
     theirs = their_rows(total.shape[0])
     total[:, :wide] = total_before[:, :wide] + gate_arrived[theirs, :]
     total[:, wide:] = total_before[:, wide:] + up_arrived[theirs, :]
     partial[...] = jnp.zeros_like(partial)
     add(blocks, [(tokens, total), (others, partial)])
-
-
-def fourth_kernel(add, n, tokens, others, total_before, partial_before, *refs):
-    blocks, (total, leaving, partial) = refs[:n], refs[n:]
-    total[...] = total_before[...]
-    partial[...] = partial_before[...]
-    add(blocks, [(tokens, total), (others, partial)])
     leaving[...] = partial[...].astype(leaving.dtype)
 
 
-def last_kernel(add, n, total, late, scale, hidden):
+def last_kernel(add, n, tokens, total_before, late, scale, *refs):
+    blocks, (hidden, total) = refs[:n], refs[n:]
     rows, wide = hidden.shape
-    theirs = their_rows(rows)
-    gate = (total[:, :wide] + late[theirs, :wide].astype(jnp.float32)) * scale[...]
-    up = (total[:, wide:] + late[theirs, wide:].astype(jnp.float32)) * scale[...]
+    total[...] = total_before[...] + late[their_rows(rows), :].astype(jnp.float32)
+    add(blocks, [(tokens, total)])
+    gate = total[:, :wide] * scale[...]
+    up = total[:, wide:] * scale[...]
     hidden[...] = (gate / (1.0 + jnp.exp(-gate)) * up).astype(hidden.dtype)
 
 
@@ -174,28 +169,22 @@
         )
         b3, total = lax.optimization_barrier((b3, total))
         b4 = along(b3)
-        total, partial = step(
+        total, late = step(
             third_kernel,
             specs=[(3, 1, 1), (3, 1, 2), (4, 0, 1)],
             arrays=[tokens, others, total, join(gate), join(up)],
             blocks=[b3, b3_rest, a4],
-            out_shape=(sums, sums),
-        )
-        b4, total = lax.optimization_barrier((b4, total))
-        total, late = step(
-            fourth_kernel,
-            specs=[(4, 1, 1)],
-            arrays=[tokens, others, total, partial],
-            blocks=[b4],
             out_shape=(sums, jax.ShapeDtypeStruct((rows, wide), jnp.bfloat16)),
             scratch=[pltpu.VMEM((rows, wide), jnp.float32)],
         )
+        late_joined = join(late)
         return step(
             last_kernel,
-            specs=[],
-            arrays=[total, join(late), scale],
-            blocks=[],
+            specs=[(4, 1, 0)],
+            arrays=[tokens, total, late_joined, scale],
+            blocks=[join(b4)],
             out_shape=jax.ShapeDtypeStruct((rows, wide // 2), jnp.bfloat16),
+            scratch=[pltpu.VMEM((rows, wide), jnp.float32)],
         )
 
     return on_device

time: 77.9 us -> 78.2 us (level); the launches traced: 77.4 us -> 76.9 us
  waiting for transfers between devices: 15 us -> 11.8 us
  blocking collectives: 23.4 us -> 25.3 us
  starting transfers between devices: 32.1 us -> 33.2 us
    ppermute x12, waiting for transfers between devices: 15 us -> 11.8 us  [move(): return lambda v: lax.ppermute(v, 'fsdp', pairs)]
    all_gather x5 -> x6, blocking collectives: 23.4 us -> 25.3 us  [join(): lax.all_gather(v, 'fsdp', axis=0, tiled=True, axis_index_groups=core_pairs)]
    ppermute x12, starting transfers between devices: 32.1 us -> 33.2 us  [move(): return lambda v: lax.ppermute(v, 'fsdp', pairs)]
    pallas_call x5 -> x4, Pallas kernels: 4.85 us -> 4.59 us  [call(): pl.pallas_call(functools.partial(kernel, functools.partial(add_blocks, sp...]
  transfers between devices with their start and end apart: 12 -> 12, of which waited for: 7 -> 5; matrix products, arithmetic and copies ran while one was open for 0% -> 0% of each run, Pallas kernels for 5% -> 5%
where the time goes in v11:
time: 78.2 us; the launch traced here: 76.9 us
  starting transfers between devices  33.2 us (42%)
  blocking collectives  25.3 us (32%)
  waiting for transfers between devices  11.8 us (15%)
  Pallas kernels  5.07 us (6%)
  other arithmetic  1.28 us (2%)
    ppermute x12, starting transfers between devices, move(): return lambda v: lax.ppermute(v, 'fsdp', pairs)  33.2 us
    all_gather x6, blocking collectives, join(): lax.all_gather(v, 'fsdp', axis=0, tiled=True, axis_index_groups=core_pairs)  25.3 us
    ppermute x12, waiting for transfers between devices, move(): return lambda v: lax.ppermute(v, 'fsdp', pairs)  11.8 us
    pallas_call x4, Pallas kernels, call(): pl.pallas_call(functools.partial(kernel, functools.partial(add_blocks, sp...  4.59 us
  transfers between devices with their start and end apart: 12, of which 5 were waited for; matrix products, arithmetic and copies ran while one was open for 0% of the time, Pallas kernels for 5%

profile of v11, /device:TPU:1, one launch (start us, length us, event | category | flops | bytes accessed | tf_op | source)
XLA Modules:
  0.0 76.9 jit_solution(14540811264161526763)
XLA Ops:
  0.0 1.3 %multiply_convert_fusion.1 = (bf16[128,640]{1,0:T(8,128)(2,1)S(1)}, bf16[128,640]{1,0:T(8,128)(2,1)S(1)}) fusion(bf16[128,640]{1,0:T(8,128)(2,1)} %param.6, f32[128]{0:T(128)} %param.5, bf16[128,640]{1,0:T(8,128)(2,1)} %param.7), kind=kLoop, calls=%fused_computation.2 | loop fusion | flops 491520 | bytes 655872 | tf_op jit(solution)/shard_map/convert
  1.3 5.5 %collective-permute-start.1 = (bf16[128,1280]{1,0:T(8,128)(2,1)S(1)}, bf16[128,1280]{1,0:T(8,128)(2,1)S(1)}, u32[]{:S(2)}, u32[]{:S(2)}) collective-permute-start(bf16[128,1280]{1,0:T(8,128)(2,1)S(1)} %pad_maximum_fusion.refs_0_), channel_id=1, source_target_pairs={{0,48},{24,72},{48,0},{72,24},{96,144},{120,168},{144,96},{168,120... | collective-permute-start | bytes 983048 | tf_op jit(solution)/shard_map/ppermute | solution.py:123
  6.8 8.9 %all_gather.18 = bf16[256,1280]{1,0:T(8,128)(2,1)S(1)} all-gather(bf16[128,1280]{1,0:T(8,128)(2,1)S(1)} %pad_maximum_fusion.refs_0_), channel_id=1, replica_groups={{0,24},{48,72},{96,120},{144,168},{192,216},{240,264},{288,312},{336,36..., dimensions={0}, use_global_device_ids=true | all-gather | bytes 983040 | tf_op jit(solution)/shard_map/all_gather | solution.py:131
  15.6 2.3 %collective-permute-start = (bf16[192,4096]{1,0:T(8,128)(2,1)S(1)}, bf16[192,4096]{1,0:T(8,128)(2,1)S(1)}, u32[]{:S(2)}, u32[]{:S(2)}) collective-permute-start(bf16[192,4096]{1,0:T(8,128)(2,1)S(1)} %copy-done), channel_id=1, source_target_pairs={{0,24},{24,0},{48,72},{72,48},{96,120},{120,96},{144,168},{168,144... | collective-permute-start | bytes 4718600 | tf_op jit(solution)/shard_map/ppermute | solution.py:123
  17.9 1.9 %collective-permute-start.4 = (bf16[256,1280]{1,0:T(8,128)(2,1)S(1)}, bf16[256,1280]{1,0:T(8,128)(2,1)S(1)}, u32[]{:S(2)}, u32[]{:S(2)}) collective-permute-start(bf16[256,1280]{1,0:T(8,128)(2,1)S(1)} %all_gather.18), channel_id=1, source_target_pairs={{0,96},{24,696},{48,144},{72,744},{96,192},{120,24},{144,240},{168... | collective-permute-start | bytes 1966088 | tf_op jit(solution)/shard_map/ppermute | solution.py:123
  19.9 4.3 %all_gather.19 = bf16[256,1280]{1,0:T(8,128)(2,1)S(1)} all-gather(bf16[128,1280]{1,0:T(8,128)(2,1)S(1)} %collective-permute-done.1.refs_0_), channel_id=1, replica_groups={{0,24},{48,72},{96,120},{144,168},{192,216},{240,264},{288,312},{336,36..., dimensions={0}, use_global_device_ids=true | all-gather | bytes 983040 | tf_op jit(solution)/shard_map/all_gather | solution.py:131
  24.2 2.6 %collective-permute-start.2 = (bf16[256,1280]{1,0:T(8,128)(2,1)S(1)}, bf16[256,1280]{1,0:T(8,128)(2,1)S(1)}, u32[]{:S(2)}, u32[]{:S(2)}) collective-permute-start(bf16[256,1280]{1,0:T(8,128)(2,1)S(1)} %all_gather.19), channel_id=1, source_target_pairs={{0,96},{24,696},{48,144},{72,744},{96,192},{120,24},{144,240},{168... | collective-permute-start | bytes 1966088 | tf_op jit(solution)/shard_map/ppermute | solution.py:123
  26.8 2.8 %collective-permute-done.4.refs_1_ = bf16[256,1280]{1,0:T(8,128)(2,1)S(1)} collective-permute-done((bf16[256,1280]{1,0:T(8,128)(2,1)S(1)}, bf16[256,1280]{1,0:T(8,128)(2,1)S(1)}, u32[]{:S(2)}, u32[]{:S(2)}) %collective-permute-start.4) | collective-permute-done | bytes 655392 | tf_op jit(solution)/shard_map/ppermute | solution.py:123
  29.5 2.8 %collective-permute-start.5 = (bf16[256,1280]{1,0:T(8,128)(2,1)S(1)}, bf16[256,1280]{1,0:T(8,128)(2,1)S(1)}, u32[]{:S(2)}, u32[]{:S(2)}) collective-permute-start(bf16[256,1280]{1,0:T(8,128)(2,1)S(1)} %collective-permute-done.4.refs_1_), channel_id=1, source_target_pairs={{0,96},{24,696},{48,144},{72,744},{96,192},{120,24},{144,240},{168... | collective-permute-start | bytes 1966088 | tf_op jit(solution)/shard_map/ppermute | solution.py:123
  32.4 4.2 %collective-permute-done.2.refs_2_ = bf16[256,1280]{1,0:T(8,128)(2,1)S(1)} collective-permute-done((bf16[256,1280]{1,0:T(8,128)(2,1)S(1)}, bf16[256,1280]{1,0:T(8,128)(2,1)S(1)}, u32[]{:S(2)}, u32[]{:S(2)}) %collective-permute-start.2) | collective-permute-done | bytes 655392 | tf_op jit(solution)/shard_map/ppermute | solution.py:123
  36.6 2.8 %collective-permute-start.3 = (bf16[256,1280]{1,0:T(8,128)(2,1)S(1)}, bf16[256,1280]{1,0:T(8,128)(2,1)S(1)}, u32[]{:S(2)}, u32[]{:S(2)}) collective-permute-start(bf16[256,1280]{1,0:T(8,128)(2,1)S(1)} %collective-permute-done.2.refs_2_), channel_id=1, source_target_pairs={{0,96},{24,696},{48,144},{72,744},{96,192},{120,24},{144,240},{168... | collective-permute-start | bytes 1966088 | tf_op jit(solution)/shard_map/ppermute | solution.py:123
  39.4 4.2 %collective-permute-done.5.refs_3_.block = bf16[256,1280]{1,0:T(8,128)(2,1)S(1)} collective-permute-done((bf16[256,1280]{1,0:T(8,128)(2,1)S(1)}, bf16[256,1280]{1,0:T(8,128)(2,1)S(1)}, u32[]{:S(2)}, u32[]{:S(2)}) %collective-permute-start.5) | collective-permute-done | bytes 655392 | tf_op jit(solution)/shard_map/ppermute | solution.py:123
  43.7 2.8 %collective-permute-start.7 = (bf16[128,1280]{1,0:T(8,128)(2,1)S(1)}, bf16[128,1280]{1,0:T(8,128)(2,1)S(1)}, u32[]{:S(2)}, u32[]{:S(2)}) collective-permute-start(bf16[128,1280]{1,0:T(8,128)(2,1)S(1)} %shard_map.48), channel_id=1, source_target_pairs={{0,96},{24,696},{48,144},{72,744},{96,192},{120,24},{144,240},{168... | collective-permute-start | bytes 983048 | tf_op jit(solution)/shard_map/ppermute | solution.py:123
  46.7 1.9 %collective-permute-start.8 = (bf16[128,1280]{1,0:T(8,128)(2,1)S(1)}, bf16[128,1280]{1,0:T(8,128)(2,1)S(1)}, u32[]{:S(2)}, u32[]{:S(2)}) collective-permute-start(bf16[128,1280]{1,0:T(8,128)(2,1)S(1)} %shard_map.49), channel_id=1, source_target_pairs={{0,96},{24,696},{48,144},{72,744},{96,192},{120,24},{144,240},{168... | collective-permute-start | bytes 983048 | tf_op jit(solution)/shard_map/ppermute | solution.py:123
  48.6 1.4 %shard_map.46 = (f32[192,1280]{1,0:T(8,128)S(1)}, f32[192,1280]{1,0:T(8,128)S(1)}, f32[192,1]{1,0:T(8,128)S(1)}) custom-call(bf16[192,4096]{1,0:T(8,128)(2,1)S(1)} %copy-done, bf16[192,4096]{1,0:T(8,128)(2,1)S(1)} %collective-permute-done.others, bf16[128,1280]{1,0:T(8,128)(2,1)S(1)} %pad_maximum_fusion.refs_0_, ...), custom_call_target="tpu_custom_call" | custom-call | flops 880803840 | bytes 6225920 | tf_op jit(solution)/shard_map/pallas_call | solution.py:102
  50.7 2.8 %collective-permute-start.6 = (bf16[128,1280]{1,0:T(8,128)(2,1)S(1)}, bf16[128,1280]{1,0:T(8,128)(2,1)S(1)}, u32[]{:S(2)}, u32[]{:S(2)}) collective-permute-start(bf16[128,1280]{1,0:T(8,128)(2,1)S(1)} %shard_map.47), channel_id=1, source_target_pairs={{0,96},{24,696},{48,144},{72,744},{96,192},{120,24},{144,240},{168... | collective-permute-start | bytes 983048 | tf_op jit(solution)/shard_map/ppermute | solution.py:123
  53.7 1.9 %collective-permute-start.9 = (bf16[128,1280]{1,0:T(8,128)(2,1)S(1)}, bf16[128,1280]{1,0:T(8,128)(2,1)S(1)}, u32[]{:S(2)}, u32[]{:S(2)}) collective-permute-start(bf16[128,1280]{1,0:T(8,128)(2,1)S(1)} %shard_map.51), channel_id=1, source_target_pairs={{0,96},{24,696},{48,144},{72,744},{96,192},{120,24},{144,240},{168... | collective-permute-start | bytes 983048 | tf_op jit(solution)/shard_map/ppermute | solution.py:123
  55.7 1.9 %collective-permute-start.10 = (bf16[128,1280]{1,0:T(8,128)(2,1)S(1)}, bf16[128,1280]{1,0:T(8,128)(2,1)S(1)}, u32[]{:S(2)}, u32[]{:S(2)}) collective-permute-start(bf16[128,1280]{1,0:T(8,128)(2,1)S(1)} %collective-permute-done.7.refs_2_), channel_id=1, source_target_pairs={{0,96},{24,696},{48,144},{72,744},{96,192},{120,24},{144,240},{168... | collective-permute-start | bytes 983048 | tf_op jit(solution)/shard_map/ppermute | solution.py:123
  57.6 1.2 %shard_map.50 = (f32[192,1280]{1,0:T(8,128)S(1)}, f32[192,640]{1,0:T(8,128)S(1)}, f32[192,640]{1,0:T(8,128)S(1)}) custom-call(bf16[192,4096]{1,0:T(8,128)(2,1)S(1)} %copy-done, bf16[192,4096]{1,0:T(8,128)(2,1)S(1)} %collective-permute-done.others, f32[192,1280]{1,0:T(8,128)S(1)} %get-tuple-element.23.total_before, ...), custom_call_target="tpu_custom_call" | custom-call | flops 629145600 | bytes 5570560 | tf_op jit(solution)/shard_map/pallas_call | solution.py:102
  58.8 4.3 %all_gather.20.gate_arrived = f32[384,640]{1,0:T(8,128)S(1)} all-gather(f32[192,640]{1,0:T(8,128)S(1)} %get-tuple-element.27), channel_id=1, replica_groups={{0,24},{48,72},{96,120},{144,168},{192,216},{240,264},{288,312},{336,36..., dimensions={0}, use_global_device_ids=true | all-gather | bytes 1474560 | tf_op jit(solution)/shard_map/all_gather | solution.py:131
  63.2 3.9 %collective-permute-start.11 = (bf16[128,1280]{1,0:T(8,128)(2,1)S(1)}, bf16[128,1280]{1,0:T(8,128)(2,1)S(1)}, u32[]{:S(2)}, u32[]{:S(2)}) collective-permute-start(bf16[128,1280]{1,0:T(8,128)(2,1)S(1)} %collective-permute-done.6.refs_0_), channel_id=1, source_target_pairs={{0,96},{24,696},{48,144},{72,744},{96,192},{120,24},{144,240},{168... | collective-permute-start | bytes 983048 | tf_op jit(solution)/shard_map/ppermute | solution.py:123
  67.1 2.5 %all_gather.21.up_arrived = f32[384,640]{1,0:T(8,128)S(1)} all-gather(f32[192,640]{1,0:T(8,128)S(1)} %get-tuple-element.28), channel_id=1, replica_groups={{0,24},{48,72},{96,120},{144,168},{192,216},{240,264},{288,312},{336,36..., dimensions={0}, use_global_device_ids=true | all-gather | bytes 1474560 | tf_op jit(solution)/shard_map/all_gather | solution.py:131
  70.5 2.9 %all_gather.22.late = bf16[384,1280]{1,0:T(8,128)(2,1)S(1)} all-gather(bf16[192,1280]{1,0:T(8,128)(2,1)S(1)} %get-tuple-element.31), channel_id=1, replica_groups={{0,24},{48,72},{96,120},{144,168},{192,216},{240,264},{288,312},{336,36..., dimensions={0}, use_global_device_ids=true | all-gather | bytes 1474560 | tf_op jit(solution)/shard_map/all_gather | solution.py:131
  73.4 2.3 %all_gather.23.refs_0_ = bf16[256,1280]{1,0:T(8,128)(2,1)S(1)} all-gather(bf16[128,1280]{1,0:T(8,128)(2,1)S(1)} %collective-permute-done.11), channel_id=1, replica_groups={{0,24},{48,72},{96,120},{144,168},{192,216},{240,264},{288,312},{336,36..., dimensions={0}, use_global_device_ids=true | all-gather | bytes 983040 | tf_op jit(solution)/shard_map/all_gather | solution.py:131
  (18 shorter events, 3.2 us)
Async XLA Ops:
  0.0 15.6 %copy-start = (bf16[192,4096]{1,0:T(8,128)(2,1)S(1)}, bf16[192,4096]{1,0:T(8,128)(2,1)}, u32[]{:S(2)}) copy-start(bf16[192,4096]{1,0:T(8,128)(2,1)} %tokens.7) | copy-start | bytes 4718596
  1.3 18.6 %collective-permute-start.1 = (bf16[128,1280]{1,0:T(8,128)(2,1)S(1)}, bf16[128,1280]{1,0:T(8,128)(2,1)S(1)}, u32[]{:S(2)}, u32[]{:S(2)}) collective-permute-start(bf16[128,1280]{1,0:T(8,128)(2,1)S(1)} %pad_maximum_fusion.refs_0_), channel_id=1, source_target_pairs={{0,48},{24,72},{48,0},{72,24},{96,144},{120,168},{144,96},{168,120... | collective-permute-start | bytes 983048 | tf_op jit(solution)/shard_map/ppermute | solution.py:123
  15.6 33.0 %collective-permute-start = (bf16[192,4096]{1,0:T(8,128)(2,1)S(1)}, bf16[192,4096]{1,0:T(8,128)(2,1)S(1)}, u32[]{:S(2)}, u32[]{:S(2)}) collective-permute-start(bf16[192,4096]{1,0:T(8,128)(2,1)S(1)} %copy-done), channel_id=1, source_target_pairs={{0,24},{24,0},{48,72},{72,48},{96,120},{120,96},{144,168},{168,144... | collective-permute-start | bytes 4718600 | tf_op jit(solution)/shard_map/ppermute | solution.py:123
  17.9 11.6 %collective-permute-start.4 = (bf16[256,1280]{1,0:T(8,128)(2,1)S(1)}, bf16[256,1280]{1,0:T(8,128)(2,1)S(1)}, u32[]{:S(2)}, u32[]{:S(2)}) collective-permute-start(bf16[256,1280]{1,0:T(8,128)(2,1)S(1)} %all_gather.18), channel_id=1, source_target_pairs={{0,96},{24,696},{48,144},{72,744},{96,192},{120,24},{144,240},{168... | collective-permute-start | bytes 1966088 | tf_op jit(solution)/shard_map/ppermute | solution.py:123
  24.2 12.4 %collective-permute-start.2 = (bf16[256,1280]{1,0:T(8,128)(2,1)S(1)}, bf16[256,1280]{1,0:T(8,128)(2,1)S(1)}, u32[]{:S(2)}, u32[]{:S(2)}) collective-permute-start(bf16[256,1280]{1,0:T(8,128)(2,1)S(1)} %all_gather.19), channel_id=1, source_target_pairs={{0,96},{24,696},{48,144},{72,744},{96,192},{120,24},{144,240},{168... | collective-permute-start | bytes 1966088 | tf_op jit(solution)/shard_map/ppermute | solution.py:123
  29.5 14.0 %collective-permute-start.5 = (bf16[256,1280]{1,0:T(8,128)(2,1)S(1)}, bf16[256,1280]{1,0:T(8,128)(2,1)S(1)}, u32[]{:S(2)}, u32[]{:S(2)}) collective-permute-start(bf16[256,1280]{1,0:T(8,128)(2,1)S(1)} %collective-permute-done.4.refs_1_), channel_id=1, source_target_pairs={{0,96},{24,696},{48,144},{72,744},{96,192},{120,24},{144,240},{168... | collective-permute-start | bytes 1966088 | tf_op jit(solution)/shard_map/ppermute | solution.py:123
  36.6 14.0 %collective-permute-start.3 = (bf16[256,1280]{1,0:T(8,128)(2,1)S(1)}, bf16[256,1280]{1,0:T(8,128)(2,1)S(1)}, u32[]{:S(2)}, u32[]{:S(2)}) collective-permute-start(bf16[256,1280]{1,0:T(8,128)(2,1)S(1)} %collective-permute-done.2.refs_2_), channel_id=1, source_target_pairs={{0,96},{24,696},{48,144},{72,744},{96,192},{120,24},{144,240},{168... | collective-permute-start | bytes 1966088 | tf_op jit(solution)/shard_map/ppermute | solution.py:123
  43.7 11.9 %collective-permute-start.7 = (bf16[128,1280]{1,0:T(8,128)(2,1)S(1)}, bf16[128,1280]{1,0:T(8,128)(2,1)S(1)}, u32[]{:S(2)}, u32[]{:S(2)}) collective-permute-start(bf16[128,1280]{1,0:T(8,128)(2,1)S(1)} %shard_map.48), channel_id=1, source_target_pairs={{0,96},{24,696},{48,144},{72,744},{96,192},{120,24},{144,240},{168... | collective-permute-start | bytes 983048 | tf_op jit(solution)/shard_map/ppermute | solution.py:123
  46.7 10.9 %collective-permute-start.8 = (bf16[128,1280]{1,0:T(8,128)(2,1)S(1)}, bf16[128,1280]{1,0:T(8,128)(2,1)S(1)}, u32[]{:S(2)}, u32[]{:S(2)}) collective-permute-start(bf16[128,1280]{1,0:T(8,128)(2,1)S(1)} %shard_map.49), channel_id=1, source_target_pairs={{0,96},{24,696},{48,144},{72,744},{96,192},{120,24},{144,240},{168... | collective-permute-start | bytes 983048 | tf_op jit(solution)/shard_map/ppermute | solution.py:123
  50.7 12.4 %collective-permute-start.6 = (bf16[128,1280]{1,0:T(8,128)(2,1)S(1)}, bf16[128,1280]{1,0:T(8,128)(2,1)S(1)}, u32[]{:S(2)}, u32[]{:S(2)}) collective-permute-start(bf16[128,1280]{1,0:T(8,128)(2,1)S(1)} %shard_map.47), channel_id=1, source_target_pairs={{0,96},{24,696},{48,144},{72,744},{96,192},{120,24},{144,240},{168... | collective-permute-start | bytes 983048 | tf_op jit(solution)/shard_map/ppermute | solution.py:123
  53.7 15.9 %collective-permute-start.9 = (bf16[128,1280]{1,0:T(8,128)(2,1)S(1)}, bf16[128,1280]{1,0:T(8,128)(2,1)S(1)}, u32[]{:S(2)}, u32[]{:S(2)}) collective-permute-start(bf16[128,1280]{1,0:T(8,128)(2,1)S(1)} %shard_map.51), channel_id=1, source_target_pairs={{0,96},{24,696},{48,144},{72,744},{96,192},{120,24},{144,240},{168... | collective-permute-start | bytes 983048 | tf_op jit(solution)/shard_map/ppermute | solution.py:123
  55.7 13.9 %collective-permute-start.10 = (bf16[128,1280]{1,0:T(8,128)(2,1)S(1)}, bf16[128,1280]{1,0:T(8,128)(2,1)S(1)}, u32[]{:S(2)}, u32[]{:S(2)}) collective-permute-start(bf16[128,1280]{1,0:T(8,128)(2,1)S(1)} %collective-permute-done.7.refs_2_), channel_id=1, source_target_pairs={{0,96},{24,696},{48,144},{72,744},{96,192},{120,24},{144,240},{168... | collective-permute-start | bytes 983048 | tf_op jit(solution)/shard_map/ppermute | solution.py:123
  63.2 10.3 %collective-permute-start.11 = (bf16[128,1280]{1,0:T(8,128)(2,1)S(1)}, bf16[128,1280]{1,0:T(8,128)(2,1)S(1)}, u32[]{:S(2)}, u32[]{:S(2)}) collective-permute-start(bf16[128,1280]{1,0:T(8,128)(2,1)S(1)} %collective-permute-done.6.refs_0_), channel_id=1, source_target_pairs={{0,96},{24,696},{48,144},{72,744},{96,192},{120,24},{144,240},{168... | collective-permute-start | bytes 983048 | tf_op jit(solution)/shard_map/ppermute | solution.py:123

commit v12 on v10

--- a/solution.py
+++ b/solution.py
@@ -76,6 +76,15 @@
     gate = (total[:, :wide] + late[theirs, :wide].astype(jnp.float32)) * scale[...]
     up = (total[:, wide:] + late[theirs, wide:].astype(jnp.float32)) * scale[...]
     hidden[...] = (gate / (1.0 + jnp.exp(-gate)) * up).astype(hidden.dtype)
+
+
+def gain_kernel(gain, gate, up, own):
+    depth, wide = gate.shape
+    shape = (depth, depth)
+    here = lax.broadcasted_iota(jnp.int32, shape, 0) == lax.broadcasted_iota(jnp.int32, shape, 1)
+    column = jnp.sum(jnp.where(here, gain[...], 0.0), axis=1, keepdims=True)
+    own[:, :wide] = (gate[...].astype(jnp.float32) * column).astype(own.dtype)
+    own[:, wide:] = (up[...].astype(jnp.float32) * column).astype(own.dtype)
 
 
 def cut_kernel(flip, depth, block, out, sem):
@@ -136,8 +145,14 @@
         return lax.all_gather(v, "fsdp", axis=0, tiled=True, axis_index_groups=core_pairs)
 
     def on_device(tokens, norm_gain, gate_weight, up_weight):
-        gain = norm_gain[:, None]
-        own = jnp.concatenate([gate_weight * gain, up_weight * gain], axis=1).astype(jnp.bfloat16)
+        vmem = pl.BlockSpec(memory_space=pltpu.VMEM)
+        own = pl.pallas_call(
+            gain_kernel,
+            out_shape=jax.ShapeDtypeStruct((gate_weight.shape[0], 2 * gate_weight.shape[1]), jnp.bfloat16),
+            in_specs=[vmem] * 3,
+            out_specs=vmem,
+            compiler_params=pltpu.CompilerParams(vmem_limit_bytes=vmem_bytes // 4),
+        )(norm_gain[None, :], gate_weight, up_weight)
         wide = own.shape[1]
         b0 = across(own)
         chip, late = lax.optimization_barrier((join(own), tokens))

time: 77.9 us -> 79.4 us (1.019)
  local copies, waits for them, and re-layouts: 0.01 us -> 2.61 us
  other arithmetic: 1.28 us -> 0 us
    unnamed x2 -> x8, local copies, waits for them, and re-layouts: 0.01 us -> 2.61 us
    another operation x1 -> x0, other arithmetic: 1.25 us -> none
where the time goes in v12:
time: 79.4 us; the launch traced here: 78.8 us
  starting transfers between devices  32.1 us (40%)
  blocking collectives  23.4 us (29%)
  waiting for transfers between devices  15 us (19%)
  Pallas kernels  5.45 us (7%)
  local copies, waits for them, and re-layouts  2.61 us (3%)
    ppermute x12, starting transfers between devices, move(): return lambda v: lax.ppermute(v, 'fsdp', pairs)  32.1 us
    all_gather x5, blocking collectives, join(): lax.all_gather(v, 'fsdp', axis=0, tiled=True, axis_index_groups=core_pairs)  23.4 us
    ppermute x12, waiting for transfers between devices, move(): return lambda v: lax.ppermute(v, 'fsdp', pairs)  15 us
    pallas_call x5, Pallas kernels, call(): pl.pallas_call(functools.partial(kernel, functools.partial(add_blocks, sp...  4.84 us
    unnamed x8, local copies, waits for them, and re-layouts  2.61 us
  transfers between devices with their start and end apart: 12, of which 7 were waited for; matrix products, arithmetic and copies ran while one was open for 0% of the time, Pallas kernels for 5%

profile of v12, /device:TPU:1, one launch (start us, length us, event | category | flops | bytes accessed | tf_op | source)
XLA Modules:
  0.0 78.8 jit_solution(8349223419081082249)
XLA Ops:
  0.0 1.0 %copy-done.1 = bf16[128,640]{1,0:T(8,128)(2,1)S(1)} copy-done((bf16[128,640]{1,0:T(8,128)(2,1)S(1)}, bf16[128,640]{1,0:T(8,128)(2,1)}, u32[]{:S(2)}) %copy-start.1) | copy-done | bytes 163864
  2.7 5.5 %collective-permute-start.1 = (bf16[128,1280]{1,0:T(8,128)(2,1)S(1)}, bf16[128,1280]{1,0:T(8,128)(2,1)S(1)}, u32[]{:S(2)}, u32[]{:S(2)}) collective-permute-start(bf16[128,1280]{1,0:T(8,128)(2,1)S(1)} %shard_map.46.refs_0_), channel_id=1, source_target_pairs={{0,48},{24,72},{48,0},{72,24},{96,144},{120,168},{144,96},{168,120... | collective-permute-start | bytes 983048 | tf_op jit(solution)/shard_map/ppermute | solution.py:137
  8.2 8.9 %all_gather.15 = bf16[256,1280]{1,0:T(8,128)(2,1)S(1)} all-gather(bf16[128,1280]{1,0:T(8,128)(2,1)S(1)} %shard_map.46.refs_0_), channel_id=1, replica_groups={{0,24},{48,72},{96,120},{144,168},{192,216},{240,264},{288,312},{336,36..., dimensions={0}, use_global_device_ids=true | all-gather | bytes 983040 | tf_op jit(solution)/shard_map/all_gather | solution.py:145
  17.1 2.3 %collective-permute-start = (bf16[192,4096]{1,0:T(8,128)(2,1)S(1)}, bf16[192,4096]{1,0:T(8,128)(2,1)S(1)}, u32[]{:S(2)}, u32[]{:S(2)}) collective-permute-start(bf16[192,4096]{1,0:T(8,128)(2,1)S(1)} %copy-done), channel_id=1, source_target_pairs={{0,24},{24,0},{48,72},{72,48},{96,120},{120,96},{144,168},{168,144... | collective-permute-start | bytes 4718600 | tf_op jit(solution)/shard_map/ppermute | solution.py:137
  19.4 1.9 %collective-permute-start.4 = (bf16[256,1280]{1,0:T(8,128)(2,1)S(1)}, bf16[256,1280]{1,0:T(8,128)(2,1)S(1)}, u32[]{:S(2)}, u32[]{:S(2)}) collective-permute-start(bf16[256,1280]{1,0:T(8,128)(2,1)S(1)} %all_gather.15), channel_id=1, source_target_pairs={{0,96},{24,696},{48,144},{72,744},{96,192},{120,24},{144,240},{168... | collective-permute-start | bytes 1966088 | tf_op jit(solution)/shard_map/ppermute | solution.py:137
  21.3 4.3 %all_gather.16 = bf16[256,1280]{1,0:T(8,128)(2,1)S(1)} all-gather(bf16[128,1280]{1,0:T(8,128)(2,1)S(1)} %collective-permute-done.1.refs_0_), channel_id=1, replica_groups={{0,24},{48,72},{96,120},{144,168},{192,216},{240,264},{288,312},{336,36..., dimensions={0}, use_global_device_ids=true | all-gather | bytes 983040 | tf_op jit(solution)/shard_map/all_gather | solution.py:145
  25.6 2.6 %collective-permute-start.2 = (bf16[256,1280]{1,0:T(8,128)(2,1)S(1)}, bf16[256,1280]{1,0:T(8,128)(2,1)S(1)}, u32[]{:S(2)}, u32[]{:S(2)}) collective-permute-start(bf16[256,1280]{1,0:T(8,128)(2,1)S(1)} %all_gather.16), channel_id=1, source_target_pairs={{0,96},{24,696},{48,144},{72,744},{96,192},{120,24},{144,240},{168... | collective-permute-start | bytes 1966088 | tf_op jit(solution)/shard_map/ppermute | solution.py:137
  28.2 2.8 %collective-permute-done.4.refs_1_ = bf16[256,1280]{1,0:T(8,128)(2,1)S(1)} collective-permute-done((bf16[256,1280]{1,0:T(8,128)(2,1)S(1)}, bf16[256,1280]{1,0:T(8,128)(2,1)S(1)}, u32[]{:S(2)}, u32[]{:S(2)}) %collective-permute-start.4) | collective-permute-done | bytes 655392 | tf_op jit(solution)/shard_map/ppermute | solution.py:137
  31.0 2.8 %collective-permute-start.5 = (bf16[256,1280]{1,0:T(8,128)(2,1)S(1)}, bf16[256,1280]{1,0:T(8,128)(2,1)S(1)}, u32[]{:S(2)}, u32[]{:S(2)}) collective-permute-start(bf16[256,1280]{1,0:T(8,128)(2,1)S(1)} %collective-permute-done.4.refs_1_), channel_id=1, source_target_pairs={{0,96},{24,696},{48,144},{72,744},{96,192},{120,24},{144,240},{168... | collective-permute-start | bytes 1966088 | tf_op jit(solution)/shard_map/ppermute | solution.py:137
  33.8 4.2 %collective-permute-done.2.refs_2_ = bf16[256,1280]{1,0:T(8,128)(2,1)S(1)} collective-permute-done((bf16[256,1280]{1,0:T(8,128)(2,1)S(1)}, bf16[256,1280]{1,0:T(8,128)(2,1)S(1)}, u32[]{:S(2)}, u32[]{:S(2)}) %collective-permute-start.2) | collective-permute-done | bytes 655392 | tf_op jit(solution)/shard_map/ppermute | solution.py:137
  38.0 2.8 %collective-permute-start.3 = (bf16[256,1280]{1,0:T(8,128)(2,1)S(1)}, bf16[256,1280]{1,0:T(8,128)(2,1)S(1)}, u32[]{:S(2)}, u32[]{:S(2)}) collective-permute-start(bf16[256,1280]{1,0:T(8,128)(2,1)S(1)} %collective-permute-done.2.refs_2_), channel_id=1, source_target_pairs={{0,96},{24,696},{48,144},{72,744},{96,192},{120,24},{144,240},{168... | collective-permute-start | bytes 1966088 | tf_op jit(solution)/shard_map/ppermute | solution.py:137
  40.9 4.2 %collective-permute-done.5.refs_3_.block = bf16[256,1280]{1,0:T(8,128)(2,1)S(1)} collective-permute-done((bf16[256,1280]{1,0:T(8,128)(2,1)S(1)}, bf16[256,1280]{1,0:T(8,128)(2,1)S(1)}, u32[]{:S(2)}, u32[]{:S(2)}) %collective-permute-start.5) | collective-permute-done | bytes 655392 | tf_op jit(solution)/shard_map/ppermute | solution.py:137
  45.2 2.8 %collective-permute-start.7 = (bf16[128,1280]{1,0:T(8,128)(2,1)S(1)}, bf16[128,1280]{1,0:T(8,128)(2,1)S(1)}, u32[]{:S(2)}, u32[]{:S(2)}) collective-permute-start(bf16[128,1280]{1,0:T(8,128)(2,1)S(1)} %shard_map.49), channel_id=1, source_target_pairs={{0,96},{24,696},{48,144},{72,744},{96,192},{120,24},{144,240},{168... | collective-permute-start | bytes 983048 | tf_op jit(solution)/shard_map/ppermute | solution.py:137
  48.1 1.9 %collective-permute-start.8 = (bf16[128,1280]{1,0:T(8,128)(2,1)S(1)}, bf16[128,1280]{1,0:T(8,128)(2,1)S(1)}, u32[]{:S(2)}, u32[]{:S(2)}) collective-permute-start(bf16[128,1280]{1,0:T(8,128)(2,1)S(1)} %shard_map.50), channel_id=1, source_target_pairs={{0,96},{24,696},{48,144},{72,744},{96,192},{120,24},{144,240},{168... | collective-permute-start | bytes 983048 | tf_op jit(solution)/shard_map/ppermute | solution.py:137
  50.1 1.4 %shard_map.47 = (f32[192,1280]{1,0:T(8,128)S(1)}, f32[192,1280]{1,0:T(8,128)S(1)}, f32[192,1]{1,0:T(8,128)S(1)}) custom-call(bf16[192,4096]{1,0:T(8,128)(2,1)S(1)} %copy-done, bf16[192,4096]{1,0:T(8,128)(2,1)S(1)} %collective-permute-done.others, bf16[128,1280]{1,0:T(8,128)(2,1)S(1)} %shard_map.46.refs_0_, ...), custom_call_target="tpu_custom_call" | custom-call | flops 880803840 | bytes 6225920 | tf_op jit(solution)/shard_map/pallas_call | solution.py:116
  52.2 2.8 %collective-permute-start.6 = (bf16[128,1280]{1,0:T(8,128)(2,1)S(1)}, bf16[128,1280]{1,0:T(8,128)(2,1)S(1)}, u32[]{:S(2)}, u32[]{:S(2)}) collective-permute-start(bf16[128,1280]{1,0:T(8,128)(2,1)S(1)} %shard_map.48), channel_id=1, source_target_pairs={{0,96},{24,696},{48,144},{72,744},{96,192},{120,24},{144,240},{168... | collective-permute-start | bytes 983048 | tf_op jit(solution)/shard_map/ppermute | solution.py:137
  55.2 1.9 %collective-permute-start.10 = (bf16[128,1280]{1,0:T(8,128)(2,1)S(1)}, bf16[128,1280]{1,0:T(8,128)(2,1)S(1)}, u32[]{:S(2)}, u32[]{:S(2)}) collective-permute-start(bf16[128,1280]{1,0:T(8,128)(2,1)S(1)} %shard_map.52), channel_id=1, source_target_pairs={{0,96},{24,696},{48,144},{72,744},{96,192},{120,24},{144,240},{168... | collective-permute-start | bytes 983048 | tf_op jit(solution)/shard_map/ppermute | solution.py:137
  57.1 1.9 %collective-permute-start.11 = (bf16[128,1280]{1,0:T(8,128)(2,1)S(1)}, bf16[128,1280]{1,0:T(8,128)(2,1)S(1)}, u32[]{:S(2)}, u32[]{:S(2)}) collective-permute-start(bf16[128,1280]{1,0:T(8,128)(2,1)S(1)} %collective-permute-done.7.refs_2_), channel_id=1, source_target_pairs={{0,96},{24,696},{48,144},{72,744},{96,192},{120,24},{144,240},{168... | collective-permute-start | bytes 983048 | tf_op jit(solution)/shard_map/ppermute | solution.py:137
  59.1 1.2 %shard_map.51 = (f32[192,1280]{1,0:T(8,128)S(1)}, f32[192,640]{1,0:T(8,128)S(1)}, f32[192,640]{1,0:T(8,128)S(1)}) custom-call(bf16[192,4096]{1,0:T(8,128)(2,1)S(1)} %copy-done, bf16[192,4096]{1,0:T(8,128)(2,1)S(1)} %collective-permute-done.others, f32[192,1280]{1,0:T(8,128)S(1)} %get-tuple-element.27.total_before, ...), custom_call_target="tpu_custom_call" | custom-call | flops 629145600 | bytes 5570560 | tf_op jit(solution)/shard_map/pallas_call | solution.py:116
  60.3 2.3 %collective-permute-done.6.refs_0_ = bf16[128,1280]{1,0:T(8,128)(2,1)S(1)} collective-permute-done((bf16[128,1280]{1,0:T(8,128)(2,1)S(1)}, bf16[128,1280]{1,0:T(8,128)(2,1)S(1)}, u32[]{:S(2)}, u32[]{:S(2)}) %collective-permute-start.6) | collective-permute-done | bytes 327712 | tf_op jit(solution)/shard_map/ppermute | solution.py:137
  62.6 2.8 %collective-permute-start.9 = (bf16[128,1280]{1,0:T(8,128)(2,1)S(1)}, bf16[128,1280]{1,0:T(8,128)(2,1)S(1)}, u32[]{:S(2)}, u32[]{:S(2)}) collective-permute-start(bf16[128,1280]{1,0:T(8,128)(2,1)S(1)} %collective-permute-done.6.refs_0_), channel_id=1, source_target_pairs={{0,96},{24,696},{48,144},{72,744},{96,192},{120,24},{144,240},{168... | collective-permute-start | bytes 983048 | tf_op jit(solution)/shard_map/ppermute | solution.py:137
  65.4 3.4 %all_gather.17.gate_arrived = f32[384,640]{1,0:T(8,128)S(1)} all-gather(f32[192,640]{1,0:T(8,128)S(1)} %get-tuple-element.32), channel_id=1, replica_groups={{0,24},{48,72},{96,120},{144,168},{192,216},{240,264},{288,312},{336,36..., dimensions={0}, use_global_device_ids=true | all-gather | bytes 1474560 | tf_op jit(solution)/shard_map/all_gather | solution.py:145
  68.9 2.5 %all_gather.18.up_arrived = f32[384,640]{1,0:T(8,128)S(1)} all-gather(f32[192,640]{1,0:T(8,128)S(1)} %get-tuple-element.33), channel_id=1, replica_groups={{0,24},{48,72},{96,120},{144,168},{192,216},{240,264},{288,312},{336,36..., dimensions={0}, use_global_device_ids=true | all-gather | bytes 1474560 | tf_op jit(solution)/shard_map/all_gather | solution.py:145
  73.5 4.3 %all_gather.19.late = bf16[384,1280]{1,0:T(8,128)(2,1)S(1)} all-gather(bf16[192,1280]{1,0:T(8,128)(2,1)S(1)} %get-tuple-element.39), channel_id=1, replica_groups={{0,24},{48,72},{96,120},{144,168},{192,216},{240,264},{288,312},{336,36..., dimensions={0}, use_global_device_ids=true | all-gather | bytes 1474560 | tf_op jit(solution)/shard_map/all_gather | solution.py:145
  (23 shorter events, 6.0 us)
Async XLA Ops:
  0.0 17.1 %copy-start = (bf16[192,4096]{1,0:T(8,128)(2,1)S(1)}, bf16[192,4096]{1,0:T(8,128)(2,1)}, u32[]{:S(2)}) copy-start(bf16[192,4096]{1,0:T(8,128)(2,1)} %tokens.7) | copy-start | bytes 4718596
  0.0 1.0 %copy-start.1 = (bf16[128,640]{1,0:T(8,128)(2,1)S(1)}, bf16[128,640]{1,0:T(8,128)(2,1)}, u32[]{:S(2)}) copy-start(bf16[128,640]{1,0:T(8,128)(2,1)} %gate.1) | copy-start | bytes 491524
  1.0 0.9 %copy-start.2 = (bf16[128,640]{1,0:T(8,128)(2,1)S(1)}, bf16[128,640]{1,0:T(8,128)(2,1)}, u32[]{:S(2)}) copy-start(bf16[128,640]{1,0:T(8,128)(2,1)} %up.1) | copy-start | bytes 491524
  2.0 0.7 copy-start.3
  2.7 18.6 %collective-permute-start.1 = (bf16[128,1280]{1,0:T(8,128)(2,1)S(1)}, bf16[128,1280]{1,0:T(8,128)(2,1)S(1)}, u32[]{:S(2)}, u32[]{:S(2)}) collective-permute-start(bf16[128,1280]{1,0:T(8,128)(2,1)S(1)} %shard_map.46.refs_0_), channel_id=1, source_target_pairs={{0,48},{24,72},{48,0},{72,24},{96,144},{120,168},{144,96},{168,120... | collective-permute-start | bytes 983048 | tf_op jit(solution)/shard_map/ppermute | solution.py:137
  17.1 33.0 %collective-permute-start = (bf16[192,4096]{1,0:T(8,128)(2,1)S(1)}, bf16[192,4096]{1,0:T(8,128)(2,1)S(1)}, u32[]{:S(2)}, u32[]{:S(2)}) collective-permute-start(bf16[192,4096]{1,0:T(8,128)(2,1)S(1)} %copy-done), channel_id=1, source_target_pairs={{0,24},{24,0},{48,72},{72,48},{96,120},{120,96},{144,168},{168,144... | collective-permute-start | bytes 4718600 | tf_op jit(solution)/shard_map/ppermute | solution.py:137
  19.4 11.6 %collective-permute-start.4 = (bf16[256,1280]{1,0:T(8,128)(2,1)S(1)}, bf16[256,1280]{1,0:T(8,128)(2,1)S(1)}, u32[]{:S(2)}, u32[]{:S(2)}) collective-permute-start(bf16[256,1280]{1,0:T(8,128)(2,1)S(1)} %all_gather.15), channel_id=1, source_target_pairs={{0,96},{24,696},{48,144},{72,744},{96,192},{120,24},{144,240},{168... | collective-permute-start | bytes 1966088 | tf_op jit(solution)/shard_map/ppermute | solution.py:137
  25.6 12.4 %collective-permute-start.2 = (bf16[256,1280]{1,0:T(8,128)(2,1)S(1)}, bf16[256,1280]{1,0:T(8,128)(2,1)S(1)}, u32[]{:S(2)}, u32[]{:S(2)}) collective-permute-start(bf16[256,1280]{1,0:T(8,128)(2,1)S(1)} %all_gather.16), channel_id=1, source_target_pairs={{0,96},{24,696},{48,144},{72,744},{96,192},{120,24},{144,240},{168... | collective-permute-start | bytes 1966088 | tf_op jit(solution)/shard_map/ppermute | solution.py:137
  31.0 14.0 %collective-permute-start.5 = (bf16[256,1280]{1,0:T(8,128)(2,1)S(1)}, bf16[256,1280]{1,0:T(8,128)(2,1)S(1)}, u32[]{:S(2)}, u32[]{:S(2)}) collective-permute-start(bf16[256,1280]{1,0:T(8,128)(2,1)S(1)} %collective-permute-done.4.refs_1_), channel_id=1, source_target_pairs={{0,96},{24,696},{48,144},{72,744},{96,192},{120,24},{144,240},{168... | collective-permute-start | bytes 1966088 | tf_op jit(solution)/shard_map/ppermute | solution.py:137
  38.0 14.0 %collective-permute-start.3 = (bf16[256,1280]{1,0:T(8,128)(2,1)S(1)}, bf16[256,1280]{1,0:T(8,128)(2,1)S(1)}, u32[]{:S(2)}, u32[]{:S(2)}) collective-permute-start(bf16[256,1280]{1,0:T(8,128)(2,1)S(1)} %collective-permute-done.2.refs_2_), channel_id=1, source_target_pairs={{0,96},{24,696},{48,144},{72,744},{96,192},{120,24},{144,240},{168... | collective-permute-start | bytes 1966088 | tf_op jit(solution)/shard_map/ppermute | solution.py:137
  45.2 11.9 %collective-permute-start.7 = (bf16[128,1280]{1,0:T(8,128)(2,1)S(1)}, bf16[128,1280]{1,0:T(8,128)(2,1)S(1)}, u32[]{:S(2)}, u32[]{:S(2)}) collective-permute-start(bf16[128,1280]{1,0:T(8,128)(2,1)S(1)} %shard_map.49), channel_id=1, source_target_pairs={{0,96},{24,696},{48,144},{72,744},{96,192},{120,24},{144,240},{168... | collective-permute-start | bytes 983048 | tf_op jit(solution)/shard_map/ppermute | solution.py:137
  48.1 10.9 %collective-permute-start.8 = (bf16[128,1280]{1,0:T(8,128)(2,1)S(1)}, bf16[128,1280]{1,0:T(8,128)(2,1)S(1)}, u32[]{:S(2)}, u32[]{:S(2)}) collective-permute-start(bf16[128,1280]{1,0:T(8,128)(2,1)S(1)} %shard_map.50), channel_id=1, source_target_pairs={{0,96},{24,696},{48,144},{72,744},{96,192},{120,24},{144,240},{168... | collective-permute-start | bytes 983048 | tf_op jit(solution)/shard_map/ppermute | solution.py:137
  52.2 10.4 %collective-permute-start.6 = (bf16[128,1280]{1,0:T(8,128)(2,1)S(1)}, bf16[128,1280]{1,0:T(8,128)(2,1)S(1)}, u32[]{:S(2)}, u32[]{:S(2)}) collective-permute-start(bf16[128,1280]{1,0:T(8,128)(2,1)S(1)} %shard_map.48), channel_id=1, source_target_pairs={{0,96},{24,696},{48,144},{72,744},{96,192},{120,24},{144,240},{168... | collective-permute-start | bytes 983048 | tf_op jit(solution)/shard_map/ppermute | solution.py:137
  55.2 16.2 %collective-permute-start.10 = (bf16[128,1280]{1,0:T(8,128)(2,1)S(1)}, bf16[128,1280]{1,0:T(8,128)(2,1)S(1)}, u32[]{:S(2)}, u32[]{:S(2)}) collective-permute-start(bf16[128,1280]{1,0:T(8,128)(2,1)S(1)} %shard_map.52), channel_id=1, source_target_pairs={{0,96},{24,696},{48,144},{72,744},{96,192},{120,24},{144,240},{168... | collective-permute-start | bytes 983048 | tf_op jit(solution)/shard_map/ppermute | solution.py:137
  57.1 14.3 %collective-permute-start.11 = (bf16[128,1280]{1,0:T(8,128)(2,1)S(1)}, bf16[128,1280]{1,0:T(8,128)(2,1)S(1)}, u32[]{:S(2)}, u32[]{:S(2)}) collective-permute-start(bf16[128,1280]{1,0:T(8,128)(2,1)S(1)} %collective-permute-done.7.refs_2_), channel_id=1, source_target_pairs={{0,96},{24,696},{48,144},{72,744},{96,192},{120,24},{144,240},{168... | collective-permute-start | bytes 983048 | tf_op jit(solution)/shard_map/ppermute | solution.py:137
  62.6 10.5 %collective-permute-start.9 = (bf16[128,1280]{1,0:T(8,128)(2,1)S(1)}, bf16[128,1280]{1,0:T(8,128)(2,1)S(1)}, u32[]{:S(2)}, u32[]{:S(2)}) collective-permute-start(bf16[128,1280]{1,0:T(8,128)(2,1)S(1)} %collective-permute-done.6.refs_0_), channel_id=1, source_target_pairs={{0,96},{24,696},{48,144},{72,744},{96,192},{120,24},{144,240},{168... | collective-permute-start | bytes 983048 | tf_op jit(solution)/shard_map/ppermute | solution.py:137
